TPU v7x, 32 devices: a whole 2x2x4 slice. The times are simulated.
32 devices in a mesh: section: 4 (over x, core), span: 8 (over z, y).
Axes of the slice: x: 2, y: 2, z: 4, core: 2. Of those that a mesh axis runs over, the one named last changes fastest.
Arguments:
- inverse_blocks: bfloat16 [16, 768, 768], P('section'), may hold values from -1.2 to 1.2
- coupling: float32 [16, 768], P('section'), may hold values from 0.05 to 0.3
- sources: bfloat16 [4, 768, 3072], P('section', None, 'span'), may hold values from -36 to 36
Outputs:
- basis: bfloat16 [4, 768, 3072], P('section', None, 'span')
- upper: float32 [4, 48, 48], P('section')
All inputs are finite; a program needn't handle non-finite values.
Results may differ from a plain program's by a relative error of at most 0.03.
Values may be sent and summed in bfloat16 or wider, within the bound.
No kernel may reach another device: no remote copies, remote signals or barrier semaphores. Data moves between devices by JAX's collectives and lax.ppermute only.
A program may use at most 64 MiB of HBM per device.

v0:
```python
import functools

import jax
import jax.numpy as jnp
import numpy as np
from jax import lax
from jax.experimental import pallas as pl
from jax.experimental.pallas import tpu as pltpu
from jax.sharding import PartitionSpec as P

K = 48
STATIONS = 4
FN = 768
HALF = K // 2
POINTS = 8
ONE = POINTS * HALF
EDGE = STATIONS * HALF
WIDE = 2 * EDGE
STEP = 6
GRANT = 48 * 1024 * 1024
SMALL = 16 * 1024 * 1024
AXES = ("section", "span")


def one_hot_order():
    at = lax.broadcasted_iota(jnp.int32, (1, POINTS * K), 1)
    point = at * 1366 >> 16
    column = at - point * K
    half = (column >= HALF).astype(jnp.int32)
    target = half * (ONE - HALF) + point * HALF + column
    row = lax.broadcasted_iota(jnp.int32, (POINTS * K, POINTS * K), 0)
    return jnp.where(row == target, 1.0, 0.0).astype(jnp.bfloat16)


def ordered(raw):
    return lax.dot_general(one_hot_order(), raw, (((1,), (1,)), ((), ())), preferred_element_type=jnp.float32)


def march_kernel(number, places, others, plan, blocks, positions, grow, raw, turn, coupling, weights, *refs):
    refs = list(refs)
    pieces = [refs.pop(0) for _ in places]
    raws = [refs.pop(0) for _ in range(raw)]
    givers = [refs.pop(0) for _ in others[0]]
    outs, (first, second, held, result, sems) = refs[:-5], refs[-5:]
    if not others[2]:
        result = outs[0]
    else:
        outs = [None] + outs
    states = [first, second]
    order = list(reversed(range(STATIONS)))
    side = turn[1]

    @pl.when(turn[0] == number)
    def _():
        copies = [
            pltpu.make_async_copy(weights.at[station], held.at[step], sems.at[step])
            for step, station in enumerate(order)
        ]
        copies[0].start()
        margin = 2 * HALF if grow else 0
        if margin:
            empty = jnp.zeros((blocks, margin, FN), jnp.float32)
            first[:, :margin, :] = empty
            first[:, margin + positions * HALF : 2 * margin + positions * HALF, :] = empty

        def total(on):
            covers = []
            if raw:
                turned = ordered(raws[0][...])
                for half in range(2):
                    covers.append((half, 0, ONE, lambda low, high, at=half * ONE: turned[at + low : at + high]))
            for piece, (where, rows, pick) in zip(pieces, places):
                block, start = where(on)
                if pick is not None:
                    covers.append((block, start, rows, lambda low, high, p=piece, k=pick(on): p[k, low:high, :]))
                elif len(piece.shape) == 3:
                    for k in range(blocks):
                        covers.append((k, start, rows, lambda low, high, p=piece, k=k: p[k, low:high, :]))
                else:
                    covers.append((block, start, rows, lambda low, high, p=piece: p[low:high, :]))
            for block in range(blocks):
                here = [cover for cover in covers if cover[0] == block]
                bounds = {0, positions * HALF}
                for _, start, rows, _ in here:
                    bounds |= {start, start + rows}
                bounds = sorted(bounds)
                for low, high in zip(bounds, bounds[1:]):
                    value = jnp.zeros((high - low, FN), jnp.float32)
                    for _, start, rows, read in here:
                        if start <= low and high <= start + rows:
                            value = value + read(low - start, high - start).astype(jnp.float32)
                    first[block, margin + low : margin + high, :] = value

        if pieces:
            for on in range(2):
                pl.when(side == on)(functools.partial(total, on))
        else:
            total(0)

        def stencil(step, chunk):
            block, begin, end = chunk
            at, rows = begin * HALF, (end - begin) * HALF
            source = states[step % 2]
            rates = coupling[order[step] : order[step] + 1, :]
            both = source[block, at : at + rows, :] + source[block, at + 2 * HALF : at + 2 * HALF + rows, :]
            update = (1.0 - 2.0 * rates) * source[block, at + HALF : at + HALF + rows, :] + rates * both
            return update.astype(jnp.bfloat16)

        copies[1].start()
        jobs = [(step, chunk) for step in range(STATIONS) for chunk in plan[step]]
        update = stencil(*jobs[0])
        for at_job, (step, chunk) in enumerate(jobs):
            block, begin, end = chunk
            at, rows = begin * HALF, (end - begin) * HALF
            current = update
            if at_job + 1 < len(jobs):
                update = stencil(*jobs[at_job + 1])
            if chunk is plan[step][0]:
                copies[step].wait()
                if step + 2 < STATIONS:
                    copies[step + 2].start()
            moved = lax.dot_general(
                current, held[step], (((1,), (1,)), ((), ())), preferred_element_type=jnp.float32
            )
            if step == STATIONS - 1:
                result[block, at : at + rows, :] = moved.astype(jnp.bfloat16)
                continue
            target = states[1 - step % 2]
            target[block, margin + at : margin + at + rows, :] = moved
            if grow:
                empty = jnp.zeros((margin, FN), jnp.float32)
                count = max(last for place, _, last in plan[step] if place == block)
                if begin == 0:
                    target[block, :margin, :] = empty
                if end == count:
                    target[block, margin + count * HALF : 2 * margin + count * HALF, :] = empty
        for out, where in zip(outs[1:], others[2]):
            start = pl.multiple_of(where(side), EDGE)
            out[...] = result[0, pl.ds(start, out.shape[0]), :]

    relay(others[1], turn, givers, outs[1:], sems)


def relay(owners, turn, givers, outs, sems):
    side = turn[1]
    for slot, value, moves in owners:

        @pl.when(turn[slot] == value)
        def _():
            copies = []
            for at, (giver, block, start, rows, out, to) in enumerate(moves):
                start = start(side)
                if not isinstance(start, int):
                    start = pl.multiple_of(start, EDGE)
                source = givers[giver].at[block(side), pl.ds(start, rows)]
                copies.append(pltpu.make_async_copy(source, outs[out].at[pl.ds(to, rows)], sems.at[at]))
            for copy in copies:
                copy.start()
            for copy in copies:
                copy.wait()


def march(turn, number, inverse_blocks, coupling, pieces, cut, blocks, positions, grow, raw=(), others=((), (), ())):
    last = positions + (2 * STATIONS if grow else -2 * STATIONS)
    most = last + 2 if grow else positions
    counts = [positions + (2 if grow else -2) * (step + 1) for step in range(STATIONS)]
    if blocks == 2:
        plan = [[(0, 0, count), (1, 0, count)] for count in counts]
    else:
        cuts = [cut - (0 if grow else 2 * step) for step in range(STATIONS)]
        plan = [[(0, 0, at), (0, at, count)] for at, count in zip(cuts, counts)]
    vmem = pl.BlockSpec(memory_space=pltpu.VMEM)
    away = pl.BlockSpec(memory_space=pl.ANY)
    whole = (blocks, last * HALF, FN)
    shapes = [jax.ShapeDtypeStruct(whole, jnp.bfloat16)]
    if others[2]:
        shapes = [jax.ShapeDtypeStruct((size, FN), jnp.bfloat16) for size in (2 * ONE, WIDE, WIDE, 2 * ONE)]
    values = [piece[0] for piece in pieces]
    return pl.pallas_call(
        functools.partial(
            march_kernel,
            number,
            [piece[1:] for piece in pieces],
            others,
            plan,
            blocks,
            positions,
            grow,
            len(raw),
        ),
        out_shape=shapes,
        in_specs=[pl.BlockSpec(memory_space=pltpu.SMEM), vmem, away]
        + [vmem] * (len(values) + len(raw))
        + [away] * len(others[0]),
        out_specs=[vmem] * len(shapes),
        scratch_shapes=[pltpu.VMEM((blocks, most * HALF, FN), jnp.float32)] * 2
        + [
            pltpu.VMEM((STATIONS, FN, FN), jnp.bfloat16),
            pltpu.VMEM(whole if others[2] else (1, 16, FN), jnp.bfloat16),
            pltpu.SemaphoreType.DMA((STATIONS,)),
        ],
        compiler_params=pltpu.CompilerParams(vmem_limit_bytes=GRANT),
        cost_estimate=pl.CostEstimate(
            flops=2 * blocks * HALF * sum(counts) * FN * FN,
            bytes_accessed=2 * STATIONS * FN * FN,
            transcendentals=0,
        ),
    )(turn, coupling, inverse_blocks, *values, *raw, *others[0])


def ship_kernel(
    number, turn, share, below, raw, crossed, edge_cross, edge_same, direct, whole, turned
):
    side, kind = turn[1], turn[2]

    def turn_over(source):
        rows = ordered(source[...])
        for half in range(2):
            turned[half, :, :] = rows[half * ONE : (half + 1) * ONE]

    @pl.when(turn[0] == number)
    def _():
        turn_over(below)
        whole[...] = share[...]
        middle = share[:, EDGE : EDGE + ONE, :].astype(jnp.float32) + turned[...]
        whole[:, EDGE : EDGE + ONE, :] = middle.astype(jnp.bfloat16)
        start = pl.multiple_of(side * ONE, ONE)
        edge_cross[...] = whole[1 - side, pl.ds(start, WIDE), :]
        edge_same[...] = whole[side, pl.ds(start, WIDE), :]
        crossed[...] = whole[1 - side]
        direct[...] = whole[side]

    @pl.when(kind >= 2)
    def _():
        turn_over(raw)
        whole[:, :ONE, :] = turned[...].astype(jnp.bfloat16)

    @pl.when(kind == 2)
    def _():
        crossed[:ONE, :] = whole[1 - side, :ONE, :]

    @pl.when(kind == 3)
    def _():
        for half in range(2):
            edge_cross[half * EDGE : (half + 1) * EDGE, :] = whole[half, ONE - EDGE : ONE, :]
            edge_same[half * EDGE : (half + 1) * EDGE, :] = whole[half, :EDGE, :]


def center_kernel(number, turn, direct, crossed, edge_same, edge_cross, out):
    @pl.when(turn[0] == number)
    def _():
        side = turn[1]
        start = pl.multiple_of(side * EDGE, EDGE)
        from_edge = pl.multiple_of((1 - side) * EDGE, EDGE)
        for block, share, edge in ((side, direct, edge_same), (1 - side, crossed, edge_cross)):
            out[block, :, :] = share[EDGE : EDGE + ONE, :]
            here = out[block, pl.ds(start, EDGE), :].astype(jnp.float32)
            more = edge[pl.ds(from_edge, EDGE), :].astype(jnp.float32)
            out[block, pl.ds(start, EDGE), :] = (here + more).astype(jnp.bfloat16)


def gram_kernel(numbers, turn, *refs):
    inputs, (rows, gram, edges, sems) = refs[: 7 * len(numbers)], refs[7 * len(numbers) :]
    side = turn[1]

    def fetch(*pairs):
        copies = [pltpu.make_async_copy(source, target, sems.at[at]) for at, (source, target) in enumerate(pairs)]
        for copy in copies:
            copy.start()
        for copy in copies:
            copy.wait()

    for at, number in enumerate(numbers):
        share, low, high, state, crossed, back, last = inputs[7 * at : 7 * at + 7]

        @pl.when(turn[0] == number)
        def _():
            halves = [slice(0, EDGE), slice(EDGE, 2 * EDGE)]
            fetch(
                *[(share.at[half, EDGE : EDGE + ONE], rows.at[half]) for half in range(2)],
                *[(low.at[halves[half]], edges.at[half, :EDGE]) for half in range(2)],
                *[(high.at[halves[half]], edges.at[half, EDGE:]) for half in range(2)],
            )
            rows[...] = (rows[...].astype(jnp.float32) + edges[...].astype(jnp.float32)).astype(jnp.bfloat16)

        @pl.when(turn[0] == number - 1)
        def _():
            start = pl.multiple_of(side * ONE, ONE)
            fetch((state.at[0, pl.ds(start, ONE)], rows.at[side]), (crossed.at[:ONE], rows.at[1 - side]))

        @pl.when(turn[0] == number - 2)
        def _():
            fetch((back, rows))

        @pl.when(turn[0] == number - 3)
        def _():
            fetch((last, rows))

    flat = rows[...].reshape(2 * ONE, FN)
    full = lax.dot_general(flat, flat, (((1,), (1,)), ((), ())), preferred_element_type=jnp.float32)
    lines = []
    for first in range(2):
        line = []
        for second in range(2):
            block = None
            for point in range(POINTS):
                down, along = first * ONE + point * HALF, second * ONE + point * HALF
                term = full[down : down + HALF, along : along + HALF]
                block = term if block is None else block + term
            line.append(block)
        lines.append(jnp.concatenate(line, 1))
    total = jnp.concatenate(lines, 0)
    gram[...] = total


def factor_kernel(scale, first, second, rows, by_column, by_place, same_point, basis, upper):
    eye = (
        lax.broadcasted_iota(jnp.int32, (K, K), 0) == lax.broadcasted_iota(jnp.int32, (K, K), 1)
    ).astype(jnp.float32)
    table = jnp.concatenate([(first[...] + second[...]) * scale, eye], 1)
    row_index = lax.broadcasted_iota(jnp.int32, (K, 2 * K), 0)
    roots = jnp.zeros((K, 2 * K), jnp.float32)
    for j in range(0, K, STEP):
        lines = [table[j + m : j + m + 1, :] for m in range(STEP)]
        columns = [jnp.broadcast_to(table[:, j + m : j + m + 1], table.shape) for m in range(STEP)]
        entries = [
            [jnp.broadcast_to(lines[m][:, j + k : j + k + 1], lines[m].shape) for k in range(STEP)]
            for m in range(STEP)
        ]
        below = table
        for m in range(STEP):
            inverse = 1.0 / entries[m][m]
            for k in range(m + 1, STEP):
                ratio = entries[m][k] * inverse
                for n in range(k, STEP):
                    entries[k][n] = entries[k][n] - ratio * entries[m][n]
                lines[k] = lines[k] - ratio * lines[m]
                columns[k] = columns[k] - ratio * columns[m]
            below = below - columns[m] * (inverse * lines[m])
            roots = jnp.where(row_index == j + m, lax.rsqrt(entries[m][m]), roots)
        table = jnp.where(row_index >= j + STEP, below, table)
        for m in range(STEP):
            table = jnp.where(row_index == j + m, lines[m], table)
    table = table * roots
    column = lax.broadcasted_iota(jnp.int32, (K, K), 1)
    row = lax.broadcasted_iota(jnp.int32, (K, K), 0)
    upper[...] = jnp.where(column >= row, table[:, :K], 0.0)
    inverse = table[:, K:]
    terms = []
    for _ in range(2):
        term = inverse.astype(jnp.bfloat16)
        inverse = inverse - term.astype(jnp.float32)
        tall = lax.dot_general(
            by_column[...], term, (((1,), (1,)), ((), ())), preferred_element_type=jnp.float32
        ).astype(jnp.bfloat16)
        spread = lax.dot_general(
            tall, by_place[...], (((1,), (0,)), ((), ())), preferred_element_type=jnp.float32
        )
        terms.append((spread * same_point[...]).astype(jnp.bfloat16))
    both = lax.dot_general(
        rows[...], jnp.concatenate(terms, 1), (((0,), (0,)), ((), ())), preferred_element_type=jnp.float32
    )
    total = both[:, : POINTS * K] + both[:, POINTS * K :]
    basis[...] = total.astype(jnp.bfloat16)


def local(inverse_blocks, coupling, sources):
    sections = lax.axis_size("section")
    spans = lax.axis_size("span")
    pairs = spans // 2
    assert sections % 4 == 0 and spans % 2 == 0 and sources.shape[2] == POINTS * K
    group = lax.axis_index("section")
    side = (lax.axis_index("span") % 2).astype(jnp.int32)

    def send(value, *legs):
        routes = []
        for groups, down, route in legs:
            for g in groups:
                for s in range(spans):
                    routes.append((g * spans + s, (g - down) % sections * spans + route(s)))
        return lax.ppermute(value, AXES, routes)

    def straight(s):
        return s

    def partner(s):
        return s ^ 1

    def neighbor(shift):
        return lambda s: (s + shift) % spans

    def pair_route(pair, side):
        return (pair % pairs) * 2 + side

    def outward(s):
        return pair_route(s // 2 + 2 * (s % 2) - 1, s % 2)

    def outward_cross(s):
        return pair_route(s // 2 + 2 * (s % 2) - 1, 1 - s % 2)

    def inward(s):
        return pair_route(s // 2 + 1 - 2 * (s % 2), s % 2)

    def of_kind(kind):
        return [g for g in range(sections) if (sections - 1 - g) % 4 == kind]

    turn = jnp.stack([group.astype(jnp.int32), side, ((sections - 1 - group) % 4).astype(jnp.int32)])

    half, point, column = np.meshgrid(np.arange(2), np.arange(POINTS), np.arange(HALF), indexing="ij")
    row_column = (half * HALF + column).reshape(-1)
    row_point = point.reshape(-1)
    place = np.arange(POINTS * K)
    by_column = jnp.asarray(np.arange(K)[None, :] == row_column[:, None], jnp.bfloat16)
    by_place = jnp.asarray(np.arange(K)[:, None] == place[None, :] % K, jnp.bfloat16)
    same_point = jnp.asarray(place[None, :] // K == row_point[:, None], jnp.float32)

    smem = pl.BlockSpec(memory_space=pltpu.SMEM)
    vmem = pl.BlockSpec(memory_space=pltpu.VMEM)
    away = pl.BlockSpec(memory_space=pl.ANY)
    raw = sources[0]
    odds, evens = list(range(1, sections, 2)), list(range(0, sections, 2))
    below = send(raw, (evens, -1, straight), (odds, 1, straight))
    incoming = None
    pair_source = wide_source = None
    candidates = []
    for g in reversed(of_kind(0)):
        pieces = [] if incoming is None else [(incoming, lambda side: (0, 0), ONE, None)]
        (share,) = march(turn, g, inverse_blocks, coupling, pieces, 0, 2, POINTS, True, (raw,))
        crossed, edge_cross, edge_same, direct, whole = pl.pallas_call(
            functools.partial(ship_kernel, g),
            out_shape=[jax.ShapeDtypeStruct((size, FN), jnp.bfloat16) for size in (2 * ONE, WIDE, WIDE, 2 * ONE)]
            + [jax.ShapeDtypeStruct(share.shape, jnp.bfloat16)],
            in_specs=[smem, vmem, vmem, vmem],
            out_specs=[vmem] * 5,
            scratch_shapes=[pltpu.VMEM((2, ONE, FN), jnp.float32)],
            compiler_params=pltpu.CompilerParams(vmem_limit_bytes=SMALL),
        )(turn, share, below, raw)
        first = incoming is None
        edge_cross = send(edge_cross, ([g], 1, outward_cross), (of_kind(3) if first else [], 0, neighbor(1)))
        crossed = send(crossed, ([g], 1, partner), (of_kind(2) if first else [], 0, partner))
        edge_same = send(edge_same, ([g], 1, outward), (of_kind(3) if first else [], 0, neighbor(-1)))
        direct = send(direct, ([g], 1, straight))
        if first:
            pair_source = [
                (whole, lambda side: (0, side * ONE), ONE, lambda side: side),
                (crossed, lambda side: (0, (1 - side) * ONE), ONE, None),
            ]
            wide_source = [
                (edge_cross.reshape(2, EDGE, FN), lambda side: (0, 0), EDGE, None),
                (whole, lambda side: (0, EDGE), ONE, None),
                (edge_same.reshape(2, EDGE, FN), lambda side: (0, EDGE + ONE), EDGE, None),
            ]

        (state,) = march(
            turn,
            g - 1,
            inverse_blocks,
            coupling,
            [
                (crossed, lambda side: (0, (1 - side) * ONE), 2 * ONE, None),
                (edge_cross, lambda side: (0, side * 2 * ONE), WIDE, None),
                (edge_same, lambda side: (0, (1 - side) * 2 * ONE), WIDE, None),
                (direct, lambda side: (0, side * ONE), 2 * ONE, None),
            ],
            14,
            1,
            3 * POINTS,
            False,
        )
        arrived = send(state, (list(range(sections)), 1, straight))

        crossed, edge_cross, edge_same, direct = march(
            turn,
            g - 2,
            inverse_blocks,
            coupling,
            [(arrived, lambda side: (0, 0), 2 * ONE, None)] + pair_source,
            10,
            1,
            2 * POINTS,
            True,
            (),
            (
                (share, state),
                (
                    (
                        0,
                        g,
                        (
                            (0, lambda side: 0, lambda side: EDGE + ONE, EDGE, 1, 0),
                            (0, lambda side: 1, lambda side: EDGE + ONE, EDGE, 1, EDGE),
                            (0, lambda side: 0, lambda side: 0, EDGE, 2, 0),
                            (0, lambda side: 1, lambda side: 0, EDGE, 2, EDGE),
                        ),
                    ),
                    (0, g - 1, ((1, lambda side: 0, lambda side: (1 - side) * ONE, ONE, 0, 0),)),
                ),
                (
                    lambda side: (1 - side) * ONE,
                    lambda side: side * 2 * ONE,
                    lambda side: (1 - side) * 2 * ONE,
                    lambda side: side * ONE,
                ),
            ),
        )
        edge_cross = send(edge_cross, ([g - 2], 1, outward_cross), ([g], 0, neighbor(1)))
        crossed = send(crossed, ([g - 2], 1, partner), ([g - 1], 0, partner))
        edge_same = send(edge_same, ([g - 2], 1, inward), ([g], 0, neighbor(-1)))
        direct = send(direct, ([g - 2], 1, straight))

        middle = pl.pallas_call(
            functools.partial(center_kernel, g - 3),
            out_shape=jax.ShapeDtypeStruct((2, ONE, FN), jnp.bfloat16),
            in_specs=[smem] + [vmem] * 4,
            out_specs=vmem,
            compiler_params=pltpu.CompilerParams(vmem_limit_bytes=SMALL),
        )(turn, direct, crossed, edge_same, edge_cross)
        back = send(middle, (evens, -1, straight), (odds, 1, straight))
        (last,) = march(
            turn,
            g - 3,
            inverse_blocks,
            coupling,
            [
                (crossed, lambda side: (1 - side, 0), 2 * ONE, None),
                (edge_cross, lambda side: (1 - side, side * ONE), WIDE, None),
                (edge_same, lambda side: (side, side * ONE), WIDE, None),
                (direct, lambda side: (side, 0), 2 * ONE, None),
            ]
            + wide_source,
            0,
            2,
            2 * POINTS,
            False,
        )
        candidates += [share, edge_cross, edge_same, state, crossed, back, last]
        if g > 3:
            incoming = send(last, ([g - 3], 1, straight))

    rows, gram = pl.pallas_call(
        functools.partial(gram_kernel, list(reversed(of_kind(0)))),
        out_shape=(
            jax.ShapeDtypeStruct((2, ONE, FN), jnp.bfloat16),
            jax.ShapeDtypeStruct((K, K), jnp.float32),
        ),
        in_specs=[smem] + [away] * len(candidates),
        out_specs=(vmem, vmem),
        scratch_shapes=[pltpu.VMEM((2, ONE, FN), jnp.bfloat16), pltpu.SemaphoreType.DMA((6,))],
        compiler_params=pltpu.CompilerParams(vmem_limit_bytes=SMALL),
    )(turn, *candidates)
    stride = 1
    terms = [gram]
    while stride < spans:
        radix = 2 if stride == 1 else min(4, spans // stride)
        total = terms[0]
        for term in terms[1:]:
            total = total + term
        terms = [total] + [
            lax.ppermute(total, "span", [(s, s ^ (digit * stride)) for s in range(spans)])
            for digit in range(1, radix)
        ]
        if radix == 4:
            terms = [terms[0] + terms[1], terms[2] + terms[3]]
        stride *= radix

    basis, upper = pl.pallas_call(
        functools.partial(factor_kernel, 1.0 / float(FN * POINTS * spans)),
        out_shape=(
            jax.ShapeDtypeStruct((FN, POINTS * K), jnp.bfloat16),
            jax.ShapeDtypeStruct((K, K), jnp.float32),
        ),
        in_specs=[vmem] * 6,
        out_specs=(vmem, vmem),
        compiler_params=pltpu.CompilerParams(vmem_limit_bytes=SMALL),
    )(*terms, rows.reshape(POINTS * K, FN), by_column, by_place, same_point)
    return (basis[None], upper[None])


def solution(mesh):
    placed = (P("section", None, None), P("section", None), P("section", None, "span"))
    return jax.shard_map(
        local,
        mesh=mesh,
        in_specs=placed,
        out_specs=(P("section", None, "span"), P("section", None, None)),
        check_vma=False,
    )
```

profile of v0, /device:TPU:0, one launch (start us, length us, event | category | flops | bytes accessed | tf_op | source)
XLA Modules:
  0.0 81.2 jit_solution(11005500460005901482)
XLA Ops:
  0.6 0.5 collective-permute-start
  1.1 0.1 pad_add_fusion.turn
  1.2 0.0 copy-start
  1.2 1.1 %copy-done = bf16[1,768,384]{2,1,0:T(8,128)(2,1)S(1)} copy-done((bf16[1,768,384]{2,1,0:T(8,128)(2,1)S(1)}, bf16[1,768,384]{2,1,0:T(8,128)(2,1)}, u32[]{:S(2)}) %copy-start) | copy-done | bytes 589848
  2.3 0.0 copy-start.4
  2.3 0.7 copy-done.4
  3.0 0.6 shard_map.77.share.refs_3_.refs_0_
  3.6 0.0 collective-permute-done.below
  3.6 1.1 %shard_map.78 = (bf16[384,768]{1,0:T(8,128)(2,1)S(1)}, bf16[192,768]{1,0:T(8,128)(2,1)S(1)}, bf16[192,768]{1,0:T(8,128)(2,1)S(1)}, bf16[384,768]{1,0:T(8,128)(2,1)S(1)}, bf16[2,384,768]{2,1,0:T(8,128)(2,1)S(1)}) custom-call(s32[3]{0:T(128)S(1)} %pad_add_fusion.turn, bf16[2,384,768]{2,1,0:T(8,128)(2,1)S(1)} %shard_map.77.share.refs_3_.refs_0_, ...), custom_call_target="tpu_custom_call" | custom-call | tf_op jit(solution)/shard_map/pallas_call | solution.py:429
  4.7 0.7 collective-permute-start.1
  5.4 0.7 collective-permute-start.4
  6.1 4.5 %collective-permute-start.2 = (bf16[192,768]{1,0:T(8,128)(2,1)S(1)}, bf16[192,768]{1,0:T(8,128)(2,1)S(1)}, u32[]{:S(2)}, u32[]{:S(2)}) collective-permute-start(bf16[192,768]{1,0:T(8,128)(2,1)S(1)} %get-tuple-element.16), channel_id=1, source_target_pairs={{24,23},{25,18},{26,17},{27,20},{28,19},{29,22},{30,21},{31,16},{0... | collective-permute-start | bytes 884744 | tf_op jit(solution)/shard_map/ppermute | solution.py:381
  10.6 5.0 %collective-permute-start.3 = (bf16[192,768]{1,0:T(8,128)(2,1)S(1)}, bf16[192,768]{1,0:T(8,128)(2,1)S(1)}, u32[]{:S(2)}, u32[]{:S(2)}) collective-permute-start(bf16[192,768]{1,0:T(8,128)(2,1)S(1)} %get-tuple-element.17), channel_id=1, source_target_pairs={{24,22},{25,19},{26,16},{27,21},{28,18},{29,23},{30,20},{31,17},{0... | collective-permute-start | bytes 884744 | tf_op jit(solution)/shard_map/ppermute | solution.py:381
  15.5 5.6 %collective-permute-done.2.refs_1_ = bf16[192,768]{1,0:T(8,128)(2,1)S(1)} collective-permute-done((bf16[192,768]{1,0:T(8,128)(2,1)S(1)}, bf16[192,768]{1,0:T(8,128)(2,1)S(1)}, u32[]{:S(2)}, u32[]{:S(2)}) %collective-permute-start.2) | collective-permute-done | bytes 294944 | tf_op jit(solution)/shard_map/ppermute | solution.py:381
  21.2 1.9 %collective-permute-done.3.refs_2_ = bf16[192,768]{1,0:T(8,128)(2,1)S(1)} collective-permute-done((bf16[192,768]{1,0:T(8,128)(2,1)S(1)}, bf16[192,768]{1,0:T(8,128)(2,1)S(1)}, u32[]{:S(2)}, u32[]{:S(2)}) %collective-permute-start.3) | collective-permute-done | bytes 294944 | tf_op jit(solution)/shard_map/ppermute | solution.py:381
  23.1 0.0 collective-permute-done.1.refs_0_.refs_2_
  23.1 0.0 collective-permute-done.4.refs_3_
  23.1 0.6 shard_map.79.refs_4_.refs_3_
  23.7 0.8 %collective-permute-start.5 = (bf16[1,384,768]{2,1,0:T(8,128)(2,1)S(1)}, bf16[1,384,768]{2,1,0:T(8,128)(2,1)S(1)}, u32[]{:S(2)}, u32[]{:S(2)}) collective-permute-start(bf16[1,384,768]{2,1,0:T(8,128)(2,1)S(1)} %shard_map.79.refs_4_.refs_3_), channel_id=1, source_target_pairs={{0,24},{1,25},{2,26},{3,27},{4,28},{5,29},{6,30},{7,31},{8,0},{9,1... | collective-permute-start | bytes 1769480 | tf_op jit(solution)/shard_map/ppermute | solution.py:381
  24.5 7.4 %collective-permute-done.5.refs_0_ = bf16[1,384,768]{2,1,0:T(8,128)(2,1)S(1)} collective-permute-done((bf16[1,384,768]{2,1,0:T(8,128)(2,1)S(1)}, bf16[1,384,768]{2,1,0:T(8,128)(2,1)S(1)}, u32[]{:S(2)}, u32[]{:S(2)}) %collective-permute-start.5) | collective-permute-done | bytes 589856 | tf_op jit(solution)/shard_map/ppermute | solution.py:381
  31.9 0.6 shard_map.80
  32.5 1.3 %collective-permute-start.8 = (bf16[384,768]{1,0:T(8,128)(2,1)S(1)}, bf16[384,768]{1,0:T(8,128)(2,1)S(1)}, u32[]{:S(2)}, u32[]{:S(2)}) collective-permute-start(bf16[384,768]{1,0:T(8,128)(2,1)S(1)} %get-tuple-element.22), channel_id=1, source_target_pairs={{8,1},{9,0},{10,3},{11,2},{12,5},{13,4},{14,7},{15,6},{16,17},{17,... | collective-permute-start | bytes 1769480 | tf_op jit(solution)/shard_map/ppermute | solution.py:381
  33.8 1.5 %collective-permute-start.9 = (bf16[384,768]{1,0:T(8,128)(2,1)S(1)}, bf16[384,768]{1,0:T(8,128)(2,1)S(1)}, u32[]{:S(2)}, u32[]{:S(2)}) collective-permute-start(bf16[384,768]{1,0:T(8,128)(2,1)S(1)} %get-tuple-element.23), channel_id=1, source_target_pairs={{8,0},{9,1},{10,2},{11,3},{12,4},{13,5},{14,6},{15,7}} | collective-permute-start | bytes 1769480 | tf_op jit(solution)/shard_map/ppermute | solution.py:381
  35.3 1.3 %collective-permute-start.6 = (bf16[192,768]{1,0:T(8,128)(2,1)S(1)}, bf16[192,768]{1,0:T(8,128)(2,1)S(1)}, u32[]{:S(2)}, u32[]{:S(2)}) collective-permute-start(bf16[192,768]{1,0:T(8,128)(2,1)S(1)} %get-tuple-element.20), channel_id=1, source_target_pairs={{8,7},{9,2},{10,1},{11,4},{12,3},{13,6},{14,5},{15,0},{24,25},{25,... | collective-permute-start | bytes 884744 | tf_op jit(solution)/shard_map/ppermute | solution.py:381
  36.6 1.3 %collective-permute-start.7 = (bf16[192,768]{1,0:T(8,128)(2,1)S(1)}, bf16[192,768]{1,0:T(8,128)(2,1)S(1)}, u32[]{:S(2)}, u32[]{:S(2)}) collective-permute-start(bf16[192,768]{1,0:T(8,128)(2,1)S(1)} %get-tuple-element.21), channel_id=1, source_target_pairs={{8,2},{9,7},{10,4},{11,1},{12,6},{13,3},{14,0},{15,5},{24,31},{25,... | collective-permute-start | bytes 884744 | tf_op jit(solution)/shard_map/ppermute | solution.py:381
  37.9 18.8 %collective-permute-done.6.edge_cross.refs_1_ = bf16[192,768]{1,0:T(8,128)(2,1)S(1)} collective-permute-done((bf16[192,768]{1,0:T(8,128)(2,1)S(1)}, bf16[192,768]{1,0:T(8,128)(2,1)S(1)}, u32[]{:S(2)}, u32[]{:S(2)}) %collective-permute-start.6) | collective-permute-done | bytes 294944 | tf_op jit(solution)/shard_map/ppermute | solution.py:381
  56.8 3.1 %collective-permute-done.7.edge_same.refs_2_ = bf16[192,768]{1,0:T(8,128)(2,1)S(1)} collective-permute-done((bf16[192,768]{1,0:T(8,128)(2,1)S(1)}, bf16[192,768]{1,0:T(8,128)(2,1)S(1)}, u32[]{:S(2)}, u32[]{:S(2)}) %collective-permute-start.7) | collective-permute-done | bytes 294944 | tf_op jit(solution)/shard_map/ppermute | solution.py:381
  59.8 0.0 collective-permute-done.8.crossed.refs_0_.refs_4_
  59.8 0.0 collective-permute-done.9.direct.refs_3_
  59.8 0.7 shard_map.81
  60.5 0.1 collective-permute-start.10
  60.6 5.6 %shard_map.82.refs_6_ = bf16[2,192,768]{2,1,0:T(8,128)(2,1)S(1)} custom-call(s32[3]{0:T(128)S(1)} %pad_add_fusion.turn, f32[4,768]{1,0:T(4,128)S(1)} %copy-done.4, bf16[4,768,768]{2,1,0:T(8,128)(2,1)} %weights.7, bf16[384,768]{1,0:T(8,128)(2,1)S(1)} %collective-permute-done.8.crossed.refs_0_.refs_4_, ...), custom_call_target="tpu_custom_call" | custom-call | flops 2491416576 | bytes 4718592 | tf_op jit(solution)/shard_map/pallas_call | solution.py:179
  66.2 0.0 copy-start.1
  66.2 0.0 copy-start.2
  66.2 0.0 copy-start.3
  66.2 0.0 collective-permute-done.10.refs_5_
  66.2 1.4 %shard_map.83 = (bf16[2,192,768]{2,1,0:T(8,128)(2,1)S(1)}, f32[48,48]{1,0:T(8,128)S(1)}) custom-call(s32[3]{0:T(128)S(1)} %pad_add_fusion.turn, bf16[2,384,768]{2,1,0:T(8,128)(2,1)S(1)} %shard_map.77.share.refs_3_.refs_0_, bf16[192,768]{1,0:T(8,128)(2,1)S(1)} %collective-permute-done.6.edge_cross.refs_1_, ...), custom_call_target="tpu_custom_call" | custom-call | tf_op jit(solution)/shard_map/pallas_call | solution.py:540
  67.6 0.1 collective-permute-start.11
  67.7 3.8 %collective-permute-done.11 = f32[48,48]{1,0:T(8,128)S(1)} collective-permute-done((f32[48,48]{1,0:T(8,128)S(1)}, f32[48,48]{1,0:T(8,128)S(1)}, u32[]{:S(2)}, u32[]{:S(2)}) %collective-permute-start.11) | collective-permute-done | bytes 9248 | tf_op jit(solution)/shard_map/ppermute | solution.py:559
  71.5 0.0 collective-permute-start.12
  71.5 1.4 %collective-permute-start.14 = (f32[48,48]{1,0:T(8,128)S(1)}, f32[48,48]{1,0:T(8,128)S(1)}, u32[]{:S(2)}, u32[]{:S(2)}) collective-permute-start(f32[48,48]{1,0:T(8,128)S(1)} %add.18), channel_id=1, source_target_pairs={{0,6},{1,7},{2,4},{3,5},{4,2},{5,3},{6,0},{7,1},{8,14},{9,15},{10,... | collective-permute-start | bytes 27656 | tf_op jit(solution)/shard_map/ppermute | solution.py:559
  72.9 2.1 %collective-permute-start.13 = (f32[48,48]{1,0:T(8,128)S(1)}, f32[48,48]{1,0:T(8,128)S(1)}, u32[]{:S(2)}, u32[]{:S(2)}) collective-permute-start(f32[48,48]{1,0:T(8,128)S(1)} %add.18), channel_id=1, source_target_pairs={{0,4},{1,5},{2,6},{3,7},{4,0},{5,1},{6,2},{7,3},{8,12},{9,13},{10,... | collective-permute-start | bytes 27656 | tf_op jit(solution)/shard_map/ppermute | solution.py:559
  75.0 0.3 collective-permute-done.12
  75.3 1.9 %collective-permute-done.14 = f32[48,48]{1,0:T(8,128)S(1)} collective-permute-done((f32[48,48]{1,0:T(8,128)S(1)}, f32[48,48]{1,0:T(8,128)S(1)}, u32[]{:S(2)}, u32[]{:S(2)}) %collective-permute-start.14) | collective-permute-done | bytes 9248 | tf_op jit(solution)/shard_map/ppermute | solution.py:559
  77.2 0.5 collective-permute-done.13
  77.6 0.0 copy-done.1
  77.6 0.0 copy-done.2
  77.7 0.0 copy-done.3
  77.7 3.5 %shard_map.84 = (bf16[768,384]{1,0:T(8,128)(2,1)}, f32[48,48]{1,0:T(8,128)}) custom-call(f32[48,48]{1,0:T(8,128)S(1)} %add.19.first, f32[48,48]{1,0:T(8,128)S(1)} %add.20.second, bf16[384,768]{1,0:T(8,128)(2,1)S(1)} %bitcast.12, bf16[384,48]{1,0:T(8,128)(2,1)S(1)} %copy-done.2, bf16[48,384]{1,0:T(8,128)(2,1)S(1)} %copy-done.3, f32[384,384]{1,0:T(8,128)S(1)} %copy-done.1), custom_call_target="tpu_custom_call" | custom-call | tf_op jit(solution)/shard_map/pallas_call | solution.py:566
  (3 shorter events, 0.0 us)
Async XLA Ops:
  0.6 3.0 %collective-permute-start = (bf16[768,384]{1,0:T(8,128)(2,1)}, bf16[768,384]{1,0:T(8,128)(2,1)S(1)}, u32[]{:S(2)}, u32[]{:S(2)}) collective-permute-start(bf16[768,384]{1,0:T(8,128)(2,1)} %bitcast.9), channel_id=1, source_target_pairs={{0,8},{1,9},{2,10},{3,11},{4,12},{5,13},{6,14},{7,15},{16,24},{17,... | collective-permute-start | bytes 1769480 | tf_op jit(solution)/shard_map/ppermute | solution.py:381
  1.2 1.1 %copy-start = (bf16[1,768,384]{2,1,0:T(8,128)(2,1)S(1)}, bf16[1,768,384]{2,1,0:T(8,128)(2,1)}, u32[]{:S(2)}) copy-start(bf16[1,768,384]{2,1,0:T(8,128)(2,1)} %param.8) | copy-start | bytes 1769476
  2.3 0.7 copy-start.4
  4.7 18.4 %collective-permute-start.1 = (bf16[384,768]{1,0:T(8,128)(2,1)S(1)}, bf16[384,768]{1,0:T(8,128)(2,1)S(1)}, u32[]{:S(2)}, u32[]{:S(2)}) collective-permute-start(bf16[384,768]{1,0:T(8,128)(2,1)S(1)} %get-tuple-element.15), channel_id=1, source_target_pairs={{24,17},{25,16},{26,19},{27,18},{28,21},{29,20},{30,23},{31,22},{8... | collective-permute-start | bytes 1769480 | tf_op jit(solution)/shard_map/ppermute | solution.py:381
  5.4 17.7 %collective-permute-start.4 = (bf16[384,768]{1,0:T(8,128)(2,1)S(1)}, bf16[384,768]{1,0:T(8,128)(2,1)S(1)}, u32[]{:S(2)}, u32[]{:S(2)}) collective-permute-start(bf16[384,768]{1,0:T(8,128)(2,1)S(1)} %get-tuple-element.18), channel_id=1, source_target_pairs={{24,16},{25,17},{26,18},{27,19},{28,20},{29,21},{30,22},{31,23}} | collective-permute-start | bytes 1769480 | tf_op jit(solution)/shard_map/ppermute | solution.py:381
  6.1 15.1 %collective-permute-start.2 = (bf16[192,768]{1,0:T(8,128)(2,1)S(1)}, bf16[192,768]{1,0:T(8,128)(2,1)S(1)}, u32[]{:S(2)}, u32[]{:S(2)}) collective-permute-start(bf16[192,768]{1,0:T(8,128)(2,1)S(1)} %get-tuple-element.16), channel_id=1, source_target_pairs={{24,23},{25,18},{26,17},{27,20},{28,19},{29,22},{30,21},{31,16},{0... | collective-permute-start | bytes 884744 | tf_op jit(solution)/shard_map/ppermute | solution.py:381
  10.6 12.5 %collective-permute-start.3 = (bf16[192,768]{1,0:T(8,128)(2,1)S(1)}, bf16[192,768]{1,0:T(8,128)(2,1)S(1)}, u32[]{:S(2)}, u32[]{:S(2)}) collective-permute-start(bf16[192,768]{1,0:T(8,128)(2,1)S(1)} %get-tuple-element.17), channel_id=1, source_target_pairs={{24,22},{25,19},{26,16},{27,21},{28,18},{29,23},{30,20},{31,17},{0... | collective-permute-start | bytes 884744 | tf_op jit(solution)/shard_map/ppermute | solution.py:381
  23.7 8.2 %collective-permute-start.5 = (bf16[1,384,768]{2,1,0:T(8,128)(2,1)S(1)}, bf16[1,384,768]{2,1,0:T(8,128)(2,1)S(1)}, u32[]{:S(2)}, u32[]{:S(2)}) collective-permute-start(bf16[1,384,768]{2,1,0:T(8,128)(2,1)S(1)} %shard_map.79.refs_4_.refs_3_), channel_id=1, source_target_pairs={{0,24},{1,25},{2,26},{3,27},{4,28},{5,29},{6,30},{7,31},{8,0},{9,1... | collective-permute-start | bytes 1769480 | tf_op jit(solution)/shard_map/ppermute | solution.py:381
  32.5 27.3 %collective-permute-start.8 = (bf16[384,768]{1,0:T(8,128)(2,1)S(1)}, bf16[384,768]{1,0:T(8,128)(2,1)S(1)}, u32[]{:S(2)}, u32[]{:S(2)}) collective-permute-start(bf16[384,768]{1,0:T(8,128)(2,1)S(1)} %get-tuple-element.22), channel_id=1, source_target_pairs={{8,1},{9,0},{10,3},{11,2},{12,5},{13,4},{14,7},{15,6},{16,17},{17,... | collective-permute-start | bytes 1769480 | tf_op jit(solution)/shard_map/ppermute | solution.py:381
  33.8 26.0 %collective-permute-start.9 = (bf16[384,768]{1,0:T(8,128)(2,1)S(1)}, bf16[384,768]{1,0:T(8,128)(2,1)S(1)}, u32[]{:S(2)}, u32[]{:S(2)}) collective-permute-start(bf16[384,768]{1,0:T(8,128)(2,1)S(1)} %get-tuple-element.23), channel_id=1, source_target_pairs={{8,0},{9,1},{10,2},{11,3},{12,4},{13,5},{14,6},{15,7}} | collective-permute-start | bytes 1769480 | tf_op jit(solution)/shard_map/ppermute | solution.py:381
  35.3 21.4 %collective-permute-start.6 = (bf16[192,768]{1,0:T(8,128)(2,1)S(1)}, bf16[192,768]{1,0:T(8,128)(2,1)S(1)}, u32[]{:S(2)}, u32[]{:S(2)}) collective-permute-start(bf16[192,768]{1,0:T(8,128)(2,1)S(1)} %get-tuple-element.20), channel_id=1, source_target_pairs={{8,7},{9,2},{10,1},{11,4},{12,3},{13,6},{14,5},{15,0},{24,25},{25,... | collective-permute-start | bytes 884744 | tf_op jit(solution)/shard_map/ppermute | solution.py:381
  36.6 23.2 %collective-permute-start.7 = (bf16[192,768]{1,0:T(8,128)(2,1)S(1)}, bf16[192,768]{1,0:T(8,128)(2,1)S(1)}, u32[]{:S(2)}, u32[]{:S(2)}) collective-permute-start(bf16[192,768]{1,0:T(8,128)(2,1)S(1)} %get-tuple-element.21), channel_id=1, source_target_pairs={{8,2},{9,7},{10,4},{11,1},{12,6},{13,3},{14,0},{15,5},{24,31},{25,... | collective-permute-start | bytes 884744 | tf_op jit(solution)/shard_map/ppermute | solution.py:381
  60.5 5.7 %collective-permute-start.10 = (bf16[2,192,768]{2,1,0:T(8,128)(2,1)S(1)}, bf16[2,192,768]{2,1,0:T(8,128)(2,1)S(1)}, u32[]{:S(2)}, u32[]{:S(2)}) collective-permute-start(bf16[2,192,768]{2,1,0:T(8,128)(2,1)S(1)} %shard_map.81), channel_id=1, source_target_pairs={{0,8},{1,9},{2,10},{3,11},{4,12},{5,13},{6,14},{7,15},{16,24},{17,... | collective-permute-start | bytes 1769480 | tf_op jit(solution)/shard_map/ppermute | solution.py:381
  66.2 11.5 %copy-start.1 = (f32[384,384]{1,0:T(8,128)S(1)}, f32[384,384]{1,0:T(8,128)}, u32[]{:S(2)}) copy-start(f32[384,384]{1,0:T(8,128)} %constant.40.clone.same_point) | copy-start | bytes 1769476
  66.2 11.5 %copy-start.2 = (bf16[384,48]{1,0:T(8,128)(2,1)S(1)}, bf16[384,48]{1,0:T(8,128)(2,1)}, u32[]{:S(2)}) copy-start(bf16[384,48]{1,0:T(8,128)(2,1)} %constant.38.clone.by_column) | copy-start | bytes 110596
  66.2 11.5 %copy-start.3 = (bf16[48,384]{1,0:T(8,128)(2,1)S(1)}, bf16[48,384]{1,0:T(8,128)(2,1)}, u32[]{:S(2)}) copy-start(bf16[48,384]{1,0:T(8,128)(2,1)} %constant.39.clone.by_place) | copy-start | bytes 110596
  67.6 3.9 %collective-permute-start.11 = (f32[48,48]{1,0:T(8,128)S(1)}, f32[48,48]{1,0:T(8,128)S(1)}, u32[]{:S(2)}, u32[]{:S(2)}) collective-permute-start(f32[48,48]{1,0:T(8,128)S(1)} %get-tuple-element.24), channel_id=1, source_target_pairs={{0,1},{1,0},{2,3},{3,2},{4,5},{5,4},{6,7},{7,6},{8,9},{9,8},{10,11... | collective-permute-start | bytes 27656 | tf_op jit(solution)/shard_map/ppermute | solution.py:559
  71.5 3.8 %collective-permute-start.12 = (f32[48,48]{1,0:T(8,128)S(1)}, f32[48,48]{1,0:T(8,128)S(1)}, u32[]{:S(2)}, u32[]{:S(2)}) collective-permute-start(f32[48,48]{1,0:T(8,128)S(1)} %add.18), channel_id=1, source_target_pairs={{0,2},{1,3},{2,0},{3,1},{4,6},{5,7},{6,4},{7,5},{8,10},{9,11},{10,... | collective-permute-start | bytes 27656 | tf_op jit(solution)/shard_map/ppermute | solution.py:559
  71.5 5.7 %collective-permute-start.14 = (f32[48,48]{1,0:T(8,128)S(1)}, f32[48,48]{1,0:T(8,128)S(1)}, u32[]{:S(2)}, u32[]{:S(2)}) collective-permute-start(f32[48,48]{1,0:T(8,128)S(1)} %add.18), channel_id=1, source_target_pairs={{0,6},{1,7},{2,4},{3,5},{4,2},{5,3},{6,0},{7,1},{8,14},{9,15},{10,... | collective-permute-start | bytes 27656 | tf_op jit(solution)/shard_map/ppermute | solution.py:559
  72.9 4.7 %collective-permute-start.13 = (f32[48,48]{1,0:T(8,128)S(1)}, f32[48,48]{1,0:T(8,128)S(1)}, u32[]{:S(2)}, u32[]{:S(2)}) collective-permute-start(f32[48,48]{1,0:T(8,128)S(1)} %add.18), channel_id=1, source_target_pairs={{0,4},{1,5},{2,6},{3,7},{4,0},{5,1},{6,2},{7,3},{8,12},{9,13},{10,... | collective-permute-start | bytes 27656 | tf_op jit(solution)/shard_map/ppermute | solution.py:559
where the time goes:
time: 81.5 us; the launch traced here: 81.2 us
  waiting for transfers between devices  43.3 us (53%)
  starting transfers between devices  21.1 us (26%)
  Pallas kernels  14 us (17%)
  local copies, waits for them, and re-layouts  1.79 us (2%)
  between operations  0.84 us (1%)
    ppermute x11, waiting for transfers between devices, send(): return lax.ppermute(value, AXES, routes)  36.9 us
    ppermute x11, starting transfers between devices, send(): return lax.ppermute(value, AXES, routes)  17.6 us
    pallas_call x4, Pallas kernels, march(): pl.pallas_call(functools.partial(march_kernel, number, [piece[1:] for pie...  7.33 us
    ppermute x4, waiting for transfers between devices, local(): lax.ppermute(total, 'span', [(s, s ^ digit * stride) for s in range(spans)])  6.47 us
    ppermute x4, starting transfers between devices, local(): lax.ppermute(total, 'span', [(s, s ^ digit * stride) for s in range(spans)])  3.56 us
    pallas_call x1, Pallas kernels, local(): pl.pallas_call(functools.partial(factor_kernel, 1.0 / float(FN * POINTS *...  3.5 us
    unnamed x10, local copies, waits for them, and re-layouts  1.79 us
  transfers between devices with their start and end apart: 15, of which 9 were waited for; matrix products, arithmetic and copies ran while one was open for 0% of the time, Pallas kernels for 8%

commit v1 on v0

--- a/solution.py
+++ b/solution.py
@@ -120,7 +120,10 @@
                 if step + 2 < STATIONS:
                     copies[step + 2].start()
             moved = lax.dot_general(
-                current, held[step], (((1,), (1,)), ((), ())), preferred_element_type=jnp.float32
+                current,
+                held[step],
+                (((1,), (1 if raw else 0,)), ((), ())),
+                preferred_element_type=jnp.float32,
             )
             if step == STATIONS - 1:
                 result[block, at : at + rows, :] = moved.astype(jnp.bfloat16)
@@ -421,7 +424,7 @@
     odds, evens = list(range(1, sections, 2)), list(range(0, sections, 2))
     below = send(raw, (evens, -1, straight), (odds, 1, straight))
     incoming = None
-    pair_source = wide_source = None
+    pair_source = wide_source = turned_blocks = None
     candidates = []
     for g in reversed(of_kind(0)):
         pieces = [] if incoming is None else [(incoming, lambda side: (0, 0), ONE, None)]
@@ -441,6 +444,8 @@
         edge_same = send(edge_same, ([g], 1, outward), (of_kind(3) if first else [], 0, neighbor(-1)))
         direct = send(direct, ([g], 1, straight))
         if first:
+            later, _ = lax.optimization_barrier((inverse_blocks, whole))
+            turned_blocks = jnp.swapaxes(later, 1, 2)
             pair_source = [
                 (whole, lambda side: (0, side * ONE), ONE, lambda side: side),
                 (crossed, lambda side: (0, (1 - side) * ONE), ONE, None),
@@ -454,7 +459,7 @@
         (state,) = march(
             turn,
             g - 1,
-            inverse_blocks,
+            turned_blocks,
             coupling,
             [
                 (crossed, lambda side: (0, (1 - side) * ONE), 2 * ONE, None),
@@ -472,7 +477,7 @@
         crossed, edge_cross, edge_same, direct = march(
             turn,
             g - 2,
-            inverse_blocks,
+            turned_blocks,
             coupling,
             [(arrived, lambda side: (0, 0), 2 * ONE, None)] + pair_source,
             10,
@@ -519,7 +524,7 @@
         (last,) = march(
             turn,
             g - 3,
-            inverse_blocks,
+            turned_blocks,
             coupling,
             [
                 (crossed, lambda side: (1 - side, 0), 2 * ONE, None),

time: 81.5 us -> 83.9 us (1.029)
  waiting for transfers between devices: 43.3 us -> 33.5 us
  local copies, waits for them, and re-layouts: 1.79 us -> 8.47 us
  starting transfers between devices: 21.1 us -> 24.3 us
  Pallas kernels: 14 us -> 16.1 us
    ppermute x11, waiting for transfers between devices: 36.9 us -> 27 us  [send(): return lax.ppermute(value, AXES, routes)]
    optimization_barrier x0 -> x1, local copies, waits for them, and re-layouts: none -> 6.67 us  [local(): later, _ = lax.optimization_barrier((inverse_blocks, whole))]
    ppermute x11, starting transfers between devices: 17.6 us -> 20.8 us  [send(): return lax.ppermute(value, AXES, routes)]
    pallas_call x4, Pallas kernels: 7.33 us -> 8.44 us  [march(): pl.pallas_call(functools.partial(march_kernel, number, [piece[1:] for pie...]
    pallas_call x1, Pallas kernels: 1.09 us -> 2.11 us  [local(): pl.pallas_call(functools.partial(ship_kernel, g), out_shape=[jax.ShapeDty...]
    unnamed x10 -> x12, local copies, waits for them, and re-layouts: 1.79 us -> 1.8 us
  transfers between devices with their start and end apart: 15 -> 15, of which waited for: 9 -> 9; matrix products, arithmetic and copies ran while one was open for 0% -> 8% of each run, Pallas kernels for 8% -> 8%
where the time goes in v1:
time: 83.9 us; the launch traced here: 83.3 us
  waiting for transfers between devices  33.5 us (40%)
  starting transfers between devices  24.3 us (29%)
  Pallas kernels  16.1 us (19%)
  local copies, waits for them, and re-layouts  8.47 us (10%)
    ppermute x11, waiting for transfers between devices, send(): return lax.ppermute(value, AXES, routes)  27 us
    ppermute x11, starting transfers between devices, send(): return lax.ppermute(value, AXES, routes)  20.8 us
    pallas_call x4, Pallas kernels, march(): pl.pallas_call(functools.partial(march_kernel, number, [piece[1:] for pie...  8.44 us
    optimization_barrier x1, local copies, waits for them, and re-layouts, local(): later, _ = lax.optimization_barrier((inverse_blocks, whole))  6.67 us
    ppermute x4, waiting for transfers between devices, local(): lax.ppermute(total, 'span', [(s, s ^ digit * stride) for s in range(spans)])  6.48 us
    ppermute x4, starting transfers between devices, local(): lax.ppermute(total, 'span', [(s, s ^ digit * stride) for s in range(spans)])  3.56 us
    pallas_call x1, Pallas kernels, local(): pl.pallas_call(functools.partial(factor_kernel, 1.0 / float(FN * POINTS *...  3.5 us
    pallas_call x1, Pallas kernels, local(): pl.pallas_call(functools.partial(ship_kernel, g), out_shape=[jax.ShapeDty...  2.11 us
  transfers between devices with their start and end apart: 15, of which 9 were waited for; matrix products, arithmetic and copies ran while one was open for 8% of the time, Pallas kernels for 8%

profile of v1, /device:TPU:0, one launch (start us, length us, event | category | flops | bytes accessed | tf_op | source)
XLA Modules:
  0.0 83.3 jit_solution(8046497139669350962)
XLA Ops:
  0.6 0.5 collective-permute-start
  1.1 0.1 pad_add_fusion.turn
  1.2 0.0 copy-start
  1.2 1.1 %copy-done = bf16[1,768,384]{2,1,0:T(8,128)(2,1)S(1)} copy-done((bf16[1,768,384]{2,1,0:T(8,128)(2,1)S(1)}, bf16[1,768,384]{2,1,0:T(8,128)(2,1)}, u32[]{:S(2)}) %copy-start) | copy-done | bytes 589848
  2.3 0.0 copy-start.4
  2.3 0.7 copy-done.4
  3.0 0.6 shard_map.77.share.refs_3_.refs_0_
  3.6 0.0 collective-permute-done.below
  3.6 2.1 %shard_map.78 = (bf16[384,768]{1,0:T(8,128)(2,1)}, bf16[192,768]{1,0:T(8,128)(2,1)}, bf16[192,768]{1,0:T(8,128)(2,1)}, bf16[384,768]{1,0:T(8,128)(2,1)S(1)}, bf16[2,384,768]{2,1,0:T(8,128)(2,1)S(1)}) custom-call(s32[3]{0:T(128)S(1)} %pad_add_fusion.turn, bf16[2,384,768]{2,1,0:T(8,128)(2,1)S(1)} %shard_map.77.share.refs_3_.refs_0_, ...), custom_call_target="tpu_custom_call" | custom-call | tf_op jit(solution)/shard_map/pallas_call | solution.py:432
  5.7 0.7 collective-permute-start.1
  6.4 1.5 %collective-permute-start.4 = (bf16[384,768]{1,0:T(8,128)(2,1)S(1)}, bf16[384,768]{1,0:T(8,128)(2,1)}, u32[]{:S(2)}, u32[]{:S(2)}) collective-permute-start(bf16[384,768]{1,0:T(8,128)(2,1)S(1)} %get-tuple-element.21), channel_id=1, source_target_pairs={{24,16},{25,17},{26,18},{27,19},{28,20},{29,21},{30,22},{31,23}} | collective-permute-start | bytes 1769480 | tf_op jit(solution)/shard_map/ppermute | solution.py:384
  7.9 4.4 %collective-permute-start.2 = (bf16[192,768]{1,0:T(8,128)(2,1)}, bf16[192,768]{1,0:T(8,128)(2,1)}, u32[]{:S(2)}, u32[]{:S(2)}) collective-permute-start(bf16[192,768]{1,0:T(8,128)(2,1)} %get-tuple-element.19), channel_id=1, source_target_pairs={{24,23},{25,18},{26,17},{27,20},{28,19},{29,22},{30,21},{31,16},{0... | collective-permute-start | bytes 884744 | tf_op jit(solution)/shard_map/ppermute | solution.py:384
  12.4 5.0 %collective-permute-start.3 = (bf16[192,768]{1,0:T(8,128)(2,1)}, bf16[192,768]{1,0:T(8,128)(2,1)}, u32[]{:S(2)}, u32[]{:S(2)}) collective-permute-start(bf16[192,768]{1,0:T(8,128)(2,1)} %get-tuple-element.20), channel_id=1, source_target_pairs={{24,22},{25,19},{26,16},{27,21},{28,18},{29,23},{30,20},{31,17},{0... | collective-permute-start | bytes 884744 | tf_op jit(solution)/shard_map/ppermute | solution.py:384
  17.3 0.0 copy-start.5
  17.3 6.7 %copy.8 = bf16[4,768,768]{1,2,0:T(8,128)(2,1)} copy(bf16[4,768,768]{2,1,0:T(8,128)(2,1)} %weights.1) | data formatting | bytes 9437184 | tf_op jit(solution)/shard_map/optimization_barrier | solution.py:447
  24.0 0.0 collective-permute-done.2.refs_1_
  24.0 0.4 collective-permute-done.3.refs_2_
  24.4 0.0 collective-permute-done.1.refs_0_.refs_2_
  24.4 0.0 collective-permute-done.4.refs_3_
  24.4 0.0 copy-done.5
  24.4 1.3 %shard_map.79.refs_4_.refs_3_ = bf16[1,384,768]{2,1,0:T(8,128)(2,1)S(1)} custom-call(s32[3]{0:T(128)S(1)} %pad_add_fusion.turn, f32[4,768]{1,0:T(4,128)S(1)} %copy-done.5, bf16[4,768,768]{2,1,0:T(8,128)(2,1)} %bitcast.14, bf16[384,768]{1,0:T(8,128)(2,1)S(1)} %collective-permute-done.1.refs_0_.refs_2_, bf16[192,768]{1,0:T(8,128)(2,1)} %collective-permute-done.2.refs_1_, ...), custom_call_target="tpu_custom_call" | custom-call | flops 2151677952 | bytes 4718592 | tf_op jit(solution)/shard_map/pallas_call | solution.py:182
  25.7 3.4 %collective-permute-start.5 = (bf16[1,384,768]{2,1,0:T(8,128)(2,1)S(1)}, bf16[1,384,768]{2,1,0:T(8,128)(2,1)S(1)}, u32[]{:S(2)}, u32[]{:S(2)}) collective-permute-start(bf16[1,384,768]{2,1,0:T(8,128)(2,1)S(1)} %shard_map.79.refs_4_.refs_3_), channel_id=1, source_target_pairs={{0,24},{1,25},{2,26},{3,27},{4,28},{5,29},{6,30},{7,31},{8,0},{9,1... | collective-permute-start | bytes 1769480 | tf_op jit(solution)/shard_map/ppermute | solution.py:384
  29.2 7.4 %collective-permute-done.5.refs_0_ = bf16[1,384,768]{2,1,0:T(8,128)(2,1)S(1)} collective-permute-done((bf16[1,384,768]{2,1,0:T(8,128)(2,1)S(1)}, bf16[1,384,768]{2,1,0:T(8,128)(2,1)S(1)}, u32[]{:S(2)}, u32[]{:S(2)}) %collective-permute-start.5) | collective-permute-done | bytes 589856 | tf_op jit(solution)/shard_map/ppermute | solution.py:384
  36.6 0.8 shard_map.80
  37.4 1.3 %collective-permute-start.8 = (bf16[384,768]{1,0:T(8,128)(2,1)S(1)}, bf16[384,768]{1,0:T(8,128)(2,1)S(1)}, u32[]{:S(2)}, u32[]{:S(2)}) collective-permute-start(bf16[384,768]{1,0:T(8,128)(2,1)S(1)} %get-tuple-element.24), channel_id=1, source_target_pairs={{8,1},{9,0},{10,3},{11,2},{12,5},{13,4},{14,7},{15,6},{16,17},{17,... | collective-permute-start | bytes 1769480 | tf_op jit(solution)/shard_map/ppermute | solution.py:384
  38.7 1.3 %collective-permute-start.9 = (bf16[384,768]{1,0:T(8,128)(2,1)S(1)}, bf16[384,768]{1,0:T(8,128)(2,1)S(1)}, u32[]{:S(2)}, u32[]{:S(2)}) collective-permute-start(bf16[384,768]{1,0:T(8,128)(2,1)S(1)} %get-tuple-element.25), channel_id=1, source_target_pairs={{8,0},{9,1},{10,2},{11,3},{12,4},{13,5},{14,6},{15,7}} | collective-permute-start | bytes 1769480 | tf_op jit(solution)/shard_map/ppermute | solution.py:384
  40.0 1.3 %collective-permute-start.6 = (bf16[192,768]{1,0:T(8,128)(2,1)S(1)}, bf16[192,768]{1,0:T(8,128)(2,1)S(1)}, u32[]{:S(2)}, u32[]{:S(2)}) collective-permute-start(bf16[192,768]{1,0:T(8,128)(2,1)S(1)} %get-tuple-element.22), channel_id=1, source_target_pairs={{8,7},{9,2},{10,1},{11,4},{12,3},{13,6},{14,5},{15,0},{24,25},{25,... | collective-permute-start | bytes 884744 | tf_op jit(solution)/shard_map/ppermute | solution.py:384
  41.3 1.3 %collective-permute-start.7 = (bf16[192,768]{1,0:T(8,128)(2,1)S(1)}, bf16[192,768]{1,0:T(8,128)(2,1)S(1)}, u32[]{:S(2)}, u32[]{:S(2)}) collective-permute-start(bf16[192,768]{1,0:T(8,128)(2,1)S(1)} %get-tuple-element.23), channel_id=1, source_target_pairs={{8,2},{9,7},{10,4},{11,1},{12,6},{13,3},{14,0},{15,5},{24,31},{25,... | collective-permute-start | bytes 884744 | tf_op jit(solution)/shard_map/ppermute | solution.py:384
  42.6 15.7 %collective-permute-done.6.edge_cross.refs_1_ = bf16[192,768]{1,0:T(8,128)(2,1)S(1)} collective-permute-done((bf16[192,768]{1,0:T(8,128)(2,1)S(1)}, bf16[192,768]{1,0:T(8,128)(2,1)S(1)}, u32[]{:S(2)}, u32[]{:S(2)}) %collective-permute-start.6) | collective-permute-done | bytes 294944 | tf_op jit(solution)/shard_map/ppermute | solution.py:384
  58.3 2.7 %collective-permute-done.7.edge_same.refs_2_ = bf16[192,768]{1,0:T(8,128)(2,1)S(1)} collective-permute-done((bf16[192,768]{1,0:T(8,128)(2,1)S(1)}, bf16[192,768]{1,0:T(8,128)(2,1)S(1)}, u32[]{:S(2)}, u32[]{:S(2)}) %collective-permute-start.7) | collective-permute-done | bytes 294944 | tf_op jit(solution)/shard_map/ppermute | solution.py:384
  60.9 0.8 %collective-permute-done.8.crossed.refs_0_.refs_4_ = bf16[384,768]{1,0:T(8,128)(2,1)S(1)} collective-permute-done((bf16[384,768]{1,0:T(8,128)(2,1)S(1)}, bf16[384,768]{1,0:T(8,128)(2,1)S(1)}, u32[]{:S(2)}, u32[]{:S(2)}) %collective-permute-start.8) | collective-permute-done | bytes 589856 | tf_op jit(solution)/shard_map/ppermute | solution.py:384
  61.8 0.0 collective-permute-done.9.direct.refs_3_
  61.8 0.7 shard_map.81
  62.5 0.1 collective-permute-start.10
  62.6 0.0 copy-start.1
  62.6 0.0 copy-start.2
  62.6 0.0 copy-start.3
  62.6 5.7 %shard_map.82.refs_6_ = bf16[2,192,768]{2,1,0:T(8,128)(2,1)S(1)} custom-call(s32[3]{0:T(128)S(1)} %pad_add_fusion.turn, f32[4,768]{1,0:T(4,128)S(1)} %copy-done.5, bf16[4,768,768]{2,1,0:T(8,128)(2,1)} %bitcast.16, bf16[384,768]{1,0:T(8,128)(2,1)S(1)} %collective-permute-done.8.crossed.refs_0_.refs_4_, ...), custom_call_target="tpu_custom_call" | custom-call | flops 2491416576 | bytes 4718592 | tf_op jit(solution)/shard_map/pallas_call | solution.py:182
  68.3 0.0 collective-permute-done.10.refs_5_
  68.3 1.4 %shard_map.83 = (bf16[2,192,768]{2,1,0:T(8,128)(2,1)S(1)}, f32[48,48]{1,0:T(8,128)S(1)}) custom-call(s32[3]{0:T(128)S(1)} %pad_add_fusion.turn, bf16[2,384,768]{2,1,0:T(8,128)(2,1)S(1)} %shard_map.77.share.refs_3_.refs_0_, bf16[192,768]{1,0:T(8,128)(2,1)S(1)} %collective-permute-done.6.edge_cross.refs_1_, ...), custom_call_target="tpu_custom_call" | custom-call | tf_op jit(solution)/shard_map/pallas_call | solution.py:545
  69.7 0.1 collective-permute-start.11
  69.8 3.8 %collective-permute-done.11 = f32[48,48]{1,0:T(8,128)S(1)} collective-permute-done((f32[48,48]{1,0:T(8,128)S(1)}, f32[48,48]{1,0:T(8,128)S(1)}, u32[]{:S(2)}, u32[]{:S(2)}) %collective-permute-start.11) | collective-permute-done | bytes 9248 | tf_op jit(solution)/shard_map/ppermute | solution.py:564
  73.6 0.0 collective-permute-start.12
  73.6 1.4 %collective-permute-start.14 = (f32[48,48]{1,0:T(8,128)S(1)}, f32[48,48]{1,0:T(8,128)S(1)}, u32[]{:S(2)}, u32[]{:S(2)}) collective-permute-start(f32[48,48]{1,0:T(8,128)S(1)} %add.18), channel_id=1, source_target_pairs={{0,6},{1,7},{2,4},{3,5},{4,2},{5,3},{6,0},{7,1},{8,14},{9,15},{10,... | collective-permute-start | bytes 27656 | tf_op jit(solution)/shard_map/ppermute | solution.py:564
  75.0 2.0 %collective-permute-start.13 = (f32[48,48]{1,0:T(8,128)S(1)}, f32[48,48]{1,0:T(8,128)S(1)}, u32[]{:S(2)}, u32[]{:S(2)}) collective-permute-start(f32[48,48]{1,0:T(8,128)S(1)} %add.18), channel_id=1, source_target_pairs={{0,4},{1,5},{2,6},{3,7},{4,0},{5,1},{6,2},{7,3},{8,12},{9,13},{10,... | collective-permute-start | bytes 27656 | tf_op jit(solution)/shard_map/ppermute | solution.py:564
  77.1 0.3 collective-permute-done.12
  77.4 1.9 %collective-permute-done.14 = f32[48,48]{1,0:T(8,128)S(1)} collective-permute-done((f32[48,48]{1,0:T(8,128)S(1)}, f32[48,48]{1,0:T(8,128)S(1)}, u32[]{:S(2)}, u32[]{:S(2)}) %collective-permute-start.14) | collective-permute-done | bytes 9248 | tf_op jit(solution)/shard_map/ppermute | solution.py:564
  79.3 0.5 collective-permute-done.13
  79.8 0.0 copy-done.1
  79.8 0.0 copy-done.2
  79.8 0.0 copy-done.3
  79.8 3.5 %shard_map.84 = (bf16[768,384]{1,0:T(8,128)(2,1)}, f32[48,48]{1,0:T(8,128)}) custom-call(f32[48,48]{1,0:T(8,128)S(1)} %add.19.first, f32[48,48]{1,0:T(8,128)S(1)} %add.20.second, bf16[384,768]{1,0:T(8,128)(2,1)S(1)} %bitcast.13, bf16[384,48]{1,0:T(8,128)(2,1)S(1)} %copy-done.2, bf16[48,384]{1,0:T(8,128)(2,1)S(1)} %copy-done.3, f32[384,384]{1,0:T(8,128)S(1)} %copy-done.1), custom_call_target="tpu_custom_call" | custom-call | tf_op jit(solution)/shard_map/pallas_call | solution.py:571
  (3 shorter events, 0.0 us)
Async XLA Ops:
  0.6 3.0 %collective-permute-start = (bf16[768,384]{1,0:T(8,128)(2,1)}, bf16[768,384]{1,0:T(8,128)(2,1)S(1)}, u32[]{:S(2)}, u32[]{:S(2)}) collective-permute-start(bf16[768,384]{1,0:T(8,128)(2,1)} %bitcast.10), channel_id=1, source_target_pairs={{0,8},{1,9},{2,10},{3,11},{4,12},{5,13},{6,14},{7,15},{16,24},{17,... | collective-permute-start | bytes 1769480 | tf_op jit(solution)/shard_map/ppermute | solution.py:384
  1.2 1.1 %copy-start = (bf16[1,768,384]{2,1,0:T(8,128)(2,1)S(1)}, bf16[1,768,384]{2,1,0:T(8,128)(2,1)}, u32[]{:S(2)}) copy-start(bf16[1,768,384]{2,1,0:T(8,128)(2,1)} %param.8) | copy-start | bytes 1769476
  2.3 0.7 copy-start.4
  5.7 18.7 %collective-permute-start.1 = (bf16[384,768]{1,0:T(8,128)(2,1)}, bf16[384,768]{1,0:T(8,128)(2,1)S(1)}, u32[]{:S(2)}, u32[]{:S(2)}) collective-permute-start(bf16[384,768]{1,0:T(8,128)(2,1)} %get-tuple-element.18), channel_id=1, source_target_pairs={{24,17},{25,16},{26,19},{27,18},{28,21},{29,20},{30,23},{31,22},{8... | collective-permute-start | bytes 1769480 | tf_op jit(solution)/shard_map/ppermute | solution.py:384
  6.4 18.0 %collective-permute-start.4 = (bf16[384,768]{1,0:T(8,128)(2,1)S(1)}, bf16[384,768]{1,0:T(8,128)(2,1)}, u32[]{:S(2)}, u32[]{:S(2)}) collective-permute-start(bf16[384,768]{1,0:T(8,128)(2,1)S(1)} %get-tuple-element.21), channel_id=1, source_target_pairs={{24,16},{25,17},{26,18},{27,19},{28,20},{29,21},{30,22},{31,23}} | collective-permute-start | bytes 1769480 | tf_op jit(solution)/shard_map/ppermute | solution.py:384
  7.9 16.1 %collective-permute-start.2 = (bf16[192,768]{1,0:T(8,128)(2,1)}, bf16[192,768]{1,0:T(8,128)(2,1)}, u32[]{:S(2)}, u32[]{:S(2)}) collective-permute-start(bf16[192,768]{1,0:T(8,128)(2,1)} %get-tuple-element.19), channel_id=1, source_target_pairs={{24,23},{25,18},{26,17},{27,20},{28,19},{29,22},{30,21},{31,16},{0... | collective-permute-start | bytes 884744 | tf_op jit(solution)/shard_map/ppermute | solution.py:384
  12.4 12.1 %collective-permute-start.3 = (bf16[192,768]{1,0:T(8,128)(2,1)}, bf16[192,768]{1,0:T(8,128)(2,1)}, u32[]{:S(2)}, u32[]{:S(2)}) collective-permute-start(bf16[192,768]{1,0:T(8,128)(2,1)} %get-tuple-element.20), channel_id=1, source_target_pairs={{24,22},{25,19},{26,16},{27,21},{28,18},{29,23},{30,20},{31,17},{0... | collective-permute-start | bytes 884744 | tf_op jit(solution)/shard_map/ppermute | solution.py:384
  17.3 7.1 %copy-start.5 = (f32[4,768]{1,0:T(4,128)S(1)}, f32[4,768]{1,0:T(4,128)}, u32[]{:S(2)}) copy-start(f32[4,768]{1,0:T(4,128)} %coupling.7) | copy-start | bytes 36868
  25.7 10.8 %collective-permute-start.5 = (bf16[1,384,768]{2,1,0:T(8,128)(2,1)S(1)}, bf16[1,384,768]{2,1,0:T(8,128)(2,1)S(1)}, u32[]{:S(2)}, u32[]{:S(2)}) collective-permute-start(bf16[1,384,768]{2,1,0:T(8,128)(2,1)S(1)} %shard_map.79.refs_4_.refs_3_), channel_id=1, source_target_pairs={{0,24},{1,25},{2,26},{3,27},{4,28},{5,29},{6,30},{7,31},{8,0},{9,1... | collective-permute-start | bytes 1769480 | tf_op jit(solution)/shard_map/ppermute | solution.py:384
  37.4 24.4 %collective-permute-start.8 = (bf16[384,768]{1,0:T(8,128)(2,1)S(1)}, bf16[384,768]{1,0:T(8,128)(2,1)S(1)}, u32[]{:S(2)}, u32[]{:S(2)}) collective-permute-start(bf16[384,768]{1,0:T(8,128)(2,1)S(1)} %get-tuple-element.24), channel_id=1, source_target_pairs={{8,1},{9,0},{10,3},{11,2},{12,5},{13,4},{14,7},{15,6},{16,17},{17,... | collective-permute-start | bytes 1769480 | tf_op jit(solution)/shard_map/ppermute | solution.py:384
  38.7 23.1 %collective-permute-start.9 = (bf16[384,768]{1,0:T(8,128)(2,1)S(1)}, bf16[384,768]{1,0:T(8,128)(2,1)S(1)}, u32[]{:S(2)}, u32[]{:S(2)}) collective-permute-start(bf16[384,768]{1,0:T(8,128)(2,1)S(1)} %get-tuple-element.25), channel_id=1, source_target_pairs={{8,0},{9,1},{10,2},{11,3},{12,4},{13,5},{14,6},{15,7}} | collective-permute-start | bytes 1769480 | tf_op jit(solution)/shard_map/ppermute | solution.py:384
  40.0 18.3 %collective-permute-start.6 = (bf16[192,768]{1,0:T(8,128)(2,1)S(1)}, bf16[192,768]{1,0:T(8,128)(2,1)S(1)}, u32[]{:S(2)}, u32[]{:S(2)}) collective-permute-start(bf16[192,768]{1,0:T(8,128)(2,1)S(1)} %get-tuple-element.22), channel_id=1, source_target_pairs={{8,7},{9,2},{10,1},{11,4},{12,3},{13,6},{14,5},{15,0},{24,25},{25,... | collective-permute-start | bytes 884744 | tf_op jit(solution)/shard_map/ppermute | solution.py:384
  41.3 19.6 %collective-permute-start.7 = (bf16[192,768]{1,0:T(8,128)(2,1)S(1)}, bf16[192,768]{1,0:T(8,128)(2,1)S(1)}, u32[]{:S(2)}, u32[]{:S(2)}) collective-permute-start(bf16[192,768]{1,0:T(8,128)(2,1)S(1)} %get-tuple-element.23), channel_id=1, source_target_pairs={{8,2},{9,7},{10,4},{11,1},{12,6},{13,3},{14,0},{15,5},{24,31},{25,... | collective-permute-start | bytes 884744 | tf_op jit(solution)/shard_map/ppermute | solution.py:384
  62.5 5.9 %collective-permute-start.10 = (bf16[2,192,768]{2,1,0:T(8,128)(2,1)S(1)}, bf16[2,192,768]{2,1,0:T(8,128)(2,1)S(1)}, u32[]{:S(2)}, u32[]{:S(2)}) collective-permute-start(bf16[2,192,768]{2,1,0:T(8,128)(2,1)S(1)} %shard_map.81), channel_id=1, source_target_pairs={{0,8},{1,9},{2,10},{3,11},{4,12},{5,13},{6,14},{7,15},{16,24},{17,... | collective-permute-start | bytes 1769480 | tf_op jit(solution)/shard_map/ppermute | solution.py:384
  62.6 17.2 %copy-start.1 = (f32[384,384]{1,0:T(8,128)S(1)}, f32[384,384]{1,0:T(8,128)}, u32[]{:S(2)}) copy-start(f32[384,384]{1,0:T(8,128)} %constant.40.clone.same_point) | copy-start | bytes 1769476
  62.6 17.2 %copy-start.2 = (bf16[384,48]{1,0:T(8,128)(2,1)S(1)}, bf16[384,48]{1,0:T(8,128)(2,1)}, u32[]{:S(2)}) copy-start(bf16[384,48]{1,0:T(8,128)(2,1)} %constant.38.clone.by_column) | copy-start | bytes 110596
  62.6 17.2 %copy-start.3 = (bf16[48,384]{1,0:T(8,128)(2,1)S(1)}, bf16[48,384]{1,0:T(8,128)(2,1)}, u32[]{:S(2)}) copy-start(bf16[48,384]{1,0:T(8,128)(2,1)} %constant.39.clone.by_place) | copy-start | bytes 110596
  69.7 3.9 %collective-permute-start.11 = (f32[48,48]{1,0:T(8,128)S(1)}, f32[48,48]{1,0:T(8,128)S(1)}, u32[]{:S(2)}, u32[]{:S(2)}) collective-permute-start(f32[48,48]{1,0:T(8,128)S(1)} %get-tuple-element.26), channel_id=1, source_target_pairs={{0,1},{1,0},{2,3},{3,2},{4,5},{5,4},{6,7},{7,6},{8,9},{9,8},{10,11... | collective-permute-start | bytes 27656 | tf_op jit(solution)/shard_map/ppermute | solution.py:564
  73.6 3.8 %collective-permute-start.12 = (f32[48,48]{1,0:T(8,128)S(1)}, f32[48,48]{1,0:T(8,128)S(1)}, u32[]{:S(2)}, u32[]{:S(2)}) collective-permute-start(f32[48,48]{1,0:T(8,128)S(1)} %add.18), channel_id=1, source_target_pairs={{0,2},{1,3},{2,0},{3,1},{4,6},{5,7},{6,4},{7,5},{8,10},{9,11},{10,... | collective-permute-start | bytes 27656 | tf_op jit(solution)/shard_map/ppermute | solution.py:564
  73.6 5.7 %collective-permute-start.14 = (f32[48,48]{1,0:T(8,128)S(1)}, f32[48,48]{1,0:T(8,128)S(1)}, u32[]{:S(2)}, u32[]{:S(2)}) collective-permute-start(f32[48,48]{1,0:T(8,128)S(1)} %add.18), channel_id=1, source_target_pairs={{0,6},{1,7},{2,4},{3,5},{4,2},{5,3},{6,0},{7,1},{8,14},{9,15},{10,... | collective-permute-start | bytes 27656 | tf_op jit(solution)/shard_map/ppermute | solution.py:564
  75.0 4.7 %collective-permute-start.13 = (f32[48,48]{1,0:T(8,128)S(1)}, f32[48,48]{1,0:T(8,128)S(1)}, u32[]{:S(2)}, u32[]{:S(2)}) collective-permute-start(f32[48,48]{1,0:T(8,128)S(1)} %add.18), channel_id=1, source_target_pairs={{0,4},{1,5},{2,6},{3,7},{4,0},{5,1},{6,2},{7,3},{8,12},{9,13},{10,... | collective-permute-start | bytes 27656 | tf_op jit(solution)/shard_map/ppermute | solution.py:564

commit v2 on v0

--- a/solution.py
+++ b/solution.py
@@ -292,25 +292,39 @@
         def _():
             fetch((back, rows))
 
+    def inner(state):
+        flat = state[...].reshape(2 * ONE, FN)
+        full = lax.dot_general(flat, flat, (((1,), (1,)), ((), ())), preferred_element_type=jnp.float32)
+        lines = []
+        for first in range(2):
+            line = []
+            for second in range(2):
+                block = None
+                for point in range(POINTS):
+                    down, along = first * ONE + point * HALF, second * ONE + point * HALF
+                    term = full[down : down + HALF, along : along + HALF]
+                    block = term if block is None else block + term
+                line.append(block)
+            lines.append(jnp.concatenate(line, 1))
+        gram[...] = jnp.concatenate(lines, 0)
+
+    @pl.when(turn[2] < 3)
+    def _():
+        inner(rows)
+
+    for at, number in enumerate(numbers):
+        last = inputs[7 * at + 6]
+
         @pl.when(turn[0] == number - 3)
         def _():
-            fetch((last, rows))
-
-    flat = rows[...].reshape(2 * ONE, FN)
-    full = lax.dot_general(flat, flat, (((1,), (1,)), ((), ())), preferred_element_type=jnp.float32)
-    lines = []
-    for first in range(2):
-        line = []
-        for second in range(2):
-            block = None
-            for point in range(POINTS):
-                down, along = first * ONE + point * HALF, second * ONE + point * HALF
-                term = full[down : down + HALF, along : along + HALF]
-                block = term if block is None else block + term
-            line.append(block)
-        lines.append(jnp.concatenate(line, 1))
-    total = jnp.concatenate(lines, 0)
-    gram[...] = total
+            copy = pltpu.make_async_copy(last, rows, sems.at[0])
+            copy.start()
+            inner(last)
+            copy.wait()
+
+
+def turn_kernel(rows, turned):
+    turned[...] = rows[...].reshape(2 * ONE, FN).T
 
 
 def factor_kernel(scale, first, second, rows, by_column, by_place, same_point, basis, upper):
@@ -358,7 +372,7 @@
         )
         terms.append((spread * same_point[...]).astype(jnp.bfloat16))
     both = lax.dot_general(
-        rows[...], jnp.concatenate(terms, 1), (((0,), (0,)), ((), ())), preferred_element_type=jnp.float32
+        rows[...], jnp.concatenate(terms, 1), (((1,), (0,)), ((), ())), preferred_element_type=jnp.float32
     )
     total = both[:, : POINTS * K] + both[:, POINTS * K :]
     basis[...] = total.astype(jnp.bfloat16)
@@ -543,11 +557,18 @@
             jax.ShapeDtypeStruct((2, ONE, FN), jnp.bfloat16),
             jax.ShapeDtypeStruct((K, K), jnp.float32),
         ),
-        in_specs=[smem] + [away] * len(candidates),
+        in_specs=[smem] + ([away] * 6 + [vmem]) * (len(candidates) // 7),
         out_specs=(vmem, vmem),
         scratch_shapes=[pltpu.VMEM((2, ONE, FN), jnp.bfloat16), pltpu.SemaphoreType.DMA((6,))],
         compiler_params=pltpu.CompilerParams(vmem_limit_bytes=SMALL),
     )(turn, *candidates)
+    turned_rows = pl.pallas_call(
+        turn_kernel,
+        out_shape=jax.ShapeDtypeStruct((FN, POINTS * K), jnp.bfloat16),
+        in_specs=[vmem],
+        out_specs=vmem,
+        compiler_params=pltpu.CompilerParams(vmem_limit_bytes=SMALL),
+    )(rows)
     stride = 1
     terms = [gram]
     while stride < spans:
@@ -572,7 +593,7 @@
         in_specs=[vmem] * 6,
         out_specs=(vmem, vmem),
         compiler_params=pltpu.CompilerParams(vmem_limit_bytes=SMALL),
-    )(*terms, rows.reshape(POINTS * K, FN), by_column, by_place, same_point)
+    )(*terms, turned_rows, by_column, by_place, same_point)
     return (basis[None], upper[None])
 
 

time: 81.5 us -> 81.6 us (level)
  no operation moved by 1% of the time
where the time goes in v2:
time: 81.6 us; the launch traced here: 81.2 us
  waiting for transfers between devices  43.1 us (53%)
  starting transfers between devices  21.1 us (26%)
  Pallas kernels  14.2 us (17%)
  local copies, waits for them, and re-layouts  1.79 us (2%)
  between operations  0.84 us (1%)
    ppermute x11, waiting for transfers between devices, send(): return lax.ppermute(value, AXES, routes)  36.9 us
    ppermute x11, starting transfers between devices, send(): return lax.ppermute(value, AXES, routes)  17.6 us
    pallas_call x4, Pallas kernels, march(): pl.pallas_call(functools.partial(march_kernel, number, [piece[1:] for pie...  7.33 us
    ppermute x4, waiting for transfers between devices, local(): lax.ppermute(total, 'span', [(s, s ^ digit * stride) for s in range(spans)])  6.26 us
    ppermute x4, starting transfers between devices, local(): lax.ppermute(total, 'span', [(s, s ^ digit * stride) for s in range(spans)])  3.56 us
    pallas_call x1, Pallas kernels, local(): pl.pallas_call(functools.partial(factor_kernel, 1.0 / float(FN * POINTS *...  3.52 us
    unnamed x10, local copies, waits for them, and re-layouts  1.79 us
  transfers between devices with their start and end apart: 15, of which 9 were waited for; matrix products, arithmetic and copies ran while one was open for 0% of the time, Pallas kernels for 8%

profile of v2, /device:TPU:0, one launch (start us, length us, event | category | flops | bytes accessed | tf_op | source)
XLA Modules:
  0.0 81.2 jit_solution(5958508727147274243)
XLA Ops:
  0.6 0.5 collective-permute-start
  1.1 0.1 pad_add_fusion.turn
  1.2 0.0 copy-start
  1.2 1.1 %copy-done = bf16[1,768,384]{2,1,0:T(8,128)(2,1)S(1)} copy-done((bf16[1,768,384]{2,1,0:T(8,128)(2,1)S(1)}, bf16[1,768,384]{2,1,0:T(8,128)(2,1)}, u32[]{:S(2)}) %copy-start) | copy-done | bytes 589848
  2.3 0.0 copy-start.4
  2.3 0.7 copy-done.4
  3.0 0.6 shard_map.77.share.refs_3_.refs_0_
  3.6 0.0 collective-permute-done.below
  3.6 1.1 %shard_map.78 = (bf16[384,768]{1,0:T(8,128)(2,1)S(1)}, bf16[192,768]{1,0:T(8,128)(2,1)S(1)}, bf16[192,768]{1,0:T(8,128)(2,1)S(1)}, bf16[384,768]{1,0:T(8,128)(2,1)S(1)}, bf16[2,384,768]{2,1,0:T(8,128)(2,1)S(1)}) custom-call(s32[3]{0:T(128)S(1)} %pad_add_fusion.turn, bf16[2,384,768]{2,1,0:T(8,128)(2,1)S(1)} %shard_map.77.share.refs_3_.refs_0_, ...), custom_call_target="tpu_custom_call" | custom-call | tf_op jit(solution)/shard_map/pallas_call | solution.py:443
  4.7 0.7 collective-permute-start.1
  5.4 0.7 collective-permute-start.4
  6.1 4.5 %collective-permute-start.2 = (bf16[192,768]{1,0:T(8,128)(2,1)S(1)}, bf16[192,768]{1,0:T(8,128)(2,1)S(1)}, u32[]{:S(2)}, u32[]{:S(2)}) collective-permute-start(bf16[192,768]{1,0:T(8,128)(2,1)S(1)} %get-tuple-element.16), channel_id=1, source_target_pairs={{24,23},{25,18},{26,17},{27,20},{28,19},{29,22},{30,21},{31,16},{0... | collective-permute-start | bytes 884744 | tf_op jit(solution)/shard_map/ppermute | solution.py:395
  10.6 5.0 %collective-permute-start.3 = (bf16[192,768]{1,0:T(8,128)(2,1)S(1)}, bf16[192,768]{1,0:T(8,128)(2,1)S(1)}, u32[]{:S(2)}, u32[]{:S(2)}) collective-permute-start(bf16[192,768]{1,0:T(8,128)(2,1)S(1)} %get-tuple-element.17), channel_id=1, source_target_pairs={{24,22},{25,19},{26,16},{27,21},{28,18},{29,23},{30,20},{31,17},{0... | collective-permute-start | bytes 884744 | tf_op jit(solution)/shard_map/ppermute | solution.py:395
  15.5 5.6 %collective-permute-done.2.refs_1_ = bf16[192,768]{1,0:T(8,128)(2,1)S(1)} collective-permute-done((bf16[192,768]{1,0:T(8,128)(2,1)S(1)}, bf16[192,768]{1,0:T(8,128)(2,1)S(1)}, u32[]{:S(2)}, u32[]{:S(2)}) %collective-permute-start.2) | collective-permute-done | bytes 294944 | tf_op jit(solution)/shard_map/ppermute | solution.py:395
  21.2 1.9 %collective-permute-done.3.refs_2_ = bf16[192,768]{1,0:T(8,128)(2,1)S(1)} collective-permute-done((bf16[192,768]{1,0:T(8,128)(2,1)S(1)}, bf16[192,768]{1,0:T(8,128)(2,1)S(1)}, u32[]{:S(2)}, u32[]{:S(2)}) %collective-permute-start.3) | collective-permute-done | bytes 294944 | tf_op jit(solution)/shard_map/ppermute | solution.py:395
  23.1 0.0 collective-permute-done.1.refs_0_.refs_2_
  23.1 0.0 collective-permute-done.4.refs_3_
  23.1 0.6 shard_map.79.refs_4_.refs_3_
  23.7 0.8 %collective-permute-start.5 = (bf16[1,384,768]{2,1,0:T(8,128)(2,1)S(1)}, bf16[1,384,768]{2,1,0:T(8,128)(2,1)S(1)}, u32[]{:S(2)}, u32[]{:S(2)}) collective-permute-start(bf16[1,384,768]{2,1,0:T(8,128)(2,1)S(1)} %shard_map.79.refs_4_.refs_3_), channel_id=1, source_target_pairs={{0,24},{1,25},{2,26},{3,27},{4,28},{5,29},{6,30},{7,31},{8,0},{9,1... | collective-permute-start | bytes 1769480 | tf_op jit(solution)/shard_map/ppermute | solution.py:395
  24.5 7.4 %collective-permute-done.5.refs_0_ = bf16[1,384,768]{2,1,0:T(8,128)(2,1)S(1)} collective-permute-done((bf16[1,384,768]{2,1,0:T(8,128)(2,1)S(1)}, bf16[1,384,768]{2,1,0:T(8,128)(2,1)S(1)}, u32[]{:S(2)}, u32[]{:S(2)}) %collective-permute-start.5) | collective-permute-done | bytes 589856 | tf_op jit(solution)/shard_map/ppermute | solution.py:395
  31.9 0.6 shard_map.80
  32.5 1.3 %collective-permute-start.8 = (bf16[384,768]{1,0:T(8,128)(2,1)S(1)}, bf16[384,768]{1,0:T(8,128)(2,1)S(1)}, u32[]{:S(2)}, u32[]{:S(2)}) collective-permute-start(bf16[384,768]{1,0:T(8,128)(2,1)S(1)} %get-tuple-element.22), channel_id=1, source_target_pairs={{8,1},{9,0},{10,3},{11,2},{12,5},{13,4},{14,7},{15,6},{16,17},{17,... | collective-permute-start | bytes 1769480 | tf_op jit(solution)/shard_map/ppermute | solution.py:395
  33.8 1.5 %collective-permute-start.9 = (bf16[384,768]{1,0:T(8,128)(2,1)S(1)}, bf16[384,768]{1,0:T(8,128)(2,1)S(1)}, u32[]{:S(2)}, u32[]{:S(2)}) collective-permute-start(bf16[384,768]{1,0:T(8,128)(2,1)S(1)} %get-tuple-element.23), channel_id=1, source_target_pairs={{8,0},{9,1},{10,2},{11,3},{12,4},{13,5},{14,6},{15,7}} | collective-permute-start | bytes 1769480 | tf_op jit(solution)/shard_map/ppermute | solution.py:395
  35.3 1.3 %collective-permute-start.6 = (bf16[192,768]{1,0:T(8,128)(2,1)S(1)}, bf16[192,768]{1,0:T(8,128)(2,1)S(1)}, u32[]{:S(2)}, u32[]{:S(2)}) collective-permute-start(bf16[192,768]{1,0:T(8,128)(2,1)S(1)} %get-tuple-element.20), channel_id=1, source_target_pairs={{8,7},{9,2},{10,1},{11,4},{12,3},{13,6},{14,5},{15,0},{24,25},{25,... | collective-permute-start | bytes 884744 | tf_op jit(solution)/shard_map/ppermute | solution.py:395
  36.6 1.3 %collective-permute-start.7 = (bf16[192,768]{1,0:T(8,128)(2,1)S(1)}, bf16[192,768]{1,0:T(8,128)(2,1)S(1)}, u32[]{:S(2)}, u32[]{:S(2)}) collective-permute-start(bf16[192,768]{1,0:T(8,128)(2,1)S(1)} %get-tuple-element.21), channel_id=1, source_target_pairs={{8,2},{9,7},{10,4},{11,1},{12,6},{13,3},{14,0},{15,5},{24,31},{25,... | collective-permute-start | bytes 884744 | tf_op jit(solution)/shard_map/ppermute | solution.py:395
  37.9 18.8 %collective-permute-done.6.edge_cross.refs_1_ = bf16[192,768]{1,0:T(8,128)(2,1)S(1)} collective-permute-done((bf16[192,768]{1,0:T(8,128)(2,1)S(1)}, bf16[192,768]{1,0:T(8,128)(2,1)S(1)}, u32[]{:S(2)}, u32[]{:S(2)}) %collective-permute-start.6) | collective-permute-done | bytes 294944 | tf_op jit(solution)/shard_map/ppermute | solution.py:395
  56.8 3.1 %collective-permute-done.7.edge_same.refs_2_ = bf16[192,768]{1,0:T(8,128)(2,1)S(1)} collective-permute-done((bf16[192,768]{1,0:T(8,128)(2,1)S(1)}, bf16[192,768]{1,0:T(8,128)(2,1)S(1)}, u32[]{:S(2)}, u32[]{:S(2)}) %collective-permute-start.7) | collective-permute-done | bytes 294944 | tf_op jit(solution)/shard_map/ppermute | solution.py:395
  59.8 0.0 collective-permute-done.8.crossed.refs_0_.refs_4_
  59.8 0.0 collective-permute-done.9.direct.refs_3_
  59.8 0.7 shard_map.81
  60.5 0.1 collective-permute-start.10
  60.6 5.6 %shard_map.82.refs_6_ = bf16[2,192,768]{2,1,0:T(8,128)(2,1)S(1)} custom-call(s32[3]{0:T(128)S(1)} %pad_add_fusion.turn, f32[4,768]{1,0:T(4,128)S(1)} %copy-done.4, bf16[4,768,768]{2,1,0:T(8,128)(2,1)} %weights.7, bf16[384,768]{1,0:T(8,128)(2,1)S(1)} %collective-permute-done.8.crossed.refs_0_.refs_4_, ...), custom_call_target="tpu_custom_call" | custom-call | flops 2491416576 | bytes 4718592 | tf_op jit(solution)/shard_map/pallas_call | solution.py:179
  66.2 0.0 collective-permute-done.10.refs_5_
  66.2 1.4 %shard_map.83 = (bf16[2,192,768]{2,1,0:T(8,128)(2,1)S(1)}, f32[48,48]{1,0:T(8,128)S(1)}) custom-call(s32[3]{0:T(128)S(1)} %pad_add_fusion.turn, bf16[2,384,768]{2,1,0:T(8,128)(2,1)S(1)} %shard_map.77.share.refs_3_.refs_0_, bf16[192,768]{1,0:T(8,128)(2,1)S(1)} %collective-permute-done.6.edge_cross.refs_1_, ...), custom_call_target="tpu_custom_call" | custom-call | tf_op jit(solution)/shard_map/pallas_call | solution.py:554
  67.6 0.0 copy-start.1
  67.6 0.0 copy-start.2
  67.6 0.0 copy-start.3
  67.6 0.1 collective-permute-start.11
  67.7 3.8 %collective-permute-done.11 = f32[48,48]{1,0:T(8,128)S(1)} collective-permute-done((f32[48,48]{1,0:T(8,128)S(1)}, f32[48,48]{1,0:T(8,128)S(1)}, u32[]{:S(2)}, u32[]{:S(2)}) %collective-permute-start.11) | collective-permute-done | bytes 9248 | tf_op jit(solution)/shard_map/ppermute | solution.py:580
  71.5 0.0 collective-permute-start.12
  71.5 1.4 %collective-permute-start.14 = (f32[48,48]{1,0:T(8,128)S(1)}, f32[48,48]{1,0:T(8,128)S(1)}, u32[]{:S(2)}, u32[]{:S(2)}) collective-permute-start(f32[48,48]{1,0:T(8,128)S(1)} %add.18), channel_id=1, source_target_pairs={{0,6},{1,7},{2,4},{3,5},{4,2},{5,3},{6,0},{7,1},{8,14},{9,15},{10,... | collective-permute-start | bytes 27656 | tf_op jit(solution)/shard_map/ppermute | solution.py:580
  72.9 2.1 %collective-permute-start.13 = (f32[48,48]{1,0:T(8,128)S(1)}, f32[48,48]{1,0:T(8,128)S(1)}, u32[]{:S(2)}, u32[]{:S(2)}) collective-permute-start(f32[48,48]{1,0:T(8,128)S(1)} %add.18), channel_id=1, source_target_pairs={{0,4},{1,5},{2,6},{3,7},{4,0},{5,1},{6,2},{7,3},{8,12},{9,13},{10,... | collective-permute-start | bytes 27656 | tf_op jit(solution)/shard_map/ppermute | solution.py:580
  75.0 0.2 shard_map.84.rows
  75.2 0.1 collective-permute-done.12
  75.3 1.9 %collective-permute-done.14 = f32[48,48]{1,0:T(8,128)S(1)} collective-permute-done((f32[48,48]{1,0:T(8,128)S(1)}, f32[48,48]{1,0:T(8,128)S(1)}, u32[]{:S(2)}, u32[]{:S(2)}) %collective-permute-start.14) | collective-permute-done | bytes 9248 | tf_op jit(solution)/shard_map/ppermute | solution.py:580
  77.2 0.5 collective-permute-done.13
  77.7 0.0 copy-done.1
  77.7 0.0 copy-done.2
  77.7 0.0 copy-done.3
  77.7 3.5 %shard_map.85 = (bf16[768,384]{1,0:T(8,128)(2,1)}, f32[48,48]{1,0:T(8,128)}) custom-call(f32[48,48]{1,0:T(8,128)S(1)} %add.19.first, f32[48,48]{1,0:T(8,128)S(1)} %add.20.second, bf16[768,384]{1,0:T(8,128)(2,1)S(1)} %shard_map.84.rows, bf16[384,48]{1,0:T(8,128)(2,1)S(1)} %copy-done.2, bf16[48,384]{1,0:T(8,128)(2,1)S(1)} %copy-done.3, f32[384,384]{1,0:T(8,128)S(1)} %copy-done.1), custom_call_target="tpu_custom_call" | custom-call | tf_op jit(solution)/shard_map/pallas_call | solution.py:587
  (3 shorter events, 0.0 us)
Async XLA Ops:
  0.6 3.0 %collective-permute-start = (bf16[768,384]{1,0:T(8,128)(2,1)}, bf16[768,384]{1,0:T(8,128)(2,1)S(1)}, u32[]{:S(2)}, u32[]{:S(2)}) collective-permute-start(bf16[768,384]{1,0:T(8,128)(2,1)} %bitcast.8), channel_id=1, source_target_pairs={{0,8},{1,9},{2,10},{3,11},{4,12},{5,13},{6,14},{7,15},{16,24},{17,... | collective-permute-start | bytes 1769480 | tf_op jit(solution)/shard_map/ppermute | solution.py:395
  1.2 1.1 %copy-start = (bf16[1,768,384]{2,1,0:T(8,128)(2,1)S(1)}, bf16[1,768,384]{2,1,0:T(8,128)(2,1)}, u32[]{:S(2)}) copy-start(bf16[1,768,384]{2,1,0:T(8,128)(2,1)} %param.8) | copy-start | bytes 1769476
  2.3 0.7 copy-start.4
  4.7 18.4 %collective-permute-start.1 = (bf16[384,768]{1,0:T(8,128)(2,1)S(1)}, bf16[384,768]{1,0:T(8,128)(2,1)S(1)}, u32[]{:S(2)}, u32[]{:S(2)}) collective-permute-start(bf16[384,768]{1,0:T(8,128)(2,1)S(1)} %get-tuple-element.15), channel_id=1, source_target_pairs={{24,17},{25,16},{26,19},{27,18},{28,21},{29,20},{30,23},{31,22},{8... | collective-permute-start | bytes 1769480 | tf_op jit(solution)/shard_map/ppermute | solution.py:395
  5.4 17.7 %collective-permute-start.4 = (bf16[384,768]{1,0:T(8,128)(2,1)S(1)}, bf16[384,768]{1,0:T(8,128)(2,1)S(1)}, u32[]{:S(2)}, u32[]{:S(2)}) collective-permute-start(bf16[384,768]{1,0:T(8,128)(2,1)S(1)} %get-tuple-element.18), channel_id=1, source_target_pairs={{24,16},{25,17},{26,18},{27,19},{28,20},{29,21},{30,22},{31,23}} | collective-permute-start | bytes 1769480 | tf_op jit(solution)/shard_map/ppermute | solution.py:395
  6.1 15.1 %collective-permute-start.2 = (bf16[192,768]{1,0:T(8,128)(2,1)S(1)}, bf16[192,768]{1,0:T(8,128)(2,1)S(1)}, u32[]{:S(2)}, u32[]{:S(2)}) collective-permute-start(bf16[192,768]{1,0:T(8,128)(2,1)S(1)} %get-tuple-element.16), channel_id=1, source_target_pairs={{24,23},{25,18},{26,17},{27,20},{28,19},{29,22},{30,21},{31,16},{0... | collective-permute-start | bytes 884744 | tf_op jit(solution)/shard_map/ppermute | solution.py:395
  10.6 12.5 %collective-permute-start.3 = (bf16[192,768]{1,0:T(8,128)(2,1)S(1)}, bf16[192,768]{1,0:T(8,128)(2,1)S(1)}, u32[]{:S(2)}, u32[]{:S(2)}) collective-permute-start(bf16[192,768]{1,0:T(8,128)(2,1)S(1)} %get-tuple-element.17), channel_id=1, source_target_pairs={{24,22},{25,19},{26,16},{27,21},{28,18},{29,23},{30,20},{31,17},{0... | collective-permute-start | bytes 884744 | tf_op jit(solution)/shard_map/ppermute | solution.py:395
  23.7 8.2 %collective-permute-start.5 = (bf16[1,384,768]{2,1,0:T(8,128)(2,1)S(1)}, bf16[1,384,768]{2,1,0:T(8,128)(2,1)S(1)}, u32[]{:S(2)}, u32[]{:S(2)}) collective-permute-start(bf16[1,384,768]{2,1,0:T(8,128)(2,1)S(1)} %shard_map.79.refs_4_.refs_3_), channel_id=1, source_target_pairs={{0,24},{1,25},{2,26},{3,27},{4,28},{5,29},{6,30},{7,31},{8,0},{9,1... | collective-permute-start | bytes 1769480 | tf_op jit(solution)/shard_map/ppermute | solution.py:395
  32.5 27.3 %collective-permute-start.8 = (bf16[384,768]{1,0:T(8,128)(2,1)S(1)}, bf16[384,768]{1,0:T(8,128)(2,1)S(1)}, u32[]{:S(2)}, u32[]{:S(2)}) collective-permute-start(bf16[384,768]{1,0:T(8,128)(2,1)S(1)} %get-tuple-element.22), channel_id=1, source_target_pairs={{8,1},{9,0},{10,3},{11,2},{12,5},{13,4},{14,7},{15,6},{16,17},{17,... | collective-permute-start | bytes 1769480 | tf_op jit(solution)/shard_map/ppermute | solution.py:395
  33.8 26.0 %collective-permute-start.9 = (bf16[384,768]{1,0:T(8,128)(2,1)S(1)}, bf16[384,768]{1,0:T(8,128)(2,1)S(1)}, u32[]{:S(2)}, u32[]{:S(2)}) collective-permute-start(bf16[384,768]{1,0:T(8,128)(2,1)S(1)} %get-tuple-element.23), channel_id=1, source_target_pairs={{8,0},{9,1},{10,2},{11,3},{12,4},{13,5},{14,6},{15,7}} | collective-permute-start | bytes 1769480 | tf_op jit(solution)/shard_map/ppermute | solution.py:395
  35.3 21.4 %collective-permute-start.6 = (bf16[192,768]{1,0:T(8,128)(2,1)S(1)}, bf16[192,768]{1,0:T(8,128)(2,1)S(1)}, u32[]{:S(2)}, u32[]{:S(2)}) collective-permute-start(bf16[192,768]{1,0:T(8,128)(2,1)S(1)} %get-tuple-element.20), channel_id=1, source_target_pairs={{8,7},{9,2},{10,1},{11,4},{12,3},{13,6},{14,5},{15,0},{24,25},{25,... | collective-permute-start | bytes 884744 | tf_op jit(solution)/shard_map/ppermute | solution.py:395
  36.6 23.2 %collective-permute-start.7 = (bf16[192,768]{1,0:T(8,128)(2,1)S(1)}, bf16[192,768]{1,0:T(8,128)(2,1)S(1)}, u32[]{:S(2)}, u32[]{:S(2)}) collective-permute-start(bf16[192,768]{1,0:T(8,128)(2,1)S(1)} %get-tuple-element.21), channel_id=1, source_target_pairs={{8,2},{9,7},{10,4},{11,1},{12,6},{13,3},{14,0},{15,5},{24,31},{25,... | collective-permute-start | bytes 884744 | tf_op jit(solution)/shard_map/ppermute | solution.py:395
  60.5 5.7 %collective-permute-start.10 = (bf16[2,192,768]{2,1,0:T(8,128)(2,1)S(1)}, bf16[2,192,768]{2,1,0:T(8,128)(2,1)S(1)}, u32[]{:S(2)}, u32[]{:S(2)}) collective-permute-start(bf16[2,192,768]{2,1,0:T(8,128)(2,1)S(1)} %shard_map.81), channel_id=1, source_target_pairs={{0,8},{1,9},{2,10},{3,11},{4,12},{5,13},{6,14},{7,15},{16,24},{17,... | collective-permute-start | bytes 1769480 | tf_op jit(solution)/shard_map/ppermute | solution.py:395
  67.6 10.1 %copy-start.1 = (f32[384,384]{1,0:T(8,128)S(1)}, f32[384,384]{1,0:T(8,128)}, u32[]{:S(2)}) copy-start(f32[384,384]{1,0:T(8,128)} %constant.40.clone.same_point) | copy-start | bytes 1769476
  67.6 10.1 %copy-start.2 = (bf16[384,48]{1,0:T(8,128)(2,1)S(1)}, bf16[384,48]{1,0:T(8,128)(2,1)}, u32[]{:S(2)}) copy-start(bf16[384,48]{1,0:T(8,128)(2,1)} %constant.38.clone.by_column) | copy-start | bytes 110596
  67.6 10.1 %copy-start.3 = (bf16[48,384]{1,0:T(8,128)(2,1)S(1)}, bf16[48,384]{1,0:T(8,128)(2,1)}, u32[]{:S(2)}) copy-start(bf16[48,384]{1,0:T(8,128)(2,1)} %constant.39.clone.by_place) | copy-start | bytes 110596
  67.6 3.9 %collective-permute-start.11 = (f32[48,48]{1,0:T(8,128)S(1)}, f32[48,48]{1,0:T(8,128)S(1)}, u32[]{:S(2)}, u32[]{:S(2)}) collective-permute-start(f32[48,48]{1,0:T(8,128)S(1)} %get-tuple-element.24), channel_id=1, source_target_pairs={{0,1},{1,0},{2,3},{3,2},{4,5},{5,4},{6,7},{7,6},{8,9},{9,8},{10,11... | collective-permute-start | bytes 27656 | tf_op jit(solution)/shard_map/ppermute | solution.py:580
  71.5 3.8 %collective-permute-start.12 = (f32[48,48]{1,0:T(8,128)S(1)}, f32[48,48]{1,0:T(8,128)S(1)}, u32[]{:S(2)}, u32[]{:S(2)}) collective-permute-start(f32[48,48]{1,0:T(8,128)S(1)} %add.18), channel_id=1, source_target_pairs={{0,2},{1,3},{2,0},{3,1},{4,6},{5,7},{6,4},{7,5},{8,10},{9,11},{10,... | collective-permute-start | bytes 27656 | tf_op jit(solution)/shard_map/ppermute | solution.py:580
  71.5 5.7 %collective-permute-start.14 = (f32[48,48]{1,0:T(8,128)S(1)}, f32[48,48]{1,0:T(8,128)S(1)}, u32[]{:S(2)}, u32[]{:S(2)}) collective-permute-start(f32[48,48]{1,0:T(8,128)S(1)} %add.18), channel_id=1, source_target_pairs={{0,6},{1,7},{2,4},{3,5},{4,2},{5,3},{6,0},{7,1},{8,14},{9,15},{10,... | collective-permute-start | bytes 27656 | tf_op jit(solution)/shard_map/ppermute | solution.py:580
  72.9 4.7 %collective-permute-start.13 = (f32[48,48]{1,0:T(8,128)S(1)}, f32[48,48]{1,0:T(8,128)S(1)}, u32[]{:S(2)}, u32[]{:S(2)}) collective-permute-start(f32[48,48]{1,0:T(8,128)S(1)} %add.18), channel_id=1, source_target_pairs={{0,4},{1,5},{2,6},{3,7},{4,0},{5,1},{6,2},{7,3},{8,12},{9,13},{10,... | collective-permute-start | bytes 27656 | tf_op jit(solution)/shard_map/ppermute | solution.py:580

commit v3 on v0

--- a/solution.py
+++ b/solution.py
@@ -40,6 +40,7 @@
     refs = list(refs)
     pieces = [refs.pop(0) for _ in places]
     raws = [refs.pop(0) for _ in range(raw)]
+    ahead = [] if raw else [refs.pop(0)]
     givers = [refs.pop(0) for _ in others[0]]
     outs, (first, second, held, result, sems) = refs[:-5], refs[-5:]
     if not others[2]:
@@ -56,7 +57,7 @@
             pltpu.make_async_copy(weights.at[station], held.at[step], sems.at[step])
             for step, station in enumerate(order)
         ]
-        copies[0].start()
+        copies[1 if ahead else 0].start()
         margin = 2 * HALF if grow else 0
         if margin:
             empty = jnp.zeros((blocks, margin, FN), jnp.float32)
@@ -106,7 +107,7 @@
             update = (1.0 - 2.0 * rates) * source[block, at + HALF : at + HALF + rows, :] + rates * both
             return update.astype(jnp.bfloat16)
 
-        copies[1].start()
+        copies[2 if ahead else 1].start()
         jobs = [(step, chunk) for step in range(STATIONS) for chunk in plan[step]]
         update = stencil(*jobs[0])
         for at_job, (step, chunk) in enumerate(jobs):
@@ -116,11 +117,16 @@
             if at_job + 1 < len(jobs):
                 update = stencil(*jobs[at_job + 1])
             if chunk is plan[step][0]:
-                copies[step].wait()
-                if step + 2 < STATIONS:
-                    copies[step + 2].start()
+                if step or not ahead:
+                    copies[step].wait()
+                later = step + (3 if ahead else 2)
+                if later < STATIONS:
+                    copies[later].start()
             moved = lax.dot_general(
-                current, held[step], (((1,), (1,)), ((), ())), preferred_element_type=jnp.float32
+                current,
+                ahead[0][...] if ahead and not step else held[step],
+                (((1,), (1,)), ((), ())),
+                preferred_element_type=jnp.float32,
             )
             if step == STATIONS - 1:
                 result[block, at : at + rows, :] = moved.astype(jnp.bfloat16)
@@ -160,7 +166,7 @@
                 copy.wait()
 
 
-def march(turn, number, inverse_blocks, coupling, pieces, cut, blocks, positions, grow, raw=(), others=((), (), ())):
+def march(turn, number, inverse_blocks, coupling, pieces, cut, blocks, positions, grow, raw=(), ahead=(), others=((), (), ())):
     last = positions + (2 * STATIONS if grow else -2 * STATIONS)
     most = last + 2 if grow else positions
     counts = [positions + (2 if grow else -2) * (step + 1) for step in range(STATIONS)]
@@ -190,7 +196,7 @@
         ),
         out_shape=shapes,
         in_specs=[pl.BlockSpec(memory_space=pltpu.SMEM), vmem, away]
-        + [vmem] * (len(values) + len(raw))
+        + [vmem] * (len(values) + len(raw) + len(ahead))
         + [away] * len(others[0]),
         out_specs=[vmem] * len(shapes),
         scratch_shapes=[pltpu.VMEM((blocks, most * HALF, FN), jnp.float32)] * 2
@@ -205,11 +211,11 @@
             bytes_accessed=2 * STATIONS * FN * FN,
             transcendentals=0,
         ),
-    )(turn, coupling, inverse_blocks, *values, *raw, *others[0])
+    )(turn, coupling, inverse_blocks, *values, *raw, *ahead, *others[0])
 
 
 def ship_kernel(
-    number, turn, share, below, raw, crossed, edge_cross, edge_same, direct, whole, turned
+    number, turn, share, below, raw, crossed, edge_cross, edge_same, direct, kept, turned, whole
 ):
     side, kind = turn[1], turn[2]
 
@@ -222,6 +228,7 @@
     def _():
         turn_over(below)
         whole[...] = share[...]
+        kept[...] = share[...]
         middle = share[:, EDGE : EDGE + ONE, :].astype(jnp.float32) + turned[...]
         whole[:, EDGE : EDGE + ONE, :] = middle.astype(jnp.bfloat16)
         start = pl.multiple_of(side * ONE, ONE)
@@ -233,17 +240,25 @@
     @pl.when(kind >= 2)
     def _():
         turn_over(raw)
-        whole[:, :ONE, :] = turned[...].astype(jnp.bfloat16)
+        kept[:, :ONE, :] = turned[...].astype(jnp.bfloat16)
 
     @pl.when(kind == 2)
     def _():
-        crossed[:ONE, :] = whole[1 - side, :ONE, :]
+        crossed[:ONE, :] = kept[1 - side, :ONE, :]
 
     @pl.when(kind == 3)
     def _():
         for half in range(2):
-            edge_cross[half * EDGE : (half + 1) * EDGE, :] = whole[half, ONE - EDGE : ONE, :]
-            edge_same[half * EDGE : (half + 1) * EDGE, :] = whole[half, :EDGE, :]
+            edge_cross[half * EDGE : (half + 1) * EDGE, :] = kept[half, ONE - EDGE : ONE, :]
+            edge_same[half * EDGE : (half + 1) * EDGE, :] = kept[half, :EDGE, :]
+
+
+def hold_kernel(turn, weights, ahead, sem):
+    @pl.when(turn[2] >= 1)
+    def _():
+        copy = pltpu.make_async_copy(weights.at[STATIONS - 1], ahead, sem)
+        copy.start()
+        copy.wait()
 
 
 def center_kernel(number, turn, direct, crossed, edge_same, edge_cross, out):
@@ -421,18 +436,18 @@
     odds, evens = list(range(1, sections, 2)), list(range(0, sections, 2))
     below = send(raw, (evens, -1, straight), (odds, 1, straight))
     incoming = None
-    pair_source = wide_source = None
+    pair_source = wide_source = ahead = None
     candidates = []
     for g in reversed(of_kind(0)):
         pieces = [] if incoming is None else [(incoming, lambda side: (0, 0), ONE, None)]
         (share,) = march(turn, g, inverse_blocks, coupling, pieces, 0, 2, POINTS, True, (raw,))
-        crossed, edge_cross, edge_same, direct, whole = pl.pallas_call(
+        crossed, edge_cross, edge_same, direct, kept = pl.pallas_call(
             functools.partial(ship_kernel, g),
             out_shape=[jax.ShapeDtypeStruct((size, FN), jnp.bfloat16) for size in (2 * ONE, WIDE, WIDE, 2 * ONE)]
             + [jax.ShapeDtypeStruct(share.shape, jnp.bfloat16)],
             in_specs=[smem, vmem, vmem, vmem],
             out_specs=[vmem] * 5,
-            scratch_shapes=[pltpu.VMEM((2, ONE, FN), jnp.float32)],
+            scratch_shapes=[pltpu.VMEM((2, ONE, FN), jnp.float32), pltpu.VMEM(share.shape, jnp.bfloat16)],
             compiler_params=pltpu.CompilerParams(vmem_limit_bytes=SMALL),
         )(turn, share, below, raw)
         first = incoming is None
@@ -441,13 +456,22 @@
         edge_same = send(edge_same, ([g], 1, outward), (of_kind(3) if first else [], 0, neighbor(-1)))
         direct = send(direct, ([g], 1, straight))
         if first:
+            later, _ = lax.optimization_barrier((turn, kept))
+            ahead = pl.pallas_call(
+                hold_kernel,
+                out_shape=jax.ShapeDtypeStruct((FN, FN), jnp.bfloat16),
+                in_specs=[smem, away],
+                out_specs=vmem,
+                scratch_shapes=[pltpu.SemaphoreType.DMA],
+                compiler_params=pltpu.CompilerParams(vmem_limit_bytes=GRANT),
+            )(later, inverse_blocks)
             pair_source = [
-                (whole, lambda side: (0, side * ONE), ONE, lambda side: side),
+                (kept, lambda side: (0, side * ONE), ONE, lambda side: side),
                 (crossed, lambda side: (0, (1 - side) * ONE), ONE, None),
             ]
             wide_source = [
                 (edge_cross.reshape(2, EDGE, FN), lambda side: (0, 0), EDGE, None),
-                (whole, lambda side: (0, EDGE), ONE, None),
+                (kept, lambda side: (0, EDGE), ONE, None),
                 (edge_same.reshape(2, EDGE, FN), lambda side: (0, EDGE + ONE), EDGE, None),
             ]
 
@@ -466,6 +490,8 @@
             1,
             3 * POINTS,
             False,
+            (),
+            (ahead,),
         )
         arrived = send(state, (list(range(sections)), 1, straight))
 
@@ -480,8 +506,9 @@
             2 * POINTS,
             True,
             (),
+            (ahead,),
             (
-                (share, state),
+                (kept, state),
                 (
                     (
                         0,
@@ -532,8 +559,10 @@
             2,
             2 * POINTS,
             False,
+            (),
+            (ahead,),
         )
-        candidates += [share, edge_cross, edge_same, state, crossed, back, last]
+        candidates += [kept, edge_cross, edge_same, state, crossed, back, last]
         if g > 3:
             incoming = send(last, ([g - 3], 1, straight))
 

time: 81.5 us -> 79.4 us (0.974)
  waiting for transfers between devices: 43.3 us -> 40.7 us
    ppermute x11, waiting for transfers between devices: 36.9 us -> 34.2 us  [send(): return lax.ppermute(value, AXES, routes)]
    unnamed x10 -> x14, local copies, waits for them, and re-layouts: 1.79 us -> 2.09 us
where the time goes in v3:
time: 79.4 us; the launch traced here: 79 us
  waiting for transfers between devices  40.7 us (51%)
  starting transfers between devices  21 us (26%)
  Pallas kernels  14.2 us (18%)
  local copies, waits for them, and re-layouts  2.09 us (3%)
  between operations  0.87 us (1%)
    ppermute x11, waiting for transfers between devices, send(): return lax.ppermute(value, AXES, routes)  34.2 us
    ppermute x11, starting transfers between devices, send(): return lax.ppermute(value, AXES, routes)  17.5 us
    pallas_call x4, Pallas kernels, march(): pl.pallas_call(functools.partial(march_kernel, number, [piece[1:] for pie...  6.78 us
    ppermute x4, waiting for transfers between devices, local(): lax.ppermute(total, 'span', [(s, s ^ digit * stride) for s in range(spans)])  6.47 us
    ppermute x4, starting transfers between devices, local(): lax.ppermute(total, 'span', [(s, s ^ digit * stride) for s in range(spans)])  3.56 us
    pallas_call x1, Pallas kernels, local(): pl.pallas_call(functools.partial(factor_kernel, 1.0 / float(FN * POINTS *...  3.5 us
    unnamed x14, local copies, waits for them, and re-layouts  2.09 us
  transfers between devices with their start and end apart: 15, of which 9 were waited for; matrix products, arithmetic and copies ran while one was open for 0% of the time, Pallas kernels for 8%

profile of v3, /device:TPU:0, one launch (start us, length us, event | category | flops | bytes accessed | tf_op | source)
XLA Modules:
  0.0 79.0 jit_solution(17459048533947067178)
XLA Ops:
  0.6 0.5 collective-permute-start
  1.1 0.0 slice-start
  1.1 0.1 pad_add_fusion.turn
  1.2 0.0 copy-start
  1.2 1.2 %copy-done = bf16[1,768,384]{2,1,0:T(8,128)(2,1)S(1)} copy-done((bf16[1,768,384]{2,1,0:T(8,128)(2,1)S(1)}, bf16[1,768,384]{2,1,0:T(8,128)(2,1)}, u32[]{:S(2)}) %copy-start) | copy-done | bytes 589848
  2.4 0.0 copy-start.2
  2.4 0.8 %copy-done.2 = f32[4,768]{1,0:T(4,128)S(1)} copy-done((f32[4,768]{1,0:T(4,128)S(1)}, f32[4,768]{1,0:T(4,128)}, u32[]{:S(2)}) %copy-start.2) | copy-done | bytes 12312
  3.3 0.0 slice-start.1
  3.3 0.6 shard_map.77.share
  3.9 0.0 collective-permute-done.below
  3.9 1.1 %shard_map.78 = (bf16[384,768]{1,0:T(8,128)(2,1)S(1)}, bf16[192,768]{1,0:T(8,128)(2,1)S(1)}, bf16[192,768]{1,0:T(8,128)(2,1)S(1)}, bf16[384,768]{1,0:T(8,128)(2,1)S(1)}, bf16[2,384,768]{2,1,0:T(8,128)(2,1)S(1)}) custom-call(s32[3]{0:T(128)S(1)} %pad_add_fusion.turn, bf16[2,384,768]{2,1,0:T(8,128)(2,1)S(1)} %shard_map.77.share, ...), custom_call_target="tpu_custom_call" | custom-call | tf_op jit(solution)/shard_map/pallas_call | solution.py:444
  5.0 0.7 collective-permute-start.1
  5.7 0.7 collective-permute-start.4
  6.4 4.5 %collective-permute-start.2 = (bf16[192,768]{1,0:T(8,128)(2,1)S(1)}, bf16[192,768]{1,0:T(8,128)(2,1)S(1)}, u32[]{:S(2)}, u32[]{:S(2)}) collective-permute-start(bf16[192,768]{1,0:T(8,128)(2,1)S(1)} %get-tuple-element.18), channel_id=1, source_target_pairs={{24,23},{25,18},{26,17},{27,20},{28,19},{29,22},{30,21},{31,16},{0... | collective-permute-start | bytes 884744 | tf_op jit(solution)/shard_map/ppermute | solution.py:396
  10.9 5.0 %collective-permute-start.3 = (bf16[192,768]{1,0:T(8,128)(2,1)S(1)}, bf16[192,768]{1,0:T(8,128)(2,1)S(1)}, u32[]{:S(2)}, u32[]{:S(2)}) collective-permute-start(bf16[192,768]{1,0:T(8,128)(2,1)S(1)} %get-tuple-element.19), channel_id=1, source_target_pairs={{24,22},{25,19},{26,16},{27,21},{28,18},{29,23},{30,20},{31,17},{0... | collective-permute-start | bytes 884744 | tf_op jit(solution)/shard_map/ppermute | solution.py:396
  15.8 0.0 slice-done
  15.9 0.0 slice-done.1
  15.9 0.8 %shard_map.79.refs_4_.refs_3_.refs_7_ = bf16[768,768]{1,0:T(8,128)(2,1)S(1)} custom-call(s32[3]{0:T(128)S(1)} %pad_add_fusion.turn, bf16[4,768,768]{2,1,0:T(8,128)(2,1)S(1)} %bitcast.10), custom_call_target="tpu_custom_call" | custom-call | tf_op jit(solution)/shard_map/pallas_call | solution.py:460
  16.7 4.8 %collective-permute-done.2.refs_1_ = bf16[192,768]{1,0:T(8,128)(2,1)S(1)} collective-permute-done((bf16[192,768]{1,0:T(8,128)(2,1)S(1)}, bf16[192,768]{1,0:T(8,128)(2,1)S(1)}, u32[]{:S(2)}, u32[]{:S(2)}) %collective-permute-start.2) | collective-permute-done | bytes 294944 | tf_op jit(solution)/shard_map/ppermute | solution.py:396
  21.5 1.9 %collective-permute-done.3.refs_2_ = bf16[192,768]{1,0:T(8,128)(2,1)S(1)} collective-permute-done((bf16[192,768]{1,0:T(8,128)(2,1)S(1)}, bf16[192,768]{1,0:T(8,128)(2,1)S(1)}, u32[]{:S(2)}, u32[]{:S(2)}) %collective-permute-start.3) | collective-permute-done | bytes 294944 | tf_op jit(solution)/shard_map/ppermute | solution.py:396
  23.4 0.0 collective-permute-done.1.refs_0_.refs_2_
  23.4 0.0 collective-permute-done.4.refs_3_
  23.4 0.6 shard_map.80.refs_5_.refs_3_
  24.0 0.9 %collective-permute-start.5 = (bf16[1,384,768]{2,1,0:T(8,128)(2,1)S(1)}, bf16[1,384,768]{2,1,0:T(8,128)(2,1)S(1)}, u32[]{:S(2)}, u32[]{:S(2)}) collective-permute-start(bf16[1,384,768]{2,1,0:T(8,128)(2,1)S(1)} %shard_map.80.refs_5_.refs_3_), channel_id=1, source_target_pairs={{0,24},{1,25},{2,26},{3,27},{4,28},{5,29},{6,30},{7,31},{8,0},{9,1... | collective-permute-start | bytes 1769480 | tf_op jit(solution)/shard_map/ppermute | solution.py:396
  24.9 7.4 %collective-permute-done.5.refs_0_ = bf16[1,384,768]{2,1,0:T(8,128)(2,1)S(1)} collective-permute-done((bf16[1,384,768]{2,1,0:T(8,128)(2,1)S(1)}, bf16[1,384,768]{2,1,0:T(8,128)(2,1)S(1)}, u32[]{:S(2)}, u32[]{:S(2)}) %collective-permute-start.5) | collective-permute-done | bytes 589856 | tf_op jit(solution)/shard_map/ppermute | solution.py:396
  32.3 0.6 shard_map.81
  32.9 1.3 %collective-permute-start.8 = (bf16[384,768]{1,0:T(8,128)(2,1)S(1)}, bf16[384,768]{1,0:T(8,128)(2,1)S(1)}, u32[]{:S(2)}, u32[]{:S(2)}) collective-permute-start(bf16[384,768]{1,0:T(8,128)(2,1)S(1)} %get-tuple-element.24), channel_id=1, source_target_pairs={{8,1},{9,0},{10,3},{11,2},{12,5},{13,4},{14,7},{15,6},{16,17},{17,... | collective-permute-start | bytes 1769480 | tf_op jit(solution)/shard_map/ppermute | solution.py:396
  34.2 1.3 %collective-permute-start.9 = (bf16[384,768]{1,0:T(8,128)(2,1)S(1)}, bf16[384,768]{1,0:T(8,128)(2,1)S(1)}, u32[]{:S(2)}, u32[]{:S(2)}) collective-permute-start(bf16[384,768]{1,0:T(8,128)(2,1)S(1)} %get-tuple-element.25), channel_id=1, source_target_pairs={{8,0},{9,1},{10,2},{11,3},{12,4},{13,5},{14,6},{15,7}} | collective-permute-start | bytes 1769480 | tf_op jit(solution)/shard_map/ppermute | solution.py:396
  35.5 1.3 %collective-permute-start.6 = (bf16[192,768]{1,0:T(8,128)(2,1)S(1)}, bf16[192,768]{1,0:T(8,128)(2,1)S(1)}, u32[]{:S(2)}, u32[]{:S(2)}) collective-permute-start(bf16[192,768]{1,0:T(8,128)(2,1)S(1)} %get-tuple-element.22), channel_id=1, source_target_pairs={{8,7},{9,2},{10,1},{11,4},{12,3},{13,6},{14,5},{15,0},{24,25},{25,... | collective-permute-start | bytes 884744 | tf_op jit(solution)/shard_map/ppermute | solution.py:396
  36.8 1.3 %collective-permute-start.7 = (bf16[192,768]{1,0:T(8,128)(2,1)S(1)}, bf16[192,768]{1,0:T(8,128)(2,1)S(1)}, u32[]{:S(2)}, u32[]{:S(2)}) collective-permute-start(bf16[192,768]{1,0:T(8,128)(2,1)S(1)} %get-tuple-element.23), channel_id=1, source_target_pairs={{8,2},{9,7},{10,4},{11,1},{12,6},{13,3},{14,0},{15,5},{24,31},{25,... | collective-permute-start | bytes 884744 | tf_op jit(solution)/shard_map/ppermute | solution.py:396
  38.1 17.0 %collective-permute-done.6.edge_cross.refs_1_ = bf16[192,768]{1,0:T(8,128)(2,1)S(1)} collective-permute-done((bf16[192,768]{1,0:T(8,128)(2,1)S(1)}, bf16[192,768]{1,0:T(8,128)(2,1)S(1)}, u32[]{:S(2)}, u32[]{:S(2)}) %collective-permute-start.6) | collective-permute-done | bytes 294944 | tf_op jit(solution)/shard_map/ppermute | solution.py:396
  55.1 3.0 %collective-permute-done.7.edge_same.refs_2_ = bf16[192,768]{1,0:T(8,128)(2,1)S(1)} collective-permute-done((bf16[192,768]{1,0:T(8,128)(2,1)S(1)}, bf16[192,768]{1,0:T(8,128)(2,1)S(1)}, u32[]{:S(2)}, u32[]{:S(2)}) %collective-permute-start.7) | collective-permute-done | bytes 294944 | tf_op jit(solution)/shard_map/ppermute | solution.py:396
  58.2 0.0 collective-permute-done.8.crossed.refs_0_.refs_4_
  58.2 0.0 collective-permute-done.9.direct.refs_3_
  58.2 0.7 shard_map.82
  58.9 0.1 collective-permute-start.10
  59.0 5.0 %shard_map.83.refs_6_ = bf16[2,192,768]{2,1,0:T(8,128)(2,1)S(1)} custom-call(s32[3]{0:T(128)S(1)} %pad_add_fusion.turn, f32[4,768]{1,0:T(4,128)S(1)} %copy-done.2, bf16[4,768,768]{2,1,0:T(8,128)(2,1)} %weights.9, bf16[384,768]{1,0:T(8,128)(2,1)S(1)} %collective-permute-done.8.crossed.refs_0_.refs_4_, ...), custom_call_target="tpu_custom_call" | custom-call | flops 2491416576 | bytes 4718592 | tf_op jit(solution)/shard_map/pallas_call | solution.py:185
  64.0 0.0 copy-start.1
  64.0 0.0 copy-start.3
  64.0 0.0 copy-start.4
  64.1 0.0 collective-permute-done.10.refs_5_
  64.1 1.4 %shard_map.84 = (bf16[2,192,768]{2,1,0:T(8,128)(2,1)S(1)}, f32[48,48]{1,0:T(8,128)S(1)}) custom-call(s32[3]{0:T(128)S(1)} %pad_add_fusion.turn, bf16[2,384,768]{2,1,0:T(8,128)(2,1)S(1)} %get-tuple-element.16.refs_1_.refs_4_.refs_5_.refs_0_, bf16[192,768]{1,0:T(8,128)(2,1)S(1)} %collective-permute-done.6.edge_cross.refs_1_, ...), custom_call_target="tpu_custom_call" | custom-call | tf_op jit(solution)/shard_map/pallas_call | solution.py:569
  65.4 0.1 collective-permute-start.11
  65.5 3.8 %collective-permute-done.11 = f32[48,48]{1,0:T(8,128)S(1)} collective-permute-done((f32[48,48]{1,0:T(8,128)S(1)}, f32[48,48]{1,0:T(8,128)S(1)}, u32[]{:S(2)}, u32[]{:S(2)}) %collective-permute-start.11) | collective-permute-done | bytes 9248 | tf_op jit(solution)/shard_map/ppermute | solution.py:588
  69.3 0.0 collective-permute-start.12
  69.3 1.4 %collective-permute-start.14 = (f32[48,48]{1,0:T(8,128)S(1)}, f32[48,48]{1,0:T(8,128)S(1)}, u32[]{:S(2)}, u32[]{:S(2)}) collective-permute-start(f32[48,48]{1,0:T(8,128)S(1)} %add.18), channel_id=1, source_target_pairs={{0,6},{1,7},{2,4},{3,5},{4,2},{5,3},{6,0},{7,1},{8,14},{9,15},{10,... | collective-permute-start | bytes 27656 | tf_op jit(solution)/shard_map/ppermute | solution.py:588
  70.8 2.1 %collective-permute-start.13 = (f32[48,48]{1,0:T(8,128)S(1)}, f32[48,48]{1,0:T(8,128)S(1)}, u32[]{:S(2)}, u32[]{:S(2)}) collective-permute-start(f32[48,48]{1,0:T(8,128)S(1)} %add.18), channel_id=1, source_target_pairs={{0,4},{1,5},{2,6},{3,7},{4,0},{5,1},{6,2},{7,3},{8,12},{9,13},{10,... | collective-permute-start | bytes 27656 | tf_op jit(solution)/shard_map/ppermute | solution.py:588
  72.8 0.3 collective-permute-done.12
  73.2 1.9 %collective-permute-done.14 = f32[48,48]{1,0:T(8,128)S(1)} collective-permute-done((f32[48,48]{1,0:T(8,128)S(1)}, f32[48,48]{1,0:T(8,128)S(1)}, u32[]{:S(2)}, u32[]{:S(2)}) %collective-permute-start.14) | collective-permute-done | bytes 9248 | tf_op jit(solution)/shard_map/ppermute | solution.py:588
  75.0 0.5 collective-permute-done.13
  75.5 0.0 copy-done.1
  75.5 0.0 copy-done.3
  75.5 0.0 copy-done.4
  75.5 3.5 %shard_map.85 = (bf16[768,384]{1,0:T(8,128)(2,1)}, f32[48,48]{1,0:T(8,128)}) custom-call(f32[48,48]{1,0:T(8,128)S(1)} %add.19.first, f32[48,48]{1,0:T(8,128)S(1)} %add.20.second, bf16[384,768]{1,0:T(8,128)(2,1)S(1)} %bitcast.16, bf16[384,48]{1,0:T(8,128)(2,1)S(1)} %copy-done.3, bf16[48,384]{1,0:T(8,128)(2,1)S(1)} %copy-done.4, f32[384,384]{1,0:T(8,128)S(1)} %copy-done.1), custom_call_target="tpu_custom_call" | custom-call | tf_op jit(solution)/shard_map/pallas_call | solution.py:595
  (4 shorter events, 0.0 us)
Async XLA Ops:
  0.6 3.3 %collective-permute-start = (bf16[768,384]{1,0:T(8,128)(2,1)}, bf16[768,384]{1,0:T(8,128)(2,1)S(1)}, u32[]{:S(2)}, u32[]{:S(2)}) collective-permute-start(bf16[768,384]{1,0:T(8,128)(2,1)} %bitcast.13), channel_id=1, source_target_pairs={{0,8},{1,9},{2,10},{3,11},{4,12},{5,13},{6,14},{7,15},{16,24},{17,... | collective-permute-start | bytes 1769480 | tf_op jit(solution)/shard_map/ppermute | solution.py:396
  1.1 14.7 %slice-start = ((s8[4718592]{0:T(1024)(128)(4,1)}), s8[4194304]{0:T(1024)(128)(4,1)S(1)}, s32[]{:S(2)}) async-start(s8[4718592]{0:T(1024)(128)(4,1)} %bitcast.9), calls=%async_computation | async-start | bytes 8388608
  1.2 1.2 %copy-start = (bf16[1,768,384]{2,1,0:T(8,128)(2,1)S(1)}, bf16[1,768,384]{2,1,0:T(8,128)(2,1)}, u32[]{:S(2)}) copy-start(bf16[1,768,384]{2,1,0:T(8,128)(2,1)} %param.8) | copy-start | bytes 1769476
  2.4 0.9 %copy-start.2 = (f32[4,768]{1,0:T(4,128)S(1)}, f32[4,768]{1,0:T(4,128)}, u32[]{:S(2)}) copy-start(f32[4,768]{1,0:T(4,128)} %coupling.7) | copy-start | bytes 36868
  3.3 12.6 %slice-start.1 = ((s8[4718592]{0:T(1024)(128)(4,1)}), s8[524288]{0:T(1024)(128)(4,1)S(1)}, s32[]{:S(2)}) async-start(s8[4718592]{0:T(1024)(128)(4,1)} %bitcast.9), calls=%async_computation.1 | async-start | bytes 1048576
  5.0 18.4 %collective-permute-start.1 = (bf16[384,768]{1,0:T(8,128)(2,1)S(1)}, bf16[384,768]{1,0:T(8,128)(2,1)S(1)}, u32[]{:S(2)}, u32[]{:S(2)}) collective-permute-start(bf16[384,768]{1,0:T(8,128)(2,1)S(1)} %get-tuple-element.17), channel_id=1, source_target_pairs={{24,17},{25,16},{26,19},{27,18},{28,21},{29,20},{30,23},{31,22},{8... | collective-permute-start | bytes 1769480 | tf_op jit(solution)/shard_map/ppermute | solution.py:396
  5.7 17.7 %collective-permute-start.4 = (bf16[384,768]{1,0:T(8,128)(2,1)S(1)}, bf16[384,768]{1,0:T(8,128)(2,1)S(1)}, u32[]{:S(2)}, u32[]{:S(2)}) collective-permute-start(bf16[384,768]{1,0:T(8,128)(2,1)S(1)} %get-tuple-element.20), channel_id=1, source_target_pairs={{24,16},{25,17},{26,18},{27,19},{28,20},{29,21},{30,22},{31,23}} | collective-permute-start | bytes 1769480 | tf_op jit(solution)/shard_map/ppermute | solution.py:396
  6.4 15.1 %collective-permute-start.2 = (bf16[192,768]{1,0:T(8,128)(2,1)S(1)}, bf16[192,768]{1,0:T(8,128)(2,1)S(1)}, u32[]{:S(2)}, u32[]{:S(2)}) collective-permute-start(bf16[192,768]{1,0:T(8,128)(2,1)S(1)} %get-tuple-element.18), channel_id=1, source_target_pairs={{24,23},{25,18},{26,17},{27,20},{28,19},{29,22},{30,21},{31,16},{0... | collective-permute-start | bytes 884744 | tf_op jit(solution)/shard_map/ppermute | solution.py:396
  10.9 12.5 %collective-permute-start.3 = (bf16[192,768]{1,0:T(8,128)(2,1)S(1)}, bf16[192,768]{1,0:T(8,128)(2,1)S(1)}, u32[]{:S(2)}, u32[]{:S(2)}) collective-permute-start(bf16[192,768]{1,0:T(8,128)(2,1)S(1)} %get-tuple-element.19), channel_id=1, source_target_pairs={{24,22},{25,19},{26,16},{27,21},{28,18},{29,23},{30,20},{31,17},{0... | collective-permute-start | bytes 884744 | tf_op jit(solution)/shard_map/ppermute | solution.py:396
  24.0 8.3 %collective-permute-start.5 = (bf16[1,384,768]{2,1,0:T(8,128)(2,1)S(1)}, bf16[1,384,768]{2,1,0:T(8,128)(2,1)S(1)}, u32[]{:S(2)}, u32[]{:S(2)}) collective-permute-start(bf16[1,384,768]{2,1,0:T(8,128)(2,1)S(1)} %shard_map.80.refs_5_.refs_3_), channel_id=1, source_target_pairs={{0,24},{1,25},{2,26},{3,27},{4,28},{5,29},{6,30},{7,31},{8,0},{9,1... | collective-permute-start | bytes 1769480 | tf_op jit(solution)/shard_map/ppermute | solution.py:396
  32.9 25.3 %collective-permute-start.8 = (bf16[384,768]{1,0:T(8,128)(2,1)S(1)}, bf16[384,768]{1,0:T(8,128)(2,1)S(1)}, u32[]{:S(2)}, u32[]{:S(2)}) collective-permute-start(bf16[384,768]{1,0:T(8,128)(2,1)S(1)} %get-tuple-element.24), channel_id=1, source_target_pairs={{8,1},{9,0},{10,3},{11,2},{12,5},{13,4},{14,7},{15,6},{16,17},{17,... | collective-permute-start | bytes 1769480 | tf_op jit(solution)/shard_map/ppermute | solution.py:396
  34.2 24.0 %collective-permute-start.9 = (bf16[384,768]{1,0:T(8,128)(2,1)S(1)}, bf16[384,768]{1,0:T(8,128)(2,1)S(1)}, u32[]{:S(2)}, u32[]{:S(2)}) collective-permute-start(bf16[384,768]{1,0:T(8,128)(2,1)S(1)} %get-tuple-element.25), channel_id=1, source_target_pairs={{8,0},{9,1},{10,2},{11,3},{12,4},{13,5},{14,6},{15,7}} | collective-permute-start | bytes 1769480 | tf_op jit(solution)/shard_map/ppermute | solution.py:396
  35.5 19.6 %collective-permute-start.6 = (bf16[192,768]{1,0:T(8,128)(2,1)S(1)}, bf16[192,768]{1,0:T(8,128)(2,1)S(1)}, u32[]{:S(2)}, u32[]{:S(2)}) collective-permute-start(bf16[192,768]{1,0:T(8,128)(2,1)S(1)} %get-tuple-element.22), channel_id=1, source_target_pairs={{8,7},{9,2},{10,1},{11,4},{12,3},{13,6},{14,5},{15,0},{24,25},{25,... | collective-permute-start | bytes 884744 | tf_op jit(solution)/shard_map/ppermute | solution.py:396
  36.8 21.4 %collective-permute-start.7 = (bf16[192,768]{1,0:T(8,128)(2,1)S(1)}, bf16[192,768]{1,0:T(8,128)(2,1)S(1)}, u32[]{:S(2)}, u32[]{:S(2)}) collective-permute-start(bf16[192,768]{1,0:T(8,128)(2,1)S(1)} %get-tuple-element.23), channel_id=1, source_target_pairs={{8,2},{9,7},{10,4},{11,1},{12,6},{13,3},{14,0},{15,5},{24,31},{25,... | collective-permute-start | bytes 884744 | tf_op jit(solution)/shard_map/ppermute | solution.py:396
  58.9 5.1 %collective-permute-start.10 = (bf16[2,192,768]{2,1,0:T(8,128)(2,1)S(1)}, bf16[2,192,768]{2,1,0:T(8,128)(2,1)S(1)}, u32[]{:S(2)}, u32[]{:S(2)}) collective-permute-start(bf16[2,192,768]{2,1,0:T(8,128)(2,1)S(1)} %shard_map.82), channel_id=1, source_target_pairs={{0,8},{1,9},{2,10},{3,11},{4,12},{5,13},{6,14},{7,15},{16,24},{17,... | collective-permute-start | bytes 1769480 | tf_op jit(solution)/shard_map/ppermute | solution.py:396
  64.0 11.5 %copy-start.1 = (f32[384,384]{1,0:T(8,128)S(1)}, f32[384,384]{1,0:T(8,128)}, u32[]{:S(2)}) copy-start(f32[384,384]{1,0:T(8,128)} %constant.40.clone.same_point) | copy-start | bytes 1769476
  64.0 11.5 %copy-start.3 = (bf16[384,48]{1,0:T(8,128)(2,1)S(1)}, bf16[384,48]{1,0:T(8,128)(2,1)}, u32[]{:S(2)}) copy-start(bf16[384,48]{1,0:T(8,128)(2,1)} %constant.38.clone.by_column) | copy-start | bytes 110596
  64.0 11.5 %copy-start.4 = (bf16[48,384]{1,0:T(8,128)(2,1)S(1)}, bf16[48,384]{1,0:T(8,128)(2,1)}, u32[]{:S(2)}) copy-start(bf16[48,384]{1,0:T(8,128)(2,1)} %constant.39.clone.by_place) | copy-start | bytes 110596
  65.4 3.9 %collective-permute-start.11 = (f32[48,48]{1,0:T(8,128)S(1)}, f32[48,48]{1,0:T(8,128)S(1)}, u32[]{:S(2)}, u32[]{:S(2)}) collective-permute-start(f32[48,48]{1,0:T(8,128)S(1)} %get-tuple-element.26), channel_id=1, source_target_pairs={{0,1},{1,0},{2,3},{3,2},{4,5},{5,4},{6,7},{7,6},{8,9},{9,8},{10,11... | collective-permute-start | bytes 27656 | tf_op jit(solution)/shard_map/ppermute | solution.py:588
  69.3 3.8 %collective-permute-start.12 = (f32[48,48]{1,0:T(8,128)S(1)}, f32[48,48]{1,0:T(8,128)S(1)}, u32[]{:S(2)}, u32[]{:S(2)}) collective-permute-start(f32[48,48]{1,0:T(8,128)S(1)} %add.18), channel_id=1, source_target_pairs={{0,2},{1,3},{2,0},{3,1},{4,6},{5,7},{6,4},{7,5},{8,10},{9,11},{10,... | collective-permute-start | bytes 27656 | tf_op jit(solution)/shard_map/ppermute | solution.py:588
  69.3 5.7 %collective-permute-start.14 = (f32[48,48]{1,0:T(8,128)S(1)}, f32[48,48]{1,0:T(8,128)S(1)}, u32[]{:S(2)}, u32[]{:S(2)}) collective-permute-start(f32[48,48]{1,0:T(8,128)S(1)} %add.18), channel_id=1, source_target_pairs={{0,6},{1,7},{2,4},{3,5},{4,2},{5,3},{6,0},{7,1},{8,14},{9,15},{10,... | collective-permute-start | bytes 27656 | tf_op jit(solution)/shard_map/ppermute | solution.py:588
  70.8 4.7 %collective-permute-start.13 = (f32[48,48]{1,0:T(8,128)S(1)}, f32[48,48]{1,0:T(8,128)S(1)}, u32[]{:S(2)}, u32[]{:S(2)}) collective-permute-start(f32[48,48]{1,0:T(8,128)S(1)} %add.18), channel_id=1, source_target_pairs={{0,4},{1,5},{2,6},{3,7},{4,0},{5,1},{6,2},{7,3},{8,12},{9,13},{10,... | collective-permute-start | bytes 27656 | tf_op jit(solution)/shard_map/ppermute | solution.py:588

commit v4 on v3

--- a/solution.py
+++ b/solution.py
@@ -16,7 +16,7 @@
 ONE = POINTS * HALF
 EDGE = STATIONS * HALF
 WIDE = 2 * EDGE
-STEP = 6
+STEP = 8
 GRANT = 48 * 1024 * 1024
 SMALL = 16 * 1024 * 1024
 AXES = ("section", "span")

time: 79.4 us -> 79.3 us (level)
  no operation moved by 1% of the time
where the time goes in v4:
time: 79.3 us; the launch traced here: 78.9 us
  waiting for transfers between devices  40.7 us (51%)
  starting transfers between devices  21 us (26%)
  Pallas kernels  14.1 us (18%)
  local copies, waits for them, and re-layouts  2.09 us (3%)
  between operations  0.87 us (1%)
    ppermute x11, waiting for transfers between devices, send(): return lax.ppermute(value, AXES, routes)  34.2 us
    ppermute x11, starting transfers between devices, send(): return lax.ppermute(value, AXES, routes)  17.5 us
    pallas_call x4, Pallas kernels, march(): pl.pallas_call(functools.partial(march_kernel, number, [piece[1:] for pie...  6.78 us
    ppermute x4, waiting for transfers between devices, local(): lax.ppermute(total, 'span', [(s, s ^ digit * stride) for s in range(spans)])  6.47 us
    ppermute x4, starting transfers between devices, local(): lax.ppermute(total, 'span', [(s, s ^ digit * stride) for s in range(spans)])  3.56 us
    pallas_call x1, Pallas kernels, local(): pl.pallas_call(functools.partial(factor_kernel, 1.0 / float(FN * POINTS *...  3.35 us
    unnamed x14, local copies, waits for them, and re-layouts  2.09 us
  transfers between devices with their start and end apart: 15, of which 9 were waited for; matrix products, arithmetic and copies ran while one was open for 0% of the time, Pallas kernels for 8%

profile of v4, /device:TPU:0, one launch (start us, length us, event | category | flops | bytes accessed | tf_op | source)
XLA Modules:
  0.0 78.9 jit_solution(11983524683831880449)
XLA Ops:
  0.6 0.5 collective-permute-start
  1.1 0.0 slice-start
  1.1 0.1 pad_add_fusion.turn
  1.2 0.0 copy-start
  1.2 1.2 %copy-done = bf16[1,768,384]{2,1,0:T(8,128)(2,1)S(1)} copy-done((bf16[1,768,384]{2,1,0:T(8,128)(2,1)S(1)}, bf16[1,768,384]{2,1,0:T(8,128)(2,1)}, u32[]{:S(2)}) %copy-start) | copy-done | bytes 589848
  2.4 0.0 copy-start.2
  2.4 0.8 %copy-done.2 = f32[4,768]{1,0:T(4,128)S(1)} copy-done((f32[4,768]{1,0:T(4,128)S(1)}, f32[4,768]{1,0:T(4,128)}, u32[]{:S(2)}) %copy-start.2) | copy-done | bytes 12312
  3.3 0.0 slice-start.1
  3.3 0.6 shard_map.77.share
  3.9 0.0 collective-permute-done.below
  3.9 1.1 %shard_map.78 = (bf16[384,768]{1,0:T(8,128)(2,1)S(1)}, bf16[192,768]{1,0:T(8,128)(2,1)S(1)}, bf16[192,768]{1,0:T(8,128)(2,1)S(1)}, bf16[384,768]{1,0:T(8,128)(2,1)S(1)}, bf16[2,384,768]{2,1,0:T(8,128)(2,1)S(1)}) custom-call(s32[3]{0:T(128)S(1)} %pad_add_fusion.turn, bf16[2,384,768]{2,1,0:T(8,128)(2,1)S(1)} %shard_map.77.share, ...), custom_call_target="tpu_custom_call" | custom-call | tf_op jit(solution)/shard_map/pallas_call | solution.py:444
  5.0 0.7 collective-permute-start.1
  5.7 0.7 collective-permute-start.4
  6.4 4.5 %collective-permute-start.2 = (bf16[192,768]{1,0:T(8,128)(2,1)S(1)}, bf16[192,768]{1,0:T(8,128)(2,1)S(1)}, u32[]{:S(2)}, u32[]{:S(2)}) collective-permute-start(bf16[192,768]{1,0:T(8,128)(2,1)S(1)} %get-tuple-element.18), channel_id=1, source_target_pairs={{24,23},{25,18},{26,17},{27,20},{28,19},{29,22},{30,21},{31,16},{0... | collective-permute-start | bytes 884744 | tf_op jit(solution)/shard_map/ppermute | solution.py:396
  10.9 5.0 %collective-permute-start.3 = (bf16[192,768]{1,0:T(8,128)(2,1)S(1)}, bf16[192,768]{1,0:T(8,128)(2,1)S(1)}, u32[]{:S(2)}, u32[]{:S(2)}) collective-permute-start(bf16[192,768]{1,0:T(8,128)(2,1)S(1)} %get-tuple-element.19), channel_id=1, source_target_pairs={{24,22},{25,19},{26,16},{27,21},{28,18},{29,23},{30,20},{31,17},{0... | collective-permute-start | bytes 884744 | tf_op jit(solution)/shard_map/ppermute | solution.py:396
  15.8 0.0 slice-done
  15.9 0.0 slice-done.1
  15.9 0.8 %shard_map.79.refs_4_.refs_3_.refs_7_ = bf16[768,768]{1,0:T(8,128)(2,1)S(1)} custom-call(s32[3]{0:T(128)S(1)} %pad_add_fusion.turn, bf16[4,768,768]{2,1,0:T(8,128)(2,1)S(1)} %bitcast.10), custom_call_target="tpu_custom_call" | custom-call | tf_op jit(solution)/shard_map/pallas_call | solution.py:460
  16.7 4.8 %collective-permute-done.2.refs_1_ = bf16[192,768]{1,0:T(8,128)(2,1)S(1)} collective-permute-done((bf16[192,768]{1,0:T(8,128)(2,1)S(1)}, bf16[192,768]{1,0:T(8,128)(2,1)S(1)}, u32[]{:S(2)}, u32[]{:S(2)}) %collective-permute-start.2) | collective-permute-done | bytes 294944 | tf_op jit(solution)/shard_map/ppermute | solution.py:396
  21.5 1.9 %collective-permute-done.3.refs_2_ = bf16[192,768]{1,0:T(8,128)(2,1)S(1)} collective-permute-done((bf16[192,768]{1,0:T(8,128)(2,1)S(1)}, bf16[192,768]{1,0:T(8,128)(2,1)S(1)}, u32[]{:S(2)}, u32[]{:S(2)}) %collective-permute-start.3) | collective-permute-done | bytes 294944 | tf_op jit(solution)/shard_map/ppermute | solution.py:396
  23.4 0.0 collective-permute-done.1.refs_0_.refs_2_
  23.4 0.0 collective-permute-done.4.refs_3_
  23.4 0.6 shard_map.80.refs_5_.refs_3_
  24.0 0.9 %collective-permute-start.5 = (bf16[1,384,768]{2,1,0:T(8,128)(2,1)S(1)}, bf16[1,384,768]{2,1,0:T(8,128)(2,1)S(1)}, u32[]{:S(2)}, u32[]{:S(2)}) collective-permute-start(bf16[1,384,768]{2,1,0:T(8,128)(2,1)S(1)} %shard_map.80.refs_5_.refs_3_), channel_id=1, source_target_pairs={{0,24},{1,25},{2,26},{3,27},{4,28},{5,29},{6,30},{7,31},{8,0},{9,1... | collective-permute-start | bytes 1769480 | tf_op jit(solution)/shard_map/ppermute | solution.py:396
  24.9 7.4 %collective-permute-done.5.refs_0_ = bf16[1,384,768]{2,1,0:T(8,128)(2,1)S(1)} collective-permute-done((bf16[1,384,768]{2,1,0:T(8,128)(2,1)S(1)}, bf16[1,384,768]{2,1,0:T(8,128)(2,1)S(1)}, u32[]{:S(2)}, u32[]{:S(2)}) %collective-permute-start.5) | collective-permute-done | bytes 589856 | tf_op jit(solution)/shard_map/ppermute | solution.py:396
  32.3 0.6 shard_map.81
  32.9 1.3 %collective-permute-start.8 = (bf16[384,768]{1,0:T(8,128)(2,1)S(1)}, bf16[384,768]{1,0:T(8,128)(2,1)S(1)}, u32[]{:S(2)}, u32[]{:S(2)}) collective-permute-start(bf16[384,768]{1,0:T(8,128)(2,1)S(1)} %get-tuple-element.24), channel_id=1, source_target_pairs={{8,1},{9,0},{10,3},{11,2},{12,5},{13,4},{14,7},{15,6},{16,17},{17,... | collective-permute-start | bytes 1769480 | tf_op jit(solution)/shard_map/ppermute | solution.py:396
  34.2 1.3 %collective-permute-start.9 = (bf16[384,768]{1,0:T(8,128)(2,1)S(1)}, bf16[384,768]{1,0:T(8,128)(2,1)S(1)}, u32[]{:S(2)}, u32[]{:S(2)}) collective-permute-start(bf16[384,768]{1,0:T(8,128)(2,1)S(1)} %get-tuple-element.25), channel_id=1, source_target_pairs={{8,0},{9,1},{10,2},{11,3},{12,4},{13,5},{14,6},{15,7}} | collective-permute-start | bytes 1769480 | tf_op jit(solution)/shard_map/ppermute | solution.py:396
  35.5 1.3 %collective-permute-start.6 = (bf16[192,768]{1,0:T(8,128)(2,1)S(1)}, bf16[192,768]{1,0:T(8,128)(2,1)S(1)}, u32[]{:S(2)}, u32[]{:S(2)}) collective-permute-start(bf16[192,768]{1,0:T(8,128)(2,1)S(1)} %get-tuple-element.22), channel_id=1, source_target_pairs={{8,7},{9,2},{10,1},{11,4},{12,3},{13,6},{14,5},{15,0},{24,25},{25,... | collective-permute-start | bytes 884744 | tf_op jit(solution)/shard_map/ppermute | solution.py:396
  36.8 1.3 %collective-permute-start.7 = (bf16[192,768]{1,0:T(8,128)(2,1)S(1)}, bf16[192,768]{1,0:T(8,128)(2,1)S(1)}, u32[]{:S(2)}, u32[]{:S(2)}) collective-permute-start(bf16[192,768]{1,0:T(8,128)(2,1)S(1)} %get-tuple-element.23), channel_id=1, source_target_pairs={{8,2},{9,7},{10,4},{11,1},{12,6},{13,3},{14,0},{15,5},{24,31},{25,... | collective-permute-start | bytes 884744 | tf_op jit(solution)/shard_map/ppermute | solution.py:396
  38.1 17.0 %collective-permute-done.6.edge_cross.refs_1_ = bf16[192,768]{1,0:T(8,128)(2,1)S(1)} collective-permute-done((bf16[192,768]{1,0:T(8,128)(2,1)S(1)}, bf16[192,768]{1,0:T(8,128)(2,1)S(1)}, u32[]{:S(2)}, u32[]{:S(2)}) %collective-permute-start.6) | collective-permute-done | bytes 294944 | tf_op jit(solution)/shard_map/ppermute | solution.py:396
  55.1 3.0 %collective-permute-done.7.edge_same.refs_2_ = bf16[192,768]{1,0:T(8,128)(2,1)S(1)} collective-permute-done((bf16[192,768]{1,0:T(8,128)(2,1)S(1)}, bf16[192,768]{1,0:T(8,128)(2,1)S(1)}, u32[]{:S(2)}, u32[]{:S(2)}) %collective-permute-start.7) | collective-permute-done | bytes 294944 | tf_op jit(solution)/shard_map/ppermute | solution.py:396
  58.2 0.0 collective-permute-done.8.crossed.refs_0_.refs_4_
  58.2 0.0 collective-permute-done.9.direct.refs_3_
  58.2 0.7 shard_map.82
  58.9 0.1 collective-permute-start.10
  59.0 5.0 %shard_map.83.refs_6_ = bf16[2,192,768]{2,1,0:T(8,128)(2,1)S(1)} custom-call(s32[3]{0:T(128)S(1)} %pad_add_fusion.turn, f32[4,768]{1,0:T(4,128)S(1)} %copy-done.2, bf16[4,768,768]{2,1,0:T(8,128)(2,1)} %weights.9, bf16[384,768]{1,0:T(8,128)(2,1)S(1)} %collective-permute-done.8.crossed.refs_0_.refs_4_, ...), custom_call_target="tpu_custom_call" | custom-call | flops 2491416576 | bytes 4718592 | tf_op jit(solution)/shard_map/pallas_call | solution.py:185
  64.0 0.0 copy-start.1
  64.0 0.0 copy-start.3
  64.0 0.0 copy-start.4
  64.1 0.0 collective-permute-done.10.refs_5_
  64.1 1.4 %shard_map.84 = (bf16[2,192,768]{2,1,0:T(8,128)(2,1)S(1)}, f32[48,48]{1,0:T(8,128)S(1)}) custom-call(s32[3]{0:T(128)S(1)} %pad_add_fusion.turn, bf16[2,384,768]{2,1,0:T(8,128)(2,1)S(1)} %get-tuple-element.16.refs_1_.refs_4_.refs_5_.refs_0_, bf16[192,768]{1,0:T(8,128)(2,1)S(1)} %collective-permute-done.6.edge_cross.refs_1_, ...), custom_call_target="tpu_custom_call" | custom-call | tf_op jit(solution)/shard_map/pallas_call | solution.py:569
  65.4 0.1 collective-permute-start.11
  65.5 3.8 %collective-permute-done.11 = f32[48,48]{1,0:T(8,128)S(1)} collective-permute-done((f32[48,48]{1,0:T(8,128)S(1)}, f32[48,48]{1,0:T(8,128)S(1)}, u32[]{:S(2)}, u32[]{:S(2)}) %collective-permute-start.11) | collective-permute-done | bytes 9248 | tf_op jit(solution)/shard_map/ppermute | solution.py:588
  69.3 0.0 collective-permute-start.12
  69.3 1.4 %collective-permute-start.14 = (f32[48,48]{1,0:T(8,128)S(1)}, f32[48,48]{1,0:T(8,128)S(1)}, u32[]{:S(2)}, u32[]{:S(2)}) collective-permute-start(f32[48,48]{1,0:T(8,128)S(1)} %add.18), channel_id=1, source_target_pairs={{0,6},{1,7},{2,4},{3,5},{4,2},{5,3},{6,0},{7,1},{8,14},{9,15},{10,... | collective-permute-start | bytes 27656 | tf_op jit(solution)/shard_map/ppermute | solution.py:588
  70.8 2.1 %collective-permute-start.13 = (f32[48,48]{1,0:T(8,128)S(1)}, f32[48,48]{1,0:T(8,128)S(1)}, u32[]{:S(2)}, u32[]{:S(2)}) collective-permute-start(f32[48,48]{1,0:T(8,128)S(1)} %add.18), channel_id=1, source_target_pairs={{0,4},{1,5},{2,6},{3,7},{4,0},{5,1},{6,2},{7,3},{8,12},{9,13},{10,... | collective-permute-start | bytes 27656 | tf_op jit(solution)/shard_map/ppermute | solution.py:588
  72.8 0.3 collective-permute-done.12
  73.2 1.9 %collective-permute-done.14 = f32[48,48]{1,0:T(8,128)S(1)} collective-permute-done((f32[48,48]{1,0:T(8,128)S(1)}, f32[48,48]{1,0:T(8,128)S(1)}, u32[]{:S(2)}, u32[]{:S(2)}) %collective-permute-start.14) | collective-permute-done | bytes 9248 | tf_op jit(solution)/shard_map/ppermute | solution.py:588
  75.0 0.5 collective-permute-done.13
  75.5 0.0 copy-done.1
  75.5 0.0 copy-done.3
  75.5 0.0 copy-done.4
  75.5 3.3 %shard_map.85 = (bf16[768,384]{1,0:T(8,128)(2,1)}, f32[48,48]{1,0:T(8,128)}) custom-call(f32[48,48]{1,0:T(8,128)S(1)} %add.19.first, f32[48,48]{1,0:T(8,128)S(1)} %add.20.second, bf16[384,768]{1,0:T(8,128)(2,1)S(1)} %bitcast.16, bf16[384,48]{1,0:T(8,128)(2,1)S(1)} %copy-done.3, bf16[48,384]{1,0:T(8,128)(2,1)S(1)} %copy-done.4, f32[384,384]{1,0:T(8,128)S(1)} %copy-done.1), custom_call_target="tpu_custom_call" | custom-call | tf_op jit(solution)/shard_map/pallas_call | solution.py:595
  (4 shorter events, 0.0 us)
Async XLA Ops:
  0.6 3.3 %collective-permute-start = (bf16[768,384]{1,0:T(8,128)(2,1)}, bf16[768,384]{1,0:T(8,128)(2,1)S(1)}, u32[]{:S(2)}, u32[]{:S(2)}) collective-permute-start(bf16[768,384]{1,0:T(8,128)(2,1)} %bitcast.13), channel_id=1, source_target_pairs={{0,8},{1,9},{2,10},{3,11},{4,12},{5,13},{6,14},{7,15},{16,24},{17,... | collective-permute-start | bytes 1769480 | tf_op jit(solution)/shard_map/ppermute | solution.py:396
  1.1 14.7 %slice-start = ((s8[4718592]{0:T(1024)(128)(4,1)}), s8[4194304]{0:T(1024)(128)(4,1)S(1)}, s32[]{:S(2)}) async-start(s8[4718592]{0:T(1024)(128)(4,1)} %bitcast.9), calls=%async_computation | async-start | bytes 8388608
  1.2 1.2 %copy-start = (bf16[1,768,384]{2,1,0:T(8,128)(2,1)S(1)}, bf16[1,768,384]{2,1,0:T(8,128)(2,1)}, u32[]{:S(2)}) copy-start(bf16[1,768,384]{2,1,0:T(8,128)(2,1)} %param.8) | copy-start | bytes 1769476
  2.4 0.9 %copy-start.2 = (f32[4,768]{1,0:T(4,128)S(1)}, f32[4,768]{1,0:T(4,128)}, u32[]{:S(2)}) copy-start(f32[4,768]{1,0:T(4,128)} %coupling.7) | copy-start | bytes 36868
  3.3 12.6 %slice-start.1 = ((s8[4718592]{0:T(1024)(128)(4,1)}), s8[524288]{0:T(1024)(128)(4,1)S(1)}, s32[]{:S(2)}) async-start(s8[4718592]{0:T(1024)(128)(4,1)} %bitcast.9), calls=%async_computation.1 | async-start | bytes 1048576
  5.0 18.4 %collective-permute-start.1 = (bf16[384,768]{1,0:T(8,128)(2,1)S(1)}, bf16[384,768]{1,0:T(8,128)(2,1)S(1)}, u32[]{:S(2)}, u32[]{:S(2)}) collective-permute-start(bf16[384,768]{1,0:T(8,128)(2,1)S(1)} %get-tuple-element.17), channel_id=1, source_target_pairs={{24,17},{25,16},{26,19},{27,18},{28,21},{29,20},{30,23},{31,22},{8... | collective-permute-start | bytes 1769480 | tf_op jit(solution)/shard_map/ppermute | solution.py:396
  5.7 17.7 %collective-permute-start.4 = (bf16[384,768]{1,0:T(8,128)(2,1)S(1)}, bf16[384,768]{1,0:T(8,128)(2,1)S(1)}, u32[]{:S(2)}, u32[]{:S(2)}) collective-permute-start(bf16[384,768]{1,0:T(8,128)(2,1)S(1)} %get-tuple-element.20), channel_id=1, source_target_pairs={{24,16},{25,17},{26,18},{27,19},{28,20},{29,21},{30,22},{31,23}} | collective-permute-start | bytes 1769480 | tf_op jit(solution)/shard_map/ppermute | solution.py:396
  6.4 15.1 %collective-permute-start.2 = (bf16[192,768]{1,0:T(8,128)(2,1)S(1)}, bf16[192,768]{1,0:T(8,128)(2,1)S(1)}, u32[]{:S(2)}, u32[]{:S(2)}) collective-permute-start(bf16[192,768]{1,0:T(8,128)(2,1)S(1)} %get-tuple-element.18), channel_id=1, source_target_pairs={{24,23},{25,18},{26,17},{27,20},{28,19},{29,22},{30,21},{31,16},{0... | collective-permute-start | bytes 884744 | tf_op jit(solution)/shard_map/ppermute | solution.py:396
  10.9 12.5 %collective-permute-start.3 = (bf16[192,768]{1,0:T(8,128)(2,1)S(1)}, bf16[192,768]{1,0:T(8,128)(2,1)S(1)}, u32[]{:S(2)}, u32[]{:S(2)}) collective-permute-start(bf16[192,768]{1,0:T(8,128)(2,1)S(1)} %get-tuple-element.19), channel_id=1, source_target_pairs={{24,22},{25,19},{26,16},{27,21},{28,18},{29,23},{30,20},{31,17},{0... | collective-permute-start | bytes 884744 | tf_op jit(solution)/shard_map/ppermute | solution.py:396
  24.0 8.3 %collective-permute-start.5 = (bf16[1,384,768]{2,1,0:T(8,128)(2,1)S(1)}, bf16[1,384,768]{2,1,0:T(8,128)(2,1)S(1)}, u32[]{:S(2)}, u32[]{:S(2)}) collective-permute-start(bf16[1,384,768]{2,1,0:T(8,128)(2,1)S(1)} %shard_map.80.refs_5_.refs_3_), channel_id=1, source_target_pairs={{0,24},{1,25},{2,26},{3,27},{4,28},{5,29},{6,30},{7,31},{8,0},{9,1... | collective-permute-start | bytes 1769480 | tf_op jit(solution)/shard_map/ppermute | solution.py:396
  32.9 25.3 %collective-permute-start.8 = (bf16[384,768]{1,0:T(8,128)(2,1)S(1)}, bf16[384,768]{1,0:T(8,128)(2,1)S(1)}, u32[]{:S(2)}, u32[]{:S(2)}) collective-permute-start(bf16[384,768]{1,0:T(8,128)(2,1)S(1)} %get-tuple-element.24), channel_id=1, source_target_pairs={{8,1},{9,0},{10,3},{11,2},{12,5},{13,4},{14,7},{15,6},{16,17},{17,... | collective-permute-start | bytes 1769480 | tf_op jit(solution)/shard_map/ppermute | solution.py:396
  34.2 24.0 %collective-permute-start.9 = (bf16[384,768]{1,0:T(8,128)(2,1)S(1)}, bf16[384,768]{1,0:T(8,128)(2,1)S(1)}, u32[]{:S(2)}, u32[]{:S(2)}) collective-permute-start(bf16[384,768]{1,0:T(8,128)(2,1)S(1)} %get-tuple-element.25), channel_id=1, source_target_pairs={{8,0},{9,1},{10,2},{11,3},{12,4},{13,5},{14,6},{15,7}} | collective-permute-start | bytes 1769480 | tf_op jit(solution)/shard_map/ppermute | solution.py:396
  35.5 19.6 %collective-permute-start.6 = (bf16[192,768]{1,0:T(8,128)(2,1)S(1)}, bf16[192,768]{1,0:T(8,128)(2,1)S(1)}, u32[]{:S(2)}, u32[]{:S(2)}) collective-permute-start(bf16[192,768]{1,0:T(8,128)(2,1)S(1)} %get-tuple-element.22), channel_id=1, source_target_pairs={{8,7},{9,2},{10,1},{11,4},{12,3},{13,6},{14,5},{15,0},{24,25},{25,... | collective-permute-start | bytes 884744 | tf_op jit(solution)/shard_map/ppermute | solution.py:396
  36.8 21.4 %collective-permute-start.7 = (bf16[192,768]{1,0:T(8,128)(2,1)S(1)}, bf16[192,768]{1,0:T(8,128)(2,1)S(1)}, u32[]{:S(2)}, u32[]{:S(2)}) collective-permute-start(bf16[192,768]{1,0:T(8,128)(2,1)S(1)} %get-tuple-element.23), channel_id=1, source_target_pairs={{8,2},{9,7},{10,4},{11,1},{12,6},{13,3},{14,0},{15,5},{24,31},{25,... | collective-permute-start | bytes 884744 | tf_op jit(solution)/shard_map/ppermute | solution.py:396
  58.9 5.1 %collective-permute-start.10 = (bf16[2,192,768]{2,1,0:T(8,128)(2,1)S(1)}, bf16[2,192,768]{2,1,0:T(8,128)(2,1)S(1)}, u32[]{:S(2)}, u32[]{:S(2)}) collective-permute-start(bf16[2,192,768]{2,1,0:T(8,128)(2,1)S(1)} %shard_map.82), channel_id=1, source_target_pairs={{0,8},{1,9},{2,10},{3,11},{4,12},{5,13},{6,14},{7,15},{16,24},{17,... | collective-permute-start | bytes 1769480 | tf_op jit(solution)/shard_map/ppermute | solution.py:396
  64.0 11.5 %copy-start.1 = (f32[384,384]{1,0:T(8,128)S(1)}, f32[384,384]{1,0:T(8,128)}, u32[]{:S(2)}) copy-start(f32[384,384]{1,0:T(8,128)} %constant.40.clone.same_point) | copy-start | bytes 1769476
  64.0 11.5 %copy-start.3 = (bf16[384,48]{1,0:T(8,128)(2,1)S(1)}, bf16[384,48]{1,0:T(8,128)(2,1)}, u32[]{:S(2)}) copy-start(bf16[384,48]{1,0:T(8,128)(2,1)} %constant.38.clone.by_column) | copy-start | bytes 110596
  64.0 11.5 %copy-start.4 = (bf16[48,384]{1,0:T(8,128)(2,1)S(1)}, bf16[48,384]{1,0:T(8,128)(2,1)}, u32[]{:S(2)}) copy-start(bf16[48,384]{1,0:T(8,128)(2,1)} %constant.39.clone.by_place) | copy-start | bytes 110596
  65.4 3.9 %collective-permute-start.11 = (f32[48,48]{1,0:T(8,128)S(1)}, f32[48,48]{1,0:T(8,128)S(1)}, u32[]{:S(2)}, u32[]{:S(2)}) collective-permute-start(f32[48,48]{1,0:T(8,128)S(1)} %get-tuple-element.26), channel_id=1, source_target_pairs={{0,1},{1,0},{2,3},{3,2},{4,5},{5,4},{6,7},{7,6},{8,9},{9,8},{10,11... | collective-permute-start | bytes 27656 | tf_op jit(solution)/shard_map/ppermute | solution.py:588
  69.3 3.8 %collective-permute-start.12 = (f32[48,48]{1,0:T(8,128)S(1)}, f32[48,48]{1,0:T(8,128)S(1)}, u32[]{:S(2)}, u32[]{:S(2)}) collective-permute-start(f32[48,48]{1,0:T(8,128)S(1)} %add.18), channel_id=1, source_target_pairs={{0,2},{1,3},{2,0},{3,1},{4,6},{5,7},{6,4},{7,5},{8,10},{9,11},{10,... | collective-permute-start | bytes 27656 | tf_op jit(solution)/shard_map/ppermute | solution.py:588
  69.3 5.7 %collective-permute-start.14 = (f32[48,48]{1,0:T(8,128)S(1)}, f32[48,48]{1,0:T(8,128)S(1)}, u32[]{:S(2)}, u32[]{:S(2)}) collective-permute-start(f32[48,48]{1,0:T(8,128)S(1)} %add.18), channel_id=1, source_target_pairs={{0,6},{1,7},{2,4},{3,5},{4,2},{5,3},{6,0},{7,1},{8,14},{9,15},{10,... | collective-permute-start | bytes 27656 | tf_op jit(solution)/shard_map/ppermute | solution.py:588
  70.8 4.7 %collective-permute-start.13 = (f32[48,48]{1,0:T(8,128)S(1)}, f32[48,48]{1,0:T(8,128)S(1)}, u32[]{:S(2)}, u32[]{:S(2)}) collective-permute-start(f32[48,48]{1,0:T(8,128)S(1)} %add.18), channel_id=1, source_target_pairs={{0,4},{1,5},{2,6},{3,7},{4,0},{5,1},{6,2},{7,3},{8,12},{9,13},{10,... | collective-permute-start | bytes 27656 | tf_op jit(solution)/shard_map/ppermute | solution.py:588

commit v5 on v4

--- a/solution.py
+++ b/solution.py
@@ -16,7 +16,7 @@
 ONE = POINTS * HALF
 EDGE = STATIONS * HALF
 WIDE = 2 * EDGE
-STEP = 8
+STEP = 12
 GRANT = 48 * 1024 * 1024
 SMALL = 16 * 1024 * 1024
 AXES = ("section", "span")

time: 79.3 us -> 79.4 us (level)
  no operation moved by 1% of the time
where the time goes in v5:
time: 79.4 us; the launch traced here: 79 us
  waiting for transfers between devices  40.7 us (51%)
  starting transfers between devices  21 us (26%)
  Pallas kernels  14.2 us (18%)
  local copies, waits for them, and re-layouts  2.09 us (3%)
  between operations  0.87 us (1%)
    ppermute x11, waiting for transfers between devices, send(): return lax.ppermute(value, AXES, routes)  34.2 us
    ppermute x11, starting transfers between devices, send(): return lax.ppermute(value, AXES, routes)  17.5 us
    pallas_call x4, Pallas kernels, march(): pl.pallas_call(functools.partial(march_kernel, number, [piece[1:] for pie...  6.78 us
    ppermute x4, waiting for transfers between devices, local(): lax.ppermute(total, 'span', [(s, s ^ digit * stride) for s in range(spans)])  6.47 us
    ppermute x4, starting transfers between devices, local(): lax.ppermute(total, 'span', [(s, s ^ digit * stride) for s in range(spans)])  3.56 us
    pallas_call x1, Pallas kernels, local(): pl.pallas_call(functools.partial(factor_kernel, 1.0 / float(FN * POINTS *...  3.47 us
    unnamed x14, local copies, waits for them, and re-layouts  2.09 us
  transfers between devices with their start and end apart: 15, of which 9 were waited for; matrix products, arithmetic and copies ran while one was open for 0% of the time, Pallas kernels for 8%

profile of v5, /device:TPU:0, one launch (start us, length us, event | category | flops | bytes accessed | tf_op | source)
XLA Modules:
  0.0 79.0 jit_solution(9200685507675267774)
XLA Ops:
  0.6 0.5 collective-permute-start
  1.1 0.0 slice-start
  1.1 0.1 pad_add_fusion.turn
  1.2 0.0 copy-start
  1.2 1.2 %copy-done = bf16[1,768,384]{2,1,0:T(8,128)(2,1)S(1)} copy-done((bf16[1,768,384]{2,1,0:T(8,128)(2,1)S(1)}, bf16[1,768,384]{2,1,0:T(8,128)(2,1)}, u32[]{:S(2)}) %copy-start) | copy-done | bytes 589848
  2.4 0.0 copy-start.2
  2.4 0.8 %copy-done.2 = f32[4,768]{1,0:T(4,128)S(1)} copy-done((f32[4,768]{1,0:T(4,128)S(1)}, f32[4,768]{1,0:T(4,128)}, u32[]{:S(2)}) %copy-start.2) | copy-done | bytes 12312
  3.3 0.0 slice-start.1
  3.3 0.6 shard_map.77.share
  3.9 0.0 collective-permute-done.below
  3.9 1.1 %shard_map.78 = (bf16[384,768]{1,0:T(8,128)(2,1)S(1)}, bf16[192,768]{1,0:T(8,128)(2,1)S(1)}, bf16[192,768]{1,0:T(8,128)(2,1)S(1)}, bf16[384,768]{1,0:T(8,128)(2,1)S(1)}, bf16[2,384,768]{2,1,0:T(8,128)(2,1)S(1)}) custom-call(s32[3]{0:T(128)S(1)} %pad_add_fusion.turn, bf16[2,384,768]{2,1,0:T(8,128)(2,1)S(1)} %shard_map.77.share, ...), custom_call_target="tpu_custom_call" | custom-call | tf_op jit(solution)/shard_map/pallas_call | solution.py:444
  5.0 0.7 collective-permute-start.1
  5.7 0.7 collective-permute-start.4
  6.4 4.5 %collective-permute-start.2 = (bf16[192,768]{1,0:T(8,128)(2,1)S(1)}, bf16[192,768]{1,0:T(8,128)(2,1)S(1)}, u32[]{:S(2)}, u32[]{:S(2)}) collective-permute-start(bf16[192,768]{1,0:T(8,128)(2,1)S(1)} %get-tuple-element.18), channel_id=1, source_target_pairs={{24,23},{25,18},{26,17},{27,20},{28,19},{29,22},{30,21},{31,16},{0... | collective-permute-start | bytes 884744 | tf_op jit(solution)/shard_map/ppermute | solution.py:396
  10.9 5.0 %collective-permute-start.3 = (bf16[192,768]{1,0:T(8,128)(2,1)S(1)}, bf16[192,768]{1,0:T(8,128)(2,1)S(1)}, u32[]{:S(2)}, u32[]{:S(2)}) collective-permute-start(bf16[192,768]{1,0:T(8,128)(2,1)S(1)} %get-tuple-element.19), channel_id=1, source_target_pairs={{24,22},{25,19},{26,16},{27,21},{28,18},{29,23},{30,20},{31,17},{0... | collective-permute-start | bytes 884744 | tf_op jit(solution)/shard_map/ppermute | solution.py:396
  15.8 0.0 slice-done
  15.9 0.0 slice-done.1
  15.9 0.8 %shard_map.79.refs_4_.refs_3_.refs_7_ = bf16[768,768]{1,0:T(8,128)(2,1)S(1)} custom-call(s32[3]{0:T(128)S(1)} %pad_add_fusion.turn, bf16[4,768,768]{2,1,0:T(8,128)(2,1)S(1)} %bitcast.10), custom_call_target="tpu_custom_call" | custom-call | tf_op jit(solution)/shard_map/pallas_call | solution.py:460
  16.7 4.8 %collective-permute-done.2.refs_1_ = bf16[192,768]{1,0:T(8,128)(2,1)S(1)} collective-permute-done((bf16[192,768]{1,0:T(8,128)(2,1)S(1)}, bf16[192,768]{1,0:T(8,128)(2,1)S(1)}, u32[]{:S(2)}, u32[]{:S(2)}) %collective-permute-start.2) | collective-permute-done | bytes 294944 | tf_op jit(solution)/shard_map/ppermute | solution.py:396
  21.5 1.9 %collective-permute-done.3.refs_2_ = bf16[192,768]{1,0:T(8,128)(2,1)S(1)} collective-permute-done((bf16[192,768]{1,0:T(8,128)(2,1)S(1)}, bf16[192,768]{1,0:T(8,128)(2,1)S(1)}, u32[]{:S(2)}, u32[]{:S(2)}) %collective-permute-start.3) | collective-permute-done | bytes 294944 | tf_op jit(solution)/shard_map/ppermute | solution.py:396
  23.4 0.0 collective-permute-done.1.refs_0_.refs_2_
  23.4 0.0 collective-permute-done.4.refs_3_
  23.4 0.6 shard_map.80.refs_5_.refs_3_
  24.0 0.9 %collective-permute-start.5 = (bf16[1,384,768]{2,1,0:T(8,128)(2,1)S(1)}, bf16[1,384,768]{2,1,0:T(8,128)(2,1)S(1)}, u32[]{:S(2)}, u32[]{:S(2)}) collective-permute-start(bf16[1,384,768]{2,1,0:T(8,128)(2,1)S(1)} %shard_map.80.refs_5_.refs_3_), channel_id=1, source_target_pairs={{0,24},{1,25},{2,26},{3,27},{4,28},{5,29},{6,30},{7,31},{8,0},{9,1... | collective-permute-start | bytes 1769480 | tf_op jit(solution)/shard_map/ppermute | solution.py:396
  24.9 7.4 %collective-permute-done.5.refs_0_ = bf16[1,384,768]{2,1,0:T(8,128)(2,1)S(1)} collective-permute-done((bf16[1,384,768]{2,1,0:T(8,128)(2,1)S(1)}, bf16[1,384,768]{2,1,0:T(8,128)(2,1)S(1)}, u32[]{:S(2)}, u32[]{:S(2)}) %collective-permute-start.5) | collective-permute-done | bytes 589856 | tf_op jit(solution)/shard_map/ppermute | solution.py:396
  32.3 0.6 shard_map.81
  32.9 1.3 %collective-permute-start.8 = (bf16[384,768]{1,0:T(8,128)(2,1)S(1)}, bf16[384,768]{1,0:T(8,128)(2,1)S(1)}, u32[]{:S(2)}, u32[]{:S(2)}) collective-permute-start(bf16[384,768]{1,0:T(8,128)(2,1)S(1)} %get-tuple-element.24), channel_id=1, source_target_pairs={{8,1},{9,0},{10,3},{11,2},{12,5},{13,4},{14,7},{15,6},{16,17},{17,... | collective-permute-start | bytes 1769480 | tf_op jit(solution)/shard_map/ppermute | solution.py:396
  34.2 1.3 %collective-permute-start.9 = (bf16[384,768]{1,0:T(8,128)(2,1)S(1)}, bf16[384,768]{1,0:T(8,128)(2,1)S(1)}, u32[]{:S(2)}, u32[]{:S(2)}) collective-permute-start(bf16[384,768]{1,0:T(8,128)(2,1)S(1)} %get-tuple-element.25), channel_id=1, source_target_pairs={{8,0},{9,1},{10,2},{11,3},{12,4},{13,5},{14,6},{15,7}} | collective-permute-start | bytes 1769480 | tf_op jit(solution)/shard_map/ppermute | solution.py:396
  35.5 1.3 %collective-permute-start.6 = (bf16[192,768]{1,0:T(8,128)(2,1)S(1)}, bf16[192,768]{1,0:T(8,128)(2,1)S(1)}, u32[]{:S(2)}, u32[]{:S(2)}) collective-permute-start(bf16[192,768]{1,0:T(8,128)(2,1)S(1)} %get-tuple-element.22), channel_id=1, source_target_pairs={{8,7},{9,2},{10,1},{11,4},{12,3},{13,6},{14,5},{15,0},{24,25},{25,... | collective-permute-start | bytes 884744 | tf_op jit(solution)/shard_map/ppermute | solution.py:396
  36.8 1.3 %collective-permute-start.7 = (bf16[192,768]{1,0:T(8,128)(2,1)S(1)}, bf16[192,768]{1,0:T(8,128)(2,1)S(1)}, u32[]{:S(2)}, u32[]{:S(2)}) collective-permute-start(bf16[192,768]{1,0:T(8,128)(2,1)S(1)} %get-tuple-element.23), channel_id=1, source_target_pairs={{8,2},{9,7},{10,4},{11,1},{12,6},{13,3},{14,0},{15,5},{24,31},{25,... | collective-permute-start | bytes 884744 | tf_op jit(solution)/shard_map/ppermute | solution.py:396
  38.1 17.0 %collective-permute-done.6.edge_cross.refs_1_ = bf16[192,768]{1,0:T(8,128)(2,1)S(1)} collective-permute-done((bf16[192,768]{1,0:T(8,128)(2,1)S(1)}, bf16[192,768]{1,0:T(8,128)(2,1)S(1)}, u32[]{:S(2)}, u32[]{:S(2)}) %collective-permute-start.6) | collective-permute-done | bytes 294944 | tf_op jit(solution)/shard_map/ppermute | solution.py:396
  55.1 3.0 %collective-permute-done.7.edge_same.refs_2_ = bf16[192,768]{1,0:T(8,128)(2,1)S(1)} collective-permute-done((bf16[192,768]{1,0:T(8,128)(2,1)S(1)}, bf16[192,768]{1,0:T(8,128)(2,1)S(1)}, u32[]{:S(2)}, u32[]{:S(2)}) %collective-permute-start.7) | collective-permute-done | bytes 294944 | tf_op jit(solution)/shard_map/ppermute | solution.py:396
  58.2 0.0 collective-permute-done.8.crossed.refs_0_.refs_4_
  58.2 0.0 collective-permute-done.9.direct.refs_3_
  58.2 0.7 shard_map.82
  58.9 0.1 collective-permute-start.10
  59.0 5.0 %shard_map.83.refs_6_ = bf16[2,192,768]{2,1,0:T(8,128)(2,1)S(1)} custom-call(s32[3]{0:T(128)S(1)} %pad_add_fusion.turn, f32[4,768]{1,0:T(4,128)S(1)} %copy-done.2, bf16[4,768,768]{2,1,0:T(8,128)(2,1)} %weights.9, bf16[384,768]{1,0:T(8,128)(2,1)S(1)} %collective-permute-done.8.crossed.refs_0_.refs_4_, ...), custom_call_target="tpu_custom_call" | custom-call | flops 2491416576 | bytes 4718592 | tf_op jit(solution)/shard_map/pallas_call | solution.py:185
  64.0 0.0 copy-start.1
  64.0 0.0 copy-start.3
  64.0 0.0 copy-start.4
  64.1 0.0 collective-permute-done.10.refs_5_
  64.1 1.4 %shard_map.84 = (bf16[2,192,768]{2,1,0:T(8,128)(2,1)S(1)}, f32[48,48]{1,0:T(8,128)S(1)}) custom-call(s32[3]{0:T(128)S(1)} %pad_add_fusion.turn, bf16[2,384,768]{2,1,0:T(8,128)(2,1)S(1)} %get-tuple-element.16.refs_1_.refs_4_.refs_5_.refs_0_, bf16[192,768]{1,0:T(8,128)(2,1)S(1)} %collective-permute-done.6.edge_cross.refs_1_, ...), custom_call_target="tpu_custom_call" | custom-call | tf_op jit(solution)/shard_map/pallas_call | solution.py:569
  65.4 0.1 collective-permute-start.11
  65.5 3.8 %collective-permute-done.11 = f32[48,48]{1,0:T(8,128)S(1)} collective-permute-done((f32[48,48]{1,0:T(8,128)S(1)}, f32[48,48]{1,0:T(8,128)S(1)}, u32[]{:S(2)}, u32[]{:S(2)}) %collective-permute-start.11) | collective-permute-done | bytes 9248 | tf_op jit(solution)/shard_map/ppermute | solution.py:588
  69.3 0.0 collective-permute-start.12
  69.3 1.4 %collective-permute-start.14 = (f32[48,48]{1,0:T(8,128)S(1)}, f32[48,48]{1,0:T(8,128)S(1)}, u32[]{:S(2)}, u32[]{:S(2)}) collective-permute-start(f32[48,48]{1,0:T(8,128)S(1)} %add.18), channel_id=1, source_target_pairs={{0,6},{1,7},{2,4},{3,5},{4,2},{5,3},{6,0},{7,1},{8,14},{9,15},{10,... | collective-permute-start | bytes 27656 | tf_op jit(solution)/shard_map/ppermute | solution.py:588
  70.8 2.1 %collective-permute-start.13 = (f32[48,48]{1,0:T(8,128)S(1)}, f32[48,48]{1,0:T(8,128)S(1)}, u32[]{:S(2)}, u32[]{:S(2)}) collective-permute-start(f32[48,48]{1,0:T(8,128)S(1)} %add.18), channel_id=1, source_target_pairs={{0,4},{1,5},{2,6},{3,7},{4,0},{5,1},{6,2},{7,3},{8,12},{9,13},{10,... | collective-permute-start | bytes 27656 | tf_op jit(solution)/shard_map/ppermute | solution.py:588
  72.8 0.3 collective-permute-done.12
  73.2 1.9 %collective-permute-done.14 = f32[48,48]{1,0:T(8,128)S(1)} collective-permute-done((f32[48,48]{1,0:T(8,128)S(1)}, f32[48,48]{1,0:T(8,128)S(1)}, u32[]{:S(2)}, u32[]{:S(2)}) %collective-permute-start.14) | collective-permute-done | bytes 9248 | tf_op jit(solution)/shard_map/ppermute | solution.py:588
  75.0 0.5 collective-permute-done.13
  75.5 0.0 copy-done.1
  75.5 0.0 copy-done.3
  75.5 0.0 copy-done.4
  75.5 3.5 %shard_map.85 = (bf16[768,384]{1,0:T(8,128)(2,1)}, f32[48,48]{1,0:T(8,128)}) custom-call(f32[48,48]{1,0:T(8,128)S(1)} %add.19.first, f32[48,48]{1,0:T(8,128)S(1)} %add.20.second, bf16[384,768]{1,0:T(8,128)(2,1)S(1)} %bitcast.16, bf16[384,48]{1,0:T(8,128)(2,1)S(1)} %copy-done.3, bf16[48,384]{1,0:T(8,128)(2,1)S(1)} %copy-done.4, f32[384,384]{1,0:T(8,128)S(1)} %copy-done.1), custom_call_target="tpu_custom_call" | custom-call | tf_op jit(solution)/shard_map/pallas_call | solution.py:595
  (4 shorter events, 0.0 us)
Async XLA Ops:
  0.6 3.3 %collective-permute-start = (bf16[768,384]{1,0:T(8,128)(2,1)}, bf16[768,384]{1,0:T(8,128)(2,1)S(1)}, u32[]{:S(2)}, u32[]{:S(2)}) collective-permute-start(bf16[768,384]{1,0:T(8,128)(2,1)} %bitcast.13), channel_id=1, source_target_pairs={{0,8},{1,9},{2,10},{3,11},{4,12},{5,13},{6,14},{7,15},{16,24},{17,... | collective-permute-start | bytes 1769480 | tf_op jit(solution)/shard_map/ppermute | solution.py:396
  1.1 14.7 %slice-start = ((s8[4718592]{0:T(1024)(128)(4,1)}), s8[4194304]{0:T(1024)(128)(4,1)S(1)}, s32[]{:S(2)}) async-start(s8[4718592]{0:T(1024)(128)(4,1)} %bitcast.9), calls=%async_computation | async-start | bytes 8388608
  1.2 1.2 %copy-start = (bf16[1,768,384]{2,1,0:T(8,128)(2,1)S(1)}, bf16[1,768,384]{2,1,0:T(8,128)(2,1)}, u32[]{:S(2)}) copy-start(bf16[1,768,384]{2,1,0:T(8,128)(2,1)} %param.8) | copy-start | bytes 1769476
  2.4 0.9 %copy-start.2 = (f32[4,768]{1,0:T(4,128)S(1)}, f32[4,768]{1,0:T(4,128)}, u32[]{:S(2)}) copy-start(f32[4,768]{1,0:T(4,128)} %coupling.7) | copy-start | bytes 36868
  3.3 12.6 %slice-start.1 = ((s8[4718592]{0:T(1024)(128)(4,1)}), s8[524288]{0:T(1024)(128)(4,1)S(1)}, s32[]{:S(2)}) async-start(s8[4718592]{0:T(1024)(128)(4,1)} %bitcast.9), calls=%async_computation.1 | async-start | bytes 1048576
  5.0 18.4 %collective-permute-start.1 = (bf16[384,768]{1,0:T(8,128)(2,1)S(1)}, bf16[384,768]{1,0:T(8,128)(2,1)S(1)}, u32[]{:S(2)}, u32[]{:S(2)}) collective-permute-start(bf16[384,768]{1,0:T(8,128)(2,1)S(1)} %get-tuple-element.17), channel_id=1, source_target_pairs={{24,17},{25,16},{26,19},{27,18},{28,21},{29,20},{30,23},{31,22},{8... | collective-permute-start | bytes 1769480 | tf_op jit(solution)/shard_map/ppermute | solution.py:396
  5.7 17.7 %collective-permute-start.4 = (bf16[384,768]{1,0:T(8,128)(2,1)S(1)}, bf16[384,768]{1,0:T(8,128)(2,1)S(1)}, u32[]{:S(2)}, u32[]{:S(2)}) collective-permute-start(bf16[384,768]{1,0:T(8,128)(2,1)S(1)} %get-tuple-element.20), channel_id=1, source_target_pairs={{24,16},{25,17},{26,18},{27,19},{28,20},{29,21},{30,22},{31,23}} | collective-permute-start | bytes 1769480 | tf_op jit(solution)/shard_map/ppermute | solution.py:396
  6.4 15.1 %collective-permute-start.2 = (bf16[192,768]{1,0:T(8,128)(2,1)S(1)}, bf16[192,768]{1,0:T(8,128)(2,1)S(1)}, u32[]{:S(2)}, u32[]{:S(2)}) collective-permute-start(bf16[192,768]{1,0:T(8,128)(2,1)S(1)} %get-tuple-element.18), channel_id=1, source_target_pairs={{24,23},{25,18},{26,17},{27,20},{28,19},{29,22},{30,21},{31,16},{0... | collective-permute-start | bytes 884744 | tf_op jit(solution)/shard_map/ppermute | solution.py:396
  10.9 12.5 %collective-permute-start.3 = (bf16[192,768]{1,0:T(8,128)(2,1)S(1)}, bf16[192,768]{1,0:T(8,128)(2,1)S(1)}, u32[]{:S(2)}, u32[]{:S(2)}) collective-permute-start(bf16[192,768]{1,0:T(8,128)(2,1)S(1)} %get-tuple-element.19), channel_id=1, source_target_pairs={{24,22},{25,19},{26,16},{27,21},{28,18},{29,23},{30,20},{31,17},{0... | collective-permute-start | bytes 884744 | tf_op jit(solution)/shard_map/ppermute | solution.py:396
  24.0 8.3 %collective-permute-start.5 = (bf16[1,384,768]{2,1,0:T(8,128)(2,1)S(1)}, bf16[1,384,768]{2,1,0:T(8,128)(2,1)S(1)}, u32[]{:S(2)}, u32[]{:S(2)}) collective-permute-start(bf16[1,384,768]{2,1,0:T(8,128)(2,1)S(1)} %shard_map.80.refs_5_.refs_3_), channel_id=1, source_target_pairs={{0,24},{1,25},{2,26},{3,27},{4,28},{5,29},{6,30},{7,31},{8,0},{9,1... | collective-permute-start | bytes 1769480 | tf_op jit(solution)/shard_map/ppermute | solution.py:396
  32.9 25.3 %collective-permute-start.8 = (bf16[384,768]{1,0:T(8,128)(2,1)S(1)}, bf16[384,768]{1,0:T(8,128)(2,1)S(1)}, u32[]{:S(2)}, u32[]{:S(2)}) collective-permute-start(bf16[384,768]{1,0:T(8,128)(2,1)S(1)} %get-tuple-element.24), channel_id=1, source_target_pairs={{8,1},{9,0},{10,3},{11,2},{12,5},{13,4},{14,7},{15,6},{16,17},{17,... | collective-permute-start | bytes 1769480 | tf_op jit(solution)/shard_map/ppermute | solution.py:396
  34.2 24.0 %collective-permute-start.9 = (bf16[384,768]{1,0:T(8,128)(2,1)S(1)}, bf16[384,768]{1,0:T(8,128)(2,1)S(1)}, u32[]{:S(2)}, u32[]{:S(2)}) collective-permute-start(bf16[384,768]{1,0:T(8,128)(2,1)S(1)} %get-tuple-element.25), channel_id=1, source_target_pairs={{8,0},{9,1},{10,2},{11,3},{12,4},{13,5},{14,6},{15,7}} | collective-permute-start | bytes 1769480 | tf_op jit(solution)/shard_map/ppermute | solution.py:396
  35.5 19.6 %collective-permute-start.6 = (bf16[192,768]{1,0:T(8,128)(2,1)S(1)}, bf16[192,768]{1,0:T(8,128)(2,1)S(1)}, u32[]{:S(2)}, u32[]{:S(2)}) collective-permute-start(bf16[192,768]{1,0:T(8,128)(2,1)S(1)} %get-tuple-element.22), channel_id=1, source_target_pairs={{8,7},{9,2},{10,1},{11,4},{12,3},{13,6},{14,5},{15,0},{24,25},{25,... | collective-permute-start | bytes 884744 | tf_op jit(solution)/shard_map/ppermute | solution.py:396
  36.8 21.4 %collective-permute-start.7 = (bf16[192,768]{1,0:T(8,128)(2,1)S(1)}, bf16[192,768]{1,0:T(8,128)(2,1)S(1)}, u32[]{:S(2)}, u32[]{:S(2)}) collective-permute-start(bf16[192,768]{1,0:T(8,128)(2,1)S(1)} %get-tuple-element.23), channel_id=1, source_target_pairs={{8,2},{9,7},{10,4},{11,1},{12,6},{13,3},{14,0},{15,5},{24,31},{25,... | collective-permute-start | bytes 884744 | tf_op jit(solution)/shard_map/ppermute | solution.py:396
  58.9 5.1 %collective-permute-start.10 = (bf16[2,192,768]{2,1,0:T(8,128)(2,1)S(1)}, bf16[2,192,768]{2,1,0:T(8,128)(2,1)S(1)}, u32[]{:S(2)}, u32[]{:S(2)}) collective-permute-start(bf16[2,192,768]{2,1,0:T(8,128)(2,1)S(1)} %shard_map.82), channel_id=1, source_target_pairs={{0,8},{1,9},{2,10},{3,11},{4,12},{5,13},{6,14},{7,15},{16,24},{17,... | collective-permute-start | bytes 1769480 | tf_op jit(solution)/shard_map/ppermute | solution.py:396
  64.0 11.5 %copy-start.1 = (f32[384,384]{1,0:T(8,128)S(1)}, f32[384,384]{1,0:T(8,128)}, u32[]{:S(2)}) copy-start(f32[384,384]{1,0:T(8,128)} %constant.40.clone.same_point) | copy-start | bytes 1769476
  64.0 11.5 %copy-start.3 = (bf16[384,48]{1,0:T(8,128)(2,1)S(1)}, bf16[384,48]{1,0:T(8,128)(2,1)}, u32[]{:S(2)}) copy-start(bf16[384,48]{1,0:T(8,128)(2,1)} %constant.38.clone.by_column) | copy-start | bytes 110596
  64.0 11.5 %copy-start.4 = (bf16[48,384]{1,0:T(8,128)(2,1)S(1)}, bf16[48,384]{1,0:T(8,128)(2,1)}, u32[]{:S(2)}) copy-start(bf16[48,384]{1,0:T(8,128)(2,1)} %constant.39.clone.by_place) | copy-start | bytes 110596
  65.4 3.9 %collective-permute-start.11 = (f32[48,48]{1,0:T(8,128)S(1)}, f32[48,48]{1,0:T(8,128)S(1)}, u32[]{:S(2)}, u32[]{:S(2)}) collective-permute-start(f32[48,48]{1,0:T(8,128)S(1)} %get-tuple-element.26), channel_id=1, source_target_pairs={{0,1},{1,0},{2,3},{3,2},{4,5},{5,4},{6,7},{7,6},{8,9},{9,8},{10,11... | collective-permute-start | bytes 27656 | tf_op jit(solution)/shard_map/ppermute | solution.py:588
  69.3 3.8 %collective-permute-start.12 = (f32[48,48]{1,0:T(8,128)S(1)}, f32[48,48]{1,0:T(8,128)S(1)}, u32[]{:S(2)}, u32[]{:S(2)}) collective-permute-start(f32[48,48]{1,0:T(8,128)S(1)} %add.18), channel_id=1, source_target_pairs={{0,2},{1,3},{2,0},{3,1},{4,6},{5,7},{6,4},{7,5},{8,10},{9,11},{10,... | collective-permute-start | bytes 27656 | tf_op jit(solution)/shard_map/ppermute | solution.py:588
  69.3 5.7 %collective-permute-start.14 = (f32[48,48]{1,0:T(8,128)S(1)}, f32[48,48]{1,0:T(8,128)S(1)}, u32[]{:S(2)}, u32[]{:S(2)}) collective-permute-start(f32[48,48]{1,0:T(8,128)S(1)} %add.18), channel_id=1, source_target_pairs={{0,6},{1,7},{2,4},{3,5},{4,2},{5,3},{6,0},{7,1},{8,14},{9,15},{10,... | collective-permute-start | bytes 27656 | tf_op jit(solution)/shard_map/ppermute | solution.py:588
  70.8 4.7 %collective-permute-start.13 = (f32[48,48]{1,0:T(8,128)S(1)}, f32[48,48]{1,0:T(8,128)S(1)}, u32[]{:S(2)}, u32[]{:S(2)}) collective-permute-start(f32[48,48]{1,0:T(8,128)S(1)} %add.18), channel_id=1, source_target_pairs={{0,4},{1,5},{2,6},{3,7},{4,0},{5,1},{6,2},{7,3},{8,12},{9,13},{10,... | collective-permute-start | bytes 27656 | tf_op jit(solution)/shard_map/ppermute | solution.py:588

commit v6 on v4

--- a/solution.py
+++ b/solution.py
@@ -486,7 +486,7 @@
                 (edge_same, lambda side: (0, (1 - side) * 2 * ONE), WIDE, None),
                 (direct, lambda side: (0, side * ONE), 2 * ONE, None),
             ],
-            14,
+            12,
             1,
             3 * POINTS,
             False,

time: 79.3 us -> 79.2 us (level)
  no operation moved by 1% of the time
where the time goes in v6:
time: 79.2 us; the launch traced here: 78.8 us
  waiting for transfers between devices  40.7 us (51%)
  starting transfers between devices  21 us (27%)
  Pallas kernels  14.1 us (18%)
  local copies, waits for them, and re-layouts  2.09 us (3%)
  between operations  0.87 us (1%)
    ppermute x11, waiting for transfers between devices, send(): return lax.ppermute(value, AXES, routes)  34.2 us
    ppermute x11, starting transfers between devices, send(): return lax.ppermute(value, AXES, routes)  17.5 us
    pallas_call x4, Pallas kernels, march(): pl.pallas_call(functools.partial(march_kernel, number, [piece[1:] for pie...  6.78 us
    ppermute x4, waiting for transfers between devices, local(): lax.ppermute(total, 'span', [(s, s ^ digit * stride) for s in range(spans)])  6.48 us
    ppermute x4, starting transfers between devices, local(): lax.ppermute(total, 'span', [(s, s ^ digit * stride) for s in range(spans)])  3.56 us
    pallas_call x1, Pallas kernels, local(): pl.pallas_call(functools.partial(factor_kernel, 1.0 / float(FN * POINTS *...  3.35 us
    unnamed x14, local copies, waits for them, and re-layouts  2.09 us
  transfers between devices with their start and end apart: 15, of which 9 were waited for; matrix products, arithmetic and copies ran while one was open for 0% of the time, Pallas kernels for 8%

profile of v6, /device:TPU:0, one launch (start us, length us, event | category | flops | bytes accessed | tf_op | source)
XLA Modules:
  0.0 78.8 jit_solution(14208921912701500216)
XLA Ops:
  0.6 0.5 collective-permute-start
  1.1 0.0 slice-start
  1.1 0.1 pad_add_fusion.turn
  1.2 0.0 copy-start
  1.2 1.2 %copy-done = bf16[1,768,384]{2,1,0:T(8,128)(2,1)S(1)} copy-done((bf16[1,768,384]{2,1,0:T(8,128)(2,1)S(1)}, bf16[1,768,384]{2,1,0:T(8,128)(2,1)}, u32[]{:S(2)}) %copy-start) | copy-done | bytes 589848
  2.4 0.0 copy-start.2
  2.4 0.8 %copy-done.2 = f32[4,768]{1,0:T(4,128)S(1)} copy-done((f32[4,768]{1,0:T(4,128)S(1)}, f32[4,768]{1,0:T(4,128)}, u32[]{:S(2)}) %copy-start.2) | copy-done | bytes 12312
  3.3 0.0 slice-start.1
  3.3 0.6 shard_map.77.share
  3.9 0.0 collective-permute-done.below
  3.9 1.1 %shard_map.78 = (bf16[384,768]{1,0:T(8,128)(2,1)S(1)}, bf16[192,768]{1,0:T(8,128)(2,1)S(1)}, bf16[192,768]{1,0:T(8,128)(2,1)S(1)}, bf16[384,768]{1,0:T(8,128)(2,1)S(1)}, bf16[2,384,768]{2,1,0:T(8,128)(2,1)S(1)}) custom-call(s32[3]{0:T(128)S(1)} %pad_add_fusion.turn, bf16[2,384,768]{2,1,0:T(8,128)(2,1)S(1)} %shard_map.77.share, ...), custom_call_target="tpu_custom_call" | custom-call | tf_op jit(solution)/shard_map/pallas_call | solution.py:444
  5.0 0.7 collective-permute-start.1
  5.7 0.7 collective-permute-start.4
  6.4 4.5 %collective-permute-start.2 = (bf16[192,768]{1,0:T(8,128)(2,1)S(1)}, bf16[192,768]{1,0:T(8,128)(2,1)S(1)}, u32[]{:S(2)}, u32[]{:S(2)}) collective-permute-start(bf16[192,768]{1,0:T(8,128)(2,1)S(1)} %get-tuple-element.18), channel_id=1, source_target_pairs={{24,23},{25,18},{26,17},{27,20},{28,19},{29,22},{30,21},{31,16},{0... | collective-permute-start | bytes 884744 | tf_op jit(solution)/shard_map/ppermute | solution.py:396
  10.9 5.0 %collective-permute-start.3 = (bf16[192,768]{1,0:T(8,128)(2,1)S(1)}, bf16[192,768]{1,0:T(8,128)(2,1)S(1)}, u32[]{:S(2)}, u32[]{:S(2)}) collective-permute-start(bf16[192,768]{1,0:T(8,128)(2,1)S(1)} %get-tuple-element.19), channel_id=1, source_target_pairs={{24,22},{25,19},{26,16},{27,21},{28,18},{29,23},{30,20},{31,17},{0... | collective-permute-start | bytes 884744 | tf_op jit(solution)/shard_map/ppermute | solution.py:396
  15.8 0.0 slice-done
  15.9 0.0 slice-done.1
  15.9 0.8 %shard_map.79.refs_4_.refs_3_.refs_7_ = bf16[768,768]{1,0:T(8,128)(2,1)S(1)} custom-call(s32[3]{0:T(128)S(1)} %pad_add_fusion.turn, bf16[4,768,768]{2,1,0:T(8,128)(2,1)S(1)} %bitcast.10), custom_call_target="tpu_custom_call" | custom-call | tf_op jit(solution)/shard_map/pallas_call | solution.py:460
  16.7 4.8 %collective-permute-done.2.refs_1_ = bf16[192,768]{1,0:T(8,128)(2,1)S(1)} collective-permute-done((bf16[192,768]{1,0:T(8,128)(2,1)S(1)}, bf16[192,768]{1,0:T(8,128)(2,1)S(1)}, u32[]{:S(2)}, u32[]{:S(2)}) %collective-permute-start.2) | collective-permute-done | bytes 294944 | tf_op jit(solution)/shard_map/ppermute | solution.py:396
  21.5 1.9 %collective-permute-done.3.refs_2_ = bf16[192,768]{1,0:T(8,128)(2,1)S(1)} collective-permute-done((bf16[192,768]{1,0:T(8,128)(2,1)S(1)}, bf16[192,768]{1,0:T(8,128)(2,1)S(1)}, u32[]{:S(2)}, u32[]{:S(2)}) %collective-permute-start.3) | collective-permute-done | bytes 294944 | tf_op jit(solution)/shard_map/ppermute | solution.py:396
  23.4 0.0 collective-permute-done.1.refs_0_.refs_2_
  23.4 0.0 collective-permute-done.4.refs_3_
  23.4 0.6 shard_map.80.refs_5_.refs_3_
  24.0 0.9 %collective-permute-start.5 = (bf16[1,384,768]{2,1,0:T(8,128)(2,1)S(1)}, bf16[1,384,768]{2,1,0:T(8,128)(2,1)S(1)}, u32[]{:S(2)}, u32[]{:S(2)}) collective-permute-start(bf16[1,384,768]{2,1,0:T(8,128)(2,1)S(1)} %shard_map.80.refs_5_.refs_3_), channel_id=1, source_target_pairs={{0,24},{1,25},{2,26},{3,27},{4,28},{5,29},{6,30},{7,31},{8,0},{9,1... | collective-permute-start | bytes 1769480 | tf_op jit(solution)/shard_map/ppermute | solution.py:396
  24.9 7.4 %collective-permute-done.5.refs_0_ = bf16[1,384,768]{2,1,0:T(8,128)(2,1)S(1)} collective-permute-done((bf16[1,384,768]{2,1,0:T(8,128)(2,1)S(1)}, bf16[1,384,768]{2,1,0:T(8,128)(2,1)S(1)}, u32[]{:S(2)}, u32[]{:S(2)}) %collective-permute-start.5) | collective-permute-done | bytes 589856 | tf_op jit(solution)/shard_map/ppermute | solution.py:396
  32.3 0.6 shard_map.81
  32.9 1.3 %collective-permute-start.8 = (bf16[384,768]{1,0:T(8,128)(2,1)S(1)}, bf16[384,768]{1,0:T(8,128)(2,1)S(1)}, u32[]{:S(2)}, u32[]{:S(2)}) collective-permute-start(bf16[384,768]{1,0:T(8,128)(2,1)S(1)} %get-tuple-element.24), channel_id=1, source_target_pairs={{8,1},{9,0},{10,3},{11,2},{12,5},{13,4},{14,7},{15,6},{16,17},{17,... | collective-permute-start | bytes 1769480 | tf_op jit(solution)/shard_map/ppermute | solution.py:396
  34.2 1.3 %collective-permute-start.9 = (bf16[384,768]{1,0:T(8,128)(2,1)S(1)}, bf16[384,768]{1,0:T(8,128)(2,1)S(1)}, u32[]{:S(2)}, u32[]{:S(2)}) collective-permute-start(bf16[384,768]{1,0:T(8,128)(2,1)S(1)} %get-tuple-element.25), channel_id=1, source_target_pairs={{8,0},{9,1},{10,2},{11,3},{12,4},{13,5},{14,6},{15,7}} | collective-permute-start | bytes 1769480 | tf_op jit(solution)/shard_map/ppermute | solution.py:396
  35.5 1.3 %collective-permute-start.6 = (bf16[192,768]{1,0:T(8,128)(2,1)S(1)}, bf16[192,768]{1,0:T(8,128)(2,1)S(1)}, u32[]{:S(2)}, u32[]{:S(2)}) collective-permute-start(bf16[192,768]{1,0:T(8,128)(2,1)S(1)} %get-tuple-element.22), channel_id=1, source_target_pairs={{8,7},{9,2},{10,1},{11,4},{12,3},{13,6},{14,5},{15,0},{24,25},{25,... | collective-permute-start | bytes 884744 | tf_op jit(solution)/shard_map/ppermute | solution.py:396
  36.8 1.3 %collective-permute-start.7 = (bf16[192,768]{1,0:T(8,128)(2,1)S(1)}, bf16[192,768]{1,0:T(8,128)(2,1)S(1)}, u32[]{:S(2)}, u32[]{:S(2)}) collective-permute-start(bf16[192,768]{1,0:T(8,128)(2,1)S(1)} %get-tuple-element.23), channel_id=1, source_target_pairs={{8,2},{9,7},{10,4},{11,1},{12,6},{13,3},{14,0},{15,5},{24,31},{25,... | collective-permute-start | bytes 884744 | tf_op jit(solution)/shard_map/ppermute | solution.py:396
  38.1 17.0 %collective-permute-done.6.edge_cross.refs_1_ = bf16[192,768]{1,0:T(8,128)(2,1)S(1)} collective-permute-done((bf16[192,768]{1,0:T(8,128)(2,1)S(1)}, bf16[192,768]{1,0:T(8,128)(2,1)S(1)}, u32[]{:S(2)}, u32[]{:S(2)}) %collective-permute-start.6) | collective-permute-done | bytes 294944 | tf_op jit(solution)/shard_map/ppermute | solution.py:396
  55.1 3.0 %collective-permute-done.7.edge_same.refs_2_ = bf16[192,768]{1,0:T(8,128)(2,1)S(1)} collective-permute-done((bf16[192,768]{1,0:T(8,128)(2,1)S(1)}, bf16[192,768]{1,0:T(8,128)(2,1)S(1)}, u32[]{:S(2)}, u32[]{:S(2)}) %collective-permute-start.7) | collective-permute-done | bytes 294944 | tf_op jit(solution)/shard_map/ppermute | solution.py:396
  58.1 0.0 collective-permute-done.8.crossed.refs_0_.refs_4_
  58.1 0.0 collective-permute-done.9.direct.refs_3_
  58.1 0.7 shard_map.82
  58.9 0.1 collective-permute-start.10
  58.9 5.0 %shard_map.83.refs_6_ = bf16[2,192,768]{2,1,0:T(8,128)(2,1)S(1)} custom-call(s32[3]{0:T(128)S(1)} %pad_add_fusion.turn, f32[4,768]{1,0:T(4,128)S(1)} %copy-done.2, bf16[4,768,768]{2,1,0:T(8,128)(2,1)} %weights.9, bf16[384,768]{1,0:T(8,128)(2,1)S(1)} %collective-permute-done.8.crossed.refs_0_.refs_4_, ...), custom_call_target="tpu_custom_call" | custom-call | flops 2491416576 | bytes 4718592 | tf_op jit(solution)/shard_map/pallas_call | solution.py:185
  64.0 0.0 copy-start.1
  64.0 0.0 copy-start.3
  64.0 0.0 copy-start.4
  64.0 0.0 collective-permute-done.10.refs_5_
  64.0 1.4 %shard_map.84 = (bf16[2,192,768]{2,1,0:T(8,128)(2,1)S(1)}, f32[48,48]{1,0:T(8,128)S(1)}) custom-call(s32[3]{0:T(128)S(1)} %pad_add_fusion.turn, bf16[2,384,768]{2,1,0:T(8,128)(2,1)S(1)} %get-tuple-element.16.refs_1_.refs_4_.refs_5_.refs_0_, bf16[192,768]{1,0:T(8,128)(2,1)S(1)} %collective-permute-done.6.edge_cross.refs_1_, ...), custom_call_target="tpu_custom_call" | custom-call | tf_op jit(solution)/shard_map/pallas_call | solution.py:569
  65.4 0.1 collective-permute-start.11
  65.5 3.8 %collective-permute-done.11 = f32[48,48]{1,0:T(8,128)S(1)} collective-permute-done((f32[48,48]{1,0:T(8,128)S(1)}, f32[48,48]{1,0:T(8,128)S(1)}, u32[]{:S(2)}, u32[]{:S(2)}) %collective-permute-start.11) | collective-permute-done | bytes 9248 | tf_op jit(solution)/shard_map/ppermute | solution.py:588
  69.3 0.0 collective-permute-start.12
  69.3 1.4 %collective-permute-start.14 = (f32[48,48]{1,0:T(8,128)S(1)}, f32[48,48]{1,0:T(8,128)S(1)}, u32[]{:S(2)}, u32[]{:S(2)}) collective-permute-start(f32[48,48]{1,0:T(8,128)S(1)} %add.18), channel_id=1, source_target_pairs={{0,6},{1,7},{2,4},{3,5},{4,2},{5,3},{6,0},{7,1},{8,14},{9,15},{10,... | collective-permute-start | bytes 27656 | tf_op jit(solution)/shard_map/ppermute | solution.py:588
  70.7 2.0 %collective-permute-start.13 = (f32[48,48]{1,0:T(8,128)S(1)}, f32[48,48]{1,0:T(8,128)S(1)}, u32[]{:S(2)}, u32[]{:S(2)}) collective-permute-start(f32[48,48]{1,0:T(8,128)S(1)} %add.18), channel_id=1, source_target_pairs={{0,4},{1,5},{2,6},{3,7},{4,0},{5,1},{6,2},{7,3},{8,12},{9,13},{10,... | collective-permute-start | bytes 27656 | tf_op jit(solution)/shard_map/ppermute | solution.py:588
  72.8 0.3 collective-permute-done.12
  73.1 1.9 %collective-permute-done.14 = f32[48,48]{1,0:T(8,128)S(1)} collective-permute-done((f32[48,48]{1,0:T(8,128)S(1)}, f32[48,48]{1,0:T(8,128)S(1)}, u32[]{:S(2)}, u32[]{:S(2)}) %collective-permute-start.14) | collective-permute-done | bytes 9248 | tf_op jit(solution)/shard_map/ppermute | solution.py:588
  75.0 0.5 collective-permute-done.13
  75.4 0.0 copy-done.1
  75.4 0.0 copy-done.3
  75.5 0.0 copy-done.4
  75.5 3.3 %shard_map.85 = (bf16[768,384]{1,0:T(8,128)(2,1)}, f32[48,48]{1,0:T(8,128)}) custom-call(f32[48,48]{1,0:T(8,128)S(1)} %add.19.first, f32[48,48]{1,0:T(8,128)S(1)} %add.20.second, bf16[384,768]{1,0:T(8,128)(2,1)S(1)} %bitcast.16, bf16[384,48]{1,0:T(8,128)(2,1)S(1)} %copy-done.3, bf16[48,384]{1,0:T(8,128)(2,1)S(1)} %copy-done.4, f32[384,384]{1,0:T(8,128)S(1)} %copy-done.1), custom_call_target="tpu_custom_call" | custom-call | tf_op jit(solution)/shard_map/pallas_call | solution.py:595
  (4 shorter events, 0.0 us)
Async XLA Ops:
  0.6 3.3 %collective-permute-start = (bf16[768,384]{1,0:T(8,128)(2,1)}, bf16[768,384]{1,0:T(8,128)(2,1)S(1)}, u32[]{:S(2)}, u32[]{:S(2)}) collective-permute-start(bf16[768,384]{1,0:T(8,128)(2,1)} %bitcast.13), channel_id=1, source_target_pairs={{0,8},{1,9},{2,10},{3,11},{4,12},{5,13},{6,14},{7,15},{16,24},{17,... | collective-permute-start | bytes 1769480 | tf_op jit(solution)/shard_map/ppermute | solution.py:396
  1.1 14.7 %slice-start = ((s8[4718592]{0:T(1024)(128)(4,1)}), s8[4194304]{0:T(1024)(128)(4,1)S(1)}, s32[]{:S(2)}) async-start(s8[4718592]{0:T(1024)(128)(4,1)} %bitcast.9), calls=%async_computation | async-start | bytes 8388608
  1.2 1.2 %copy-start = (bf16[1,768,384]{2,1,0:T(8,128)(2,1)S(1)}, bf16[1,768,384]{2,1,0:T(8,128)(2,1)}, u32[]{:S(2)}) copy-start(bf16[1,768,384]{2,1,0:T(8,128)(2,1)} %param.8) | copy-start | bytes 1769476
  2.4 0.9 %copy-start.2 = (f32[4,768]{1,0:T(4,128)S(1)}, f32[4,768]{1,0:T(4,128)}, u32[]{:S(2)}) copy-start(f32[4,768]{1,0:T(4,128)} %coupling.7) | copy-start | bytes 36868
  3.3 12.6 %slice-start.1 = ((s8[4718592]{0:T(1024)(128)(4,1)}), s8[524288]{0:T(1024)(128)(4,1)S(1)}, s32[]{:S(2)}) async-start(s8[4718592]{0:T(1024)(128)(4,1)} %bitcast.9), calls=%async_computation.1 | async-start | bytes 1048576
  5.0 18.4 %collective-permute-start.1 = (bf16[384,768]{1,0:T(8,128)(2,1)S(1)}, bf16[384,768]{1,0:T(8,128)(2,1)S(1)}, u32[]{:S(2)}, u32[]{:S(2)}) collective-permute-start(bf16[384,768]{1,0:T(8,128)(2,1)S(1)} %get-tuple-element.17), channel_id=1, source_target_pairs={{24,17},{25,16},{26,19},{27,18},{28,21},{29,20},{30,23},{31,22},{8... | collective-permute-start | bytes 1769480 | tf_op jit(solution)/shard_map/ppermute | solution.py:396
  5.7 17.7 %collective-permute-start.4 = (bf16[384,768]{1,0:T(8,128)(2,1)S(1)}, bf16[384,768]{1,0:T(8,128)(2,1)S(1)}, u32[]{:S(2)}, u32[]{:S(2)}) collective-permute-start(bf16[384,768]{1,0:T(8,128)(2,1)S(1)} %get-tuple-element.20), channel_id=1, source_target_pairs={{24,16},{25,17},{26,18},{27,19},{28,20},{29,21},{30,22},{31,23}} | collective-permute-start | bytes 1769480 | tf_op jit(solution)/shard_map/ppermute | solution.py:396
  6.4 15.1 %collective-permute-start.2 = (bf16[192,768]{1,0:T(8,128)(2,1)S(1)}, bf16[192,768]{1,0:T(8,128)(2,1)S(1)}, u32[]{:S(2)}, u32[]{:S(2)}) collective-permute-start(bf16[192,768]{1,0:T(8,128)(2,1)S(1)} %get-tuple-element.18), channel_id=1, source_target_pairs={{24,23},{25,18},{26,17},{27,20},{28,19},{29,22},{30,21},{31,16},{0... | collective-permute-start | bytes 884744 | tf_op jit(solution)/shard_map/ppermute | solution.py:396
  10.9 12.5 %collective-permute-start.3 = (bf16[192,768]{1,0:T(8,128)(2,1)S(1)}, bf16[192,768]{1,0:T(8,128)(2,1)S(1)}, u32[]{:S(2)}, u32[]{:S(2)}) collective-permute-start(bf16[192,768]{1,0:T(8,128)(2,1)S(1)} %get-tuple-element.19), channel_id=1, source_target_pairs={{24,22},{25,19},{26,16},{27,21},{28,18},{29,23},{30,20},{31,17},{0... | collective-permute-start | bytes 884744 | tf_op jit(solution)/shard_map/ppermute | solution.py:396
  24.0 8.3 %collective-permute-start.5 = (bf16[1,384,768]{2,1,0:T(8,128)(2,1)S(1)}, bf16[1,384,768]{2,1,0:T(8,128)(2,1)S(1)}, u32[]{:S(2)}, u32[]{:S(2)}) collective-permute-start(bf16[1,384,768]{2,1,0:T(8,128)(2,1)S(1)} %shard_map.80.refs_5_.refs_3_), channel_id=1, source_target_pairs={{0,24},{1,25},{2,26},{3,27},{4,28},{5,29},{6,30},{7,31},{8,0},{9,1... | collective-permute-start | bytes 1769480 | tf_op jit(solution)/shard_map/ppermute | solution.py:396
  32.9 25.2 %collective-permute-start.8 = (bf16[384,768]{1,0:T(8,128)(2,1)S(1)}, bf16[384,768]{1,0:T(8,128)(2,1)S(1)}, u32[]{:S(2)}, u32[]{:S(2)}) collective-permute-start(bf16[384,768]{1,0:T(8,128)(2,1)S(1)} %get-tuple-element.24), channel_id=1, source_target_pairs={{8,1},{9,0},{10,3},{11,2},{12,5},{13,4},{14,7},{15,6},{16,17},{17,... | collective-permute-start | bytes 1769480 | tf_op jit(solution)/shard_map/ppermute | solution.py:396
  34.2 24.0 %collective-permute-start.9 = (bf16[384,768]{1,0:T(8,128)(2,1)S(1)}, bf16[384,768]{1,0:T(8,128)(2,1)S(1)}, u32[]{:S(2)}, u32[]{:S(2)}) collective-permute-start(bf16[384,768]{1,0:T(8,128)(2,1)S(1)} %get-tuple-element.25), channel_id=1, source_target_pairs={{8,0},{9,1},{10,2},{11,3},{12,4},{13,5},{14,6},{15,7}} | collective-permute-start | bytes 1769480 | tf_op jit(solution)/shard_map/ppermute | solution.py:396
  35.5 19.6 %collective-permute-start.6 = (bf16[192,768]{1,0:T(8,128)(2,1)S(1)}, bf16[192,768]{1,0:T(8,128)(2,1)S(1)}, u32[]{:S(2)}, u32[]{:S(2)}) collective-permute-start(bf16[192,768]{1,0:T(8,128)(2,1)S(1)} %get-tuple-element.22), channel_id=1, source_target_pairs={{8,7},{9,2},{10,1},{11,4},{12,3},{13,6},{14,5},{15,0},{24,25},{25,... | collective-permute-start | bytes 884744 | tf_op jit(solution)/shard_map/ppermute | solution.py:396
  36.8 21.3 %collective-permute-start.7 = (bf16[192,768]{1,0:T(8,128)(2,1)S(1)}, bf16[192,768]{1,0:T(8,128)(2,1)S(1)}, u32[]{:S(2)}, u32[]{:S(2)}) collective-permute-start(bf16[192,768]{1,0:T(8,128)(2,1)S(1)} %get-tuple-element.23), channel_id=1, source_target_pairs={{8,2},{9,7},{10,4},{11,1},{12,6},{13,3},{14,0},{15,5},{24,31},{25,... | collective-permute-start | bytes 884744 | tf_op jit(solution)/shard_map/ppermute | solution.py:396
  58.9 5.1 %collective-permute-start.10 = (bf16[2,192,768]{2,1,0:T(8,128)(2,1)S(1)}, bf16[2,192,768]{2,1,0:T(8,128)(2,1)S(1)}, u32[]{:S(2)}, u32[]{:S(2)}) collective-permute-start(bf16[2,192,768]{2,1,0:T(8,128)(2,1)S(1)} %shard_map.82), channel_id=1, source_target_pairs={{0,8},{1,9},{2,10},{3,11},{4,12},{5,13},{6,14},{7,15},{16,24},{17,... | collective-permute-start | bytes 1769480 | tf_op jit(solution)/shard_map/ppermute | solution.py:396
  64.0 11.5 %copy-start.1 = (f32[384,384]{1,0:T(8,128)S(1)}, f32[384,384]{1,0:T(8,128)}, u32[]{:S(2)}) copy-start(f32[384,384]{1,0:T(8,128)} %constant.40.clone.same_point) | copy-start | bytes 1769476
  64.0 11.5 %copy-start.3 = (bf16[384,48]{1,0:T(8,128)(2,1)S(1)}, bf16[384,48]{1,0:T(8,128)(2,1)}, u32[]{:S(2)}) copy-start(bf16[384,48]{1,0:T(8,128)(2,1)} %constant.38.clone.by_column) | copy-start | bytes 110596
  64.0 11.5 %copy-start.4 = (bf16[48,384]{1,0:T(8,128)(2,1)S(1)}, bf16[48,384]{1,0:T(8,128)(2,1)}, u32[]{:S(2)}) copy-start(bf16[48,384]{1,0:T(8,128)(2,1)} %constant.39.clone.by_place) | copy-start | bytes 110596
  65.4 3.9 %collective-permute-start.11 = (f32[48,48]{1,0:T(8,128)S(1)}, f32[48,48]{1,0:T(8,128)S(1)}, u32[]{:S(2)}, u32[]{:S(2)}) collective-permute-start(f32[48,48]{1,0:T(8,128)S(1)} %get-tuple-element.26), channel_id=1, source_target_pairs={{0,1},{1,0},{2,3},{3,2},{4,5},{5,4},{6,7},{7,6},{8,9},{9,8},{10,11... | collective-permute-start | bytes 27656 | tf_op jit(solution)/shard_map/ppermute | solution.py:588
  69.3 3.8 %collective-permute-start.12 = (f32[48,48]{1,0:T(8,128)S(1)}, f32[48,48]{1,0:T(8,128)S(1)}, u32[]{:S(2)}, u32[]{:S(2)}) collective-permute-start(f32[48,48]{1,0:T(8,128)S(1)} %add.18), channel_id=1, source_target_pairs={{0,2},{1,3},{2,0},{3,1},{4,6},{5,7},{6,4},{7,5},{8,10},{9,11},{10,... | collective-permute-start | bytes 27656 | tf_op jit(solution)/shard_map/ppermute | solution.py:588
  69.3 5.7 %collective-permute-start.14 = (f32[48,48]{1,0:T(8,128)S(1)}, f32[48,48]{1,0:T(8,128)S(1)}, u32[]{:S(2)}, u32[]{:S(2)}) collective-permute-start(f32[48,48]{1,0:T(8,128)S(1)} %add.18), channel_id=1, source_target_pairs={{0,6},{1,7},{2,4},{3,5},{4,2},{5,3},{6,0},{7,1},{8,14},{9,15},{10,... | collective-permute-start | bytes 27656 | tf_op jit(solution)/shard_map/ppermute | solution.py:588
  70.7 4.7 %collective-permute-start.13 = (f32[48,48]{1,0:T(8,128)S(1)}, f32[48,48]{1,0:T(8,128)S(1)}, u32[]{:S(2)}, u32[]{:S(2)}) collective-permute-start(f32[48,48]{1,0:T(8,128)S(1)} %add.18), channel_id=1, source_target_pairs={{0,4},{1,5},{2,6},{3,7},{4,0},{5,1},{6,2},{7,3},{8,12},{9,13},{10,... | collective-permute-start | bytes 27656 | tf_op jit(solution)/shard_map/ppermute | solution.py:588
